TPU v7x, 32 devices: a whole 2x2x4 slice. The times are simulated.
32 devices in a mesh: panel: 2 (over x), leaf: 16 (over z, y, core).
Axes of the slice: x: 2, y: 2, z: 4, core: 2. Of those that a mesh axis runs over, the one named last changes fastest.
Arguments:
- sources: bfloat16 [2, 832, 2, 1536], P('panel', 'leaf'), may hold values from -6 to 6
- transmission: float32 [2, 832, 128], P('panel', 'leaf')
- media: int32 [2, 832, 1], P('panel', 'leaf'), may hold values from 0 to 15; in each aligned block of 52 rows (0 to 51, 52 to 103, ..., all dimensions but the last counted through in order) at most 8 rows name the same one
- sep_code: int32 [2, 16], P('panel', 'leaf'), may hold values from 0 to 7
- leaf_factors: bfloat16 [16, 2, 768, 768], P('leaf'), may hold values from -0.15625 to 0.15625
- sep_factors: bfloat16 [2, 2, 384, 384], replicated, may hold values from -0.15625 to 0.15625
Outputs:
- solutions: bfloat16 [2, 832, 2, 1536], P('panel', 'leaf')
Inputs may be any that keep to these rules, and one draw needn't show every extreme that they name: `media`: among the 52 leaves of one device (aligned blocks of rows) no library entry is named more than 8 times, a bound that some block reaches.
All inputs are finite; a program needn't handle non-finite values.
Results may differ from a plain program's by a relative error of at most 0.0065.
Values may be sent and summed in bfloat16 or wider, within the bound.
No kernel may reach another device: no remote copies, remote signals or barrier semaphores. Data moves between devices by JAX's collectives and lax.ppermute only.
A program may use at most 64 MiB of HBM per device.

v0:
```python
import math

import jax
import jax.numpy as jnp
from jax import lax
from jax.sharding import PartitionSpec as P


def from_behind(value, axis, steps):
    count = lax.axis_size(axis)
    initial, last = (max(0, -steps), min(count, count - steps))
    return lax.ppermute(value, axis, [(source, source + steps) for source in range(initial, last)])


def from_partner(value, axis, distance):
    mask = 2**distance
    pairs = [(source, source ^ mask) for source in range(lax.axis_size(axis))]
    return lax.ppermute(value, axis, pairs)


def complex_times(left, right, half):
    left_re, left_im = (left[..., :half], left[..., half:])
    right_re, right_im = (right[..., :half], right[..., half:])
    return jnp.concatenate(
        [left_re * right_re - left_im * right_im, left_re * right_im + left_im * right_re], axis=-1
    )


def block_matrix(pair):
    real_part, imag_part = (pair[0], pair[1])
    upper = jnp.concatenate([real_part, imag_part], axis=1)
    lower = jnp.concatenate([-imag_part, real_part], axis=1)
    return jnp.concatenate([upper, lower], axis=0)


def face_rows(source, width, front):
    return jnp.concatenate(
        [source[..., width - front : width], source[..., 2 * width - front :]], axis=-1
    )


def lift_face(incoming, width, front):
    gap = jnp.zeros(incoming.shape[:-1] + (width - front,), jnp.float32)
    return jnp.concatenate([gap, incoming[..., :front], gap, incoming[..., front:]], axis=-1)


def lift_top(values, width, sep):
    gap = jnp.zeros(values.shape[:-1] + (width - sep,), jnp.float32)
    return jnp.concatenate([values[..., :sep], gap, values[..., sep:], gap], axis=-1)


def trace_rows(solved, width, sep):
    return jnp.concatenate([solved[..., :sep], solved[..., width : width + sep]], axis=-1)


def other_rows(solved, width, sep):
    return jnp.concatenate([solved[..., sep:width], solved[..., width + sep :]], axis=-1)


def assemble(traces, others, width, sep):
    rest = width - sep
    return jnp.concatenate(
        [traces[..., :sep], others[..., :rest], traces[..., sep:], others[..., rest:]], axis=-1
    )


def on_device(sources, transmission, media, sep_code, leaf_factors, sep_factors):
    leaves, shots, width2 = (sources.shape[1], sources.shape[2], sources.shape[3])
    leaf_n = width2 // 2
    front = transmission.shape[2] // 2
    sep_n = sep_factors.shape[2]
    sep_lib = sep_factors.shape[0]
    nleaf = lax.axis_size("leaf")
    levels = nleaf.bit_length() - 1
    capacity = max(2, leaves * 5 // (nleaf * 2))
    source = sources[0]
    tau = transmission[0]
    face = face_rows(source, leaf_n, front).astype(jnp.float32)

    def advance(step, incoming):
        leaving = complex_times(tau[:, None, :], incoming + face, front)
        return from_behind(leaving, "panel", 1)

    arriving = lax.fori_loop(
        0, lax.axis_size("panel") - 1, advance, jnp.zeros(face.shape, jnp.float32)
    )
    rhs = (source.astype(jnp.float32) + lift_face(arriving, leaf_n, front)).astype(jnp.bfloat16)
    kinds = media[0, :, 0]
    hits = (kinds[:, None] == jnp.arange(nleaf, dtype=jnp.int32)[None, :]).astype(jnp.int32)
    rank = jnp.sum((jnp.cumsum(hits, axis=0) - hits) * hits, axis=1)
    slot = kinds * capacity + rank
    send = jnp.zeros((nleaf * capacity, shots, width2), jnp.bfloat16).at[slot].set(rhs)
    send = send.reshape(nleaf, capacity, shots, width2)
    big_leaf = block_matrix(leaf_factors[0])
    arrived = lax.all_to_all(send, "leaf", split_axis=0, concat_axis=0, tiled=True)
    solved_here = jnp.dot(arrived.reshape(-1, width2), big_leaf, preferred_element_type=jnp.float32)
    solved_here = solved_here.astype(jnp.bfloat16).reshape(arrived.shape)
    traces = lax.all_to_all(
        trace_rows(solved_here, leaf_n, sep_n), "leaf", split_axis=0, concat_axis=0, tiled=True
    ).reshape(nleaf * capacity, shots, 2 * sep_n)[slot]
    others = lax.all_to_all(
        other_rows(solved_here, leaf_n, sep_n), "leaf", split_axis=0, concat_axis=0, tiled=True
    ).reshape(nleaf * capacity, shots, width2 - 2 * sep_n)[slot]
    solved = assemble(traces, others, leaf_n, sep_n)
    own_trace = jnp.sum(traces.astype(jnp.float32), axis=0)
    own_code = sep_code.reshape(1)
    partial_sum, partial_code = (own_trace, own_code)
    level_sums, level_codes = ([], [])
    for bit in range(levels):
        other_sum, other_code = from_partner((partial_sum, partial_code), "leaf", bit)
        partial_sum = partial_sum + other_sum
        partial_code = partial_code + other_code
        level_sums.append(partial_sum)
        level_codes.append(partial_code[0])
    sep_sol = jnp.zeros((shots, 2 * sep_n), jnp.float32)
    for level in reversed(range(levels)):
        scaled = level_sums[level] * (1.0 / math.sqrt(leaves * 2 ** (level + 1)))
        chosen = lax.dynamic_index_in_dim(
            sep_factors, level_codes[level] % sep_lib, 0, keepdims=False
        )
        operand = (scaled - sep_sol).astype(jnp.bfloat16)
        sep_sol = jnp.dot(operand, block_matrix(chosen), preferred_element_type=jnp.float32)
    result = solved.astype(jnp.float32) - lift_top(sep_sol[None], leaf_n, sep_n)
    return result.astype(jnp.bfloat16)[None]


def solution(mesh):
    return jax.shard_map(
        on_device,
        mesh=mesh,
        in_specs=(
            P("panel", "leaf", None, None),
            P("panel", "leaf", None),
            P("panel", "leaf", None),
            P("panel", "leaf"),
            P("leaf", None, None, None),
            P(),
        ),
        out_specs=P("panel", "leaf", None, None),
        check_vma=False,
    )
```

profile of v0, /device:TPU:0, one launch (start us, length us, event | category | flops | bytes accessed | tf_op | source)
XLA Modules:
  0.0 107.0 jit_solution(2605050026149338928)
XLA Ops:
  2.2 4.8 %collective-permute-start = (f32[52,2,128]{2,1,0:T(2,128)S(1)}, f32[52,2,128]{2,1,0:T(2,128)S(1)}, u32[]{:S(2)}, u32[]{:S(2)}) collective-permute-start(f32[52,2,128]{2,1,0:T(2,128)S(1)} %pad_maximum_fusion.2), channel_id=1, source_target_pairs={{0,16},{1,17},{2,18},{3,19},{4,20},{5,21},{6,22},{7,23},{8,24},{9,... | collective-permute-start | bytes 159752 | tf_op jit(solution)/shard_map/while/body/eval_jaxpr/ppermute | solution.py:12
  9.6 1.8 %concatenate.84 = f32[52,2,1536]{2,1,0:T(2,128)S(1)} concatenate(f32[52,2,704]{2,1,0:T(2,128)S(1)} %broadcast_in_dim.9, f32[52,2,64]{2,1,0:T(2,128)S(1)} %get-tuple-element.50, f32[52,2,704]{2,1,0:T(2,128)S(1)} %broadcast_in_dim.9, f32[52,2,64]{2,1,0:T(2,128)S(1)} %get-tuple-element.49), dimensions={2} | concatenate | bytes 1277952 | tf_op jit(solution)/shard_map/concatenate | solution.py:44
  11.5 1.5 %add_convert_fusion = bf16[52,2,1536]{2,1,0:T(2,128)(2,1)S(1)} fusion(f32[52,2,1536]{2,1,0:T(2,128)S(1)} %concatenate.84, bf16[1,52,2,1536]{3,2,1,0:T(2,128)(2,1)} %param.6), kind=kLoop, calls=%fused_computation.48 | loop fusion | flops 479232 | bytes 1277952 | tf_op jit(solution)/shard_map/convert_element_type | solution.py:87
  13.0 1.3 %broadcast_in_dim.8 = bf16[128,2,1536]{2,1,0:T(2,128)(2,1)} broadcast(bf16[]{:T(256)} %constant.52.clone.1), dimensions={} | broadcast | bytes 786434 | tf_op jit(solution)/shard_map/broadcast_in_dim | solution.py:92
  14.2 8.1 %scatter_fusion = bf16[128,2,1536]{2,1,0:T(2,128)(2,1)} fusion(bf16[128,2,1536]{2,1,0:T(2,128)(2,1)} %broadcast_in_dim.8, s32[52]{0:T(128)S(1)} %fusion.63, bf16[52,2,1536]{2,1,0:T(2,128)(2,1)S(1)} %add_convert_fusion), kind=kCustom, calls=%fused_computation.2 | custom fusion | bytes 958672 | tf_op jit(solution)/shard_map/scatter | solution.py:92
  22.3 5.9 %all-to-all-start = ((bf16[16,8,2,1536]{3,2,1,0:T(2,128)(2,1)}), bf16[16,8,2,1536]{3,2,1,0:T(2,128)(2,1)S(1)}, u32[]{:S(2)}, u32[]{:S(2)}) async-start(bf16[16,8,2,1536]{3,2,1,0:T(2,128)(2,1)} %bitcast.6), calls=%async_computation | async-start | bytes 1572864 | tf_op jit(solution)/shard_map/all_to_all | solution.py:95
  28.3 1.1 %fusion.73 = bf16[768,768]{1,0:T(8,128)(2,1)} fusion(bf16[1,2,768,768]{3,2,1,0:T(8,128)(2,1)S(1)} %copy-done), kind=kLoop, calls=%fused_computation.91 | loop fusion | flops 589824 | bytes 2359296 | tf_op jit(solution)/shard_map/neg | solution.py:32
  29.4 1.6 %slice_bitcast_fusion = (bf16[768,768]{1,0:T(8,128)(2,1)}, bf16[768,768]{1,0:T(8,128)(2,1)}) fusion(bf16[1,2,768,768]{3,2,1,0:T(8,128)(2,1)S(1)} %copy-done), kind=kLoop, calls=%fused_computation.44 | loop fusion | bytes 4718592 | tf_op jit(solution)/shard_map/squeeze | solution.py:30
  31.0 16.0 %all-to-all-done = bf16[16,8,2,1536]{3,2,1,0:T(2,128)(2,1)S(1)} async-done(((bf16[16,8,2,1536]{3,2,1,0:T(2,128)(2,1)}), bf16[16,8,2,1536]{3,2,1,0:T(2,128)(2,1)S(1)}, u32[]{:S(2)}, u32[]{:S(2)}) %all-to-all-start) | async-done | bytes 786464 | tf_op jit(solution)/shard_map/all_to_all | solution.py:95
  47.3 3.7 %fusion.8 = bf16[256,1536]{1,0:T(8,128)(2,1)S(1)} fusion(bf16[256,1536]{1,0:T(8,128)(2,1)S(1)} %reshape.129, bf16[768,768]{1,0:T(8,128)(2,1)} %get-tuple-element.26, bf16[768,768]{1,0:T(8,128)(2,1)} %fusion.73, bf16[768,768]{1,0:T(8,128)(2,1)} %get-tuple-element.25), kind=kOutput, calls=%fused_computation.11 | convolution fusion | flops 1227227136 | bytes 5111808 | tf_op jit(solution)/shard_map/dot_general | solution.py:96
  51.9 1.1 %pad_maximum_fusion = bf16[16,8,2,768]{3,2,1,0:T(2,128)(2,1)} fusion(bf16[16,8,2,384]{3,2,1,0:T(2,128)(2,1)S(1)} %get-tuple-element.40, bf16[16,8,2,384]{3,2,1,0:T(2,128)(2,1)S(1)} %get-tuple-element.37), kind=kLoop, calls=%fused_computation.49 | loop fusion | flops 786432 | bytes 786432 | tf_op jit(solution)/shard_map/concatenate | solution.py:53
  53.0 5.5 %all-to-all-start.1 = ((bf16[16,8,2,768]{3,2,1,0:T(2,128)(2,1)}), bf16[16,8,2,768]{3,2,1,0:T(2,128)(2,1)S(1)}, u32[]{:S(2)}, u32[]{:S(2)}) async-start(bf16[16,8,2,768]{3,2,1,0:T(2,128)(2,1)} %pad_maximum_fusion), calls=%async_computation.1 | async-start | bytes 786432 | tf_op jit(solution)/shard_map/all_to_all | solution.py:98
  59.5 1.1 %pad_maximum_fusion.1 = bf16[16,8,2,768]{3,2,1,0:T(2,128)(2,1)} fusion(bf16[16,8,2,384]{3,2,1,0:T(2,128)(2,1)S(1)} %get-tuple-element.38, bf16[16,8,2,384]{3,2,1,0:T(2,128)(2,1)S(1)} %get-tuple-element.39), kind=kLoop, calls=%fused_computation.50 | loop fusion | flops 786432 | bytes 786432 | tf_op jit(solution)/shard_map/concatenate | solution.py:57
  60.6 10.0 %all-to-all-done.1 = bf16[16,8,2,768]{3,2,1,0:T(2,128)(2,1)S(1)} async-done(((bf16[16,8,2,768]{3,2,1,0:T(2,128)(2,1)}), bf16[16,8,2,768]{3,2,1,0:T(2,128)(2,1)S(1)}, u32[]{:S(2)}, u32[]{:S(2)}) %all-to-all-start.1) | async-done | bytes 393248 | tf_op jit(solution)/shard_map/all_to_all | solution.py:98
  70.6 3.6 %all-to-all-start.2 = ((bf16[16,8,2,768]{3,2,1,0:T(2,128)(2,1)}), bf16[16,8,2,768]{3,2,1,0:T(2,128)(2,1)S(1)}, u32[]{:S(2)}, u32[]{:S(2)}) async-start(bf16[16,8,2,768]{3,2,1,0:T(2,128)(2,1)} %pad_maximum_fusion.1), calls=%async_computation.2 | async-start | bytes 786432 | tf_op jit(solution)/shard_map/all_to_all | solution.py:101
  74.9 3.2 %collective-permute-start.6 = (s32[1]{0:T(128)}, s32[1]{0:T(128)}, u32[]{:S(2)}, u32[]{:S(2)}) collective-permute-start(s32[1]{0:T(128)} %add.91), channel_id=1, source_target_pairs={{0,2},{1,3},{2,0},{3,1},{4,6},{5,7},{6,4},{7,5},{8,10},{9,11},{10,... | collective-permute-start | bytes 20 | tf_op jit(solution)/shard_map/ppermute | solution.py:18
  79.3 3.2 %collective-permute-start.7 = (s32[1]{0:T(128)}, s32[1]{0:T(128)}, u32[]{:S(2)}, u32[]{:S(2)}) collective-permute-start(s32[1]{0:T(128)} %add.92), channel_id=1, source_target_pairs={{0,4},{1,5},{2,6},{3,7},{4,0},{5,1},{6,2},{7,3},{8,12},{9,13},{10,... | collective-permute-start | bytes 20 | tf_op jit(solution)/shard_map/ppermute | solution.py:18
  83.7 4.4 %collective-permute-start.8 = (s32[1]{0:T(128)}, s32[1]{0:T(128)}, u32[]{:S(2)}, u32[]{:S(2)}) collective-permute-start(s32[1]{0:T(128)} %add.93), channel_id=1, source_target_pairs={{0,8},{1,9},{2,10},{3,11},{4,12},{5,13},{6,14},{7,15},{8,0},{9,1},... | collective-permute-start | bytes 20 | tf_op jit(solution)/shard_map/ppermute | solution.py:18
  90.2 1.1 %fusion.74 = (bf16[384,384]{1,0:T(8,128)(2,1)S(1)}, bf16[384,384]{1,0:T(8,128)(2,1)S(1)}, bf16[384,384]{1,0:T(8,128)(2,1)}, bf16[384,384]{1,0:T(8,128)(2,1)}, bf...) fusion(bf16[2,2,384,384]{3,2,1,0:T(8,128)(2,1)S(1)} %copy-done., ...), kind=kLoop, calls=%fused_computation.92 | loop fusion | flops 589824 | bytes 3538964 | tf_op jit(solution)/shard_map/neg | solution.py:32
  91.4 1.7 %collective-permute-start.2 = (f32[2,768]{1,0:T(2,128)S(1)}, f32[2,768]{1,0:T(2,128)S(1)}, u32[]{:S(2)}, u32[]{:S(2)}) collective-permute-start(f32[2,768]{1,0:T(2,128)S(1)} %add.87), channel_id=1, source_target_pairs={{0,2},{1,3},{2,0},{3,1},{4,6},{5,7},{6,4},{7,5},{8,10},{9,11},{10,... | collective-permute-start | bytes 18440 | tf_op jit(solution)/shard_map/ppermute | solution.py:18
  95.1 1.6 %collective-permute-start.3 = (f32[2,768]{1,0:T(2,128)S(1)}, f32[2,768]{1,0:T(2,128)S(1)}, u32[]{:S(2)}, u32[]{:S(2)}) collective-permute-start(f32[2,768]{1,0:T(2,128)S(1)} %add.88), channel_id=1, source_target_pairs={{0,4},{1,5},{2,6},{3,7},{4,0},{5,1},{6,2},{7,3},{8,12},{9,13},{10,... | collective-permute-start | bytes 18440 | tf_op jit(solution)/shard_map/ppermute | solution.py:18
  98.7 2.9 %collective-permute-start.4 = (f32[2,768]{1,0:T(2,128)S(1)}, f32[2,768]{1,0:T(2,128)S(1)}, u32[]{:S(2)}, u32[]{:S(2)}) collective-permute-start(f32[2,768]{1,0:T(2,128)S(1)} %add.89), channel_id=1, source_target_pairs={{0,8},{1,9},{2,10},{3,11},{4,12},{5,13},{6,14},{7,15},{8,0},{9,1},... | collective-permute-start | bytes 18440 | tf_op jit(solution)/shard_map/ppermute | solution.py:18
  101.7 1.5 %collective-permute-done.4 = f32[2,768]{1,0:T(2,128)S(1)} collective-permute-done((f32[2,768]{1,0:T(2,128)S(1)}, f32[2,768]{1,0:T(2,128)S(1)}, u32[]{:S(2)}, u32[]{:S(2)}) %collective-permute-start.4) | collective-permute-done | bytes 6176 | tf_op jit(solution)/shard_map/ppermute | solution.py:18
  103.2 2.2 %subtract_convert_fusion.2 = bf16[2,768]{1,0:T(2,128)(2,1)S(1)} fusion(f32[2,768]{1,0:T(2,128)S(1)} %add.88, bf16[384,384]{1,0:T(8,128)(2,1)} %get-tuple-element.35, bf16[384,384]{1,0:T(8,128)(2,1)} %get-tuple-element.27, bf16[384,384]{1,0:T(8,128)(2,1)} %get-tuple-element.28, f32[2,768]{1,0:T(2,128)S(1)} %add.89, bf16[384,384]{1,0:T(8,128)(2,1)} %get-tuple-element.36, ...), kind=kOutput, calls=%fused_computation.75 | convolution fusion | flops 14169600 | bytes 1790976 | tf_op jit(solution)/shard_map/dot_general | solution.py:122
  (49 shorter events, 14.6 us)
Async XLA Ops:
  2.2 7.2 %collective-permute-start = (f32[52,2,128]{2,1,0:T(2,128)S(1)}, f32[52,2,128]{2,1,0:T(2,128)S(1)}, u32[]{:S(2)}, u32[]{:S(2)}) collective-permute-start(f32[52,2,128]{2,1,0:T(2,128)S(1)} %pad_maximum_fusion.2), channel_id=1, source_target_pairs={{0,16},{1,17},{2,18},{3,19},{4,20},{5,21},{6,22},{7,23},{8,24},{9,... | collective-permute-start | bytes 159752 | tf_op jit(solution)/shard_map/while/body/eval_jaxpr/ppermute | solution.py:12
  11.5 16.8 %copy-start = (bf16[1,2,768,768]{3,2,1,0:T(8,128)(2,1)S(1)}, bf16[1,2,768,768]{3,2,1,0:T(8,128)(2,1)}, u32[]{:S(2)}) copy-start(bf16[1,2,768,768]{3,2,1,0:T(8,128)(2,1)} %param.10) | copy-start | bytes 7077892
  22.3 24.7 %all-to-all-start = ((bf16[16,8,2,1536]{3,2,1,0:T(2,128)(2,1)}), bf16[16,8,2,1536]{3,2,1,0:T(2,128)(2,1)S(1)}, u32[]{:S(2)}, u32[]{:S(2)}) async-start(bf16[16,8,2,1536]{3,2,1,0:T(2,128)(2,1)} %bitcast.6), calls=%async_computation | async-start | bytes 1572864 | tf_op jit(solution)/shard_map/all_to_all | solution.py:95
  51.3 38.9 %copy-start.1 = (bf16[2,2,384,384]{3,2,1,0:T(8,128)(2,1)S(1)}, bf16[2,2,384,384]{3,2,1,0:T(8,128)(2,1)}, u32[]{:S(2)}) copy-start(bf16[2,2,384,384]{3,2,1,0:T(8,128)(2,1)} %param.11) | copy-start | bytes 3538948
  53.0 17.7 %all-to-all-start.1 = ((bf16[16,8,2,768]{3,2,1,0:T(2,128)(2,1)}), bf16[16,8,2,768]{3,2,1,0:T(2,128)(2,1)S(1)}, u32[]{:S(2)}, u32[]{:S(2)}) async-start(bf16[16,8,2,768]{3,2,1,0:T(2,128)(2,1)} %pad_maximum_fusion), calls=%async_computation.1 | async-start | bytes 786432 | tf_op jit(solution)/shard_map/all_to_all | solution.py:98
  58.4 15.8 %collective-permute-start.5 = (s32[1]{0:T(128)}, s32[1]{0:T(128)}, u32[]{:S(2)}, u32[]{:S(2)}) collective-permute-start(s32[1]{0:T(128)} %bitcast.15), channel_id=1, source_target_pairs={{0,1},{1,0},{2,3},{3,2},{4,5},{5,4},{6,7},{7,6},{8,9},{9,8},{10,11... | collective-permute-start | bytes 20 | tf_op jit(solution)/shard_map/ppermute | solution.py:18
  70.6 26.2 %all-to-all-start.2 = ((bf16[16,8,2,768]{3,2,1,0:T(2,128)(2,1)}), bf16[16,8,2,768]{3,2,1,0:T(2,128)(2,1)S(1)}, u32[]{:S(2)}, u32[]{:S(2)}) async-start(bf16[16,8,2,768]{3,2,1,0:T(2,128)(2,1)} %pad_maximum_fusion.1), calls=%async_computation.2 | async-start | bytes 786432 | tf_op jit(solution)/shard_map/all_to_all | solution.py:101
  74.9 3.8 %collective-permute-start.6 = (s32[1]{0:T(128)}, s32[1]{0:T(128)}, u32[]{:S(2)}, u32[]{:S(2)}) collective-permute-start(s32[1]{0:T(128)} %add.91), channel_id=1, source_target_pairs={{0,2},{1,3},{2,0},{3,1},{4,6},{5,7},{6,4},{7,5},{8,10},{9,11},{10,... | collective-permute-start | bytes 20 | tf_op jit(solution)/shard_map/ppermute | solution.py:18
  79.3 3.7 %collective-permute-start.7 = (s32[1]{0:T(128)}, s32[1]{0:T(128)}, u32[]{:S(2)}, u32[]{:S(2)}) collective-permute-start(s32[1]{0:T(128)} %add.92), channel_id=1, source_target_pairs={{0,4},{1,5},{2,6},{3,7},{4,0},{5,1},{6,2},{7,3},{8,12},{9,13},{10,... | collective-permute-start | bytes 20 | tf_op jit(solution)/shard_map/ppermute | solution.py:18
  83.7 4.8 %collective-permute-start.8 = (s32[1]{0:T(128)}, s32[1]{0:T(128)}, u32[]{:S(2)}, u32[]{:S(2)}) collective-permute-start(s32[1]{0:T(128)} %add.93), channel_id=1, source_target_pairs={{0,8},{1,9},{2,10},{3,11},{4,12},{5,13},{6,14},{7,15},{8,0},{9,1},... | collective-permute-start | bytes 20 | tf_op jit(solution)/shard_map/ppermute | solution.py:18
  90.1 1.2 %collective-permute-start.1 = (f32[2,768]{1,0:T(2,128)S(1)}, f32[2,768]{1,0:T(2,128)S(1)}, u32[]{:S(2)}, u32[]{:S(2)}) collective-permute-start(f32[2,768]{1,0:T(2,128)S(1)} %convert_reduce_fusion), channel_id=1, source_target_pairs={{0,1},{1,0},{2,3},{3,2},{4,5},{5,4},{6,7},{7,6},{8,9},{9,8},{10,11... | collective-permute-start | bytes 18440 | tf_op jit(solution)/shard_map/ppermute | solution.py:18
  91.4 3.7 %collective-permute-start.2 = (f32[2,768]{1,0:T(2,128)S(1)}, f32[2,768]{1,0:T(2,128)S(1)}, u32[]{:S(2)}, u32[]{:S(2)}) collective-permute-start(f32[2,768]{1,0:T(2,128)S(1)} %add.87), channel_id=1, source_target_pairs={{0,2},{1,3},{2,0},{3,1},{4,6},{5,7},{6,4},{7,5},{8,10},{9,11},{10,... | collective-permute-start | bytes 18440 | tf_op jit(solution)/shard_map/ppermute | solution.py:18
  95.1 3.6 %collective-permute-start.3 = (f32[2,768]{1,0:T(2,128)S(1)}, f32[2,768]{1,0:T(2,128)S(1)}, u32[]{:S(2)}, u32[]{:S(2)}) collective-permute-start(f32[2,768]{1,0:T(2,128)S(1)} %add.88), channel_id=1, source_target_pairs={{0,4},{1,5},{2,6},{3,7},{4,0},{5,1},{6,2},{7,3},{8,12},{9,13},{10,... | collective-permute-start | bytes 18440 | tf_op jit(solution)/shard_map/ppermute | solution.py:18
  98.7 4.5 %collective-permute-start.4 = (f32[2,768]{1,0:T(2,128)S(1)}, f32[2,768]{1,0:T(2,128)S(1)}, u32[]{:S(2)}, u32[]{:S(2)}) collective-permute-start(f32[2,768]{1,0:T(2,128)S(1)} %add.89), channel_id=1, source_target_pairs={{0,8},{1,9},{2,10},{3,11},{4,12},{5,13},{6,14},{7,15},{8,0},{9,1},... | collective-permute-start | bytes 18440 | tf_op jit(solution)/shard_map/ppermute | solution.py:18
  103.2 2.2 %copy-start.2 = (bf16[384,384]{1,0:T(8,128)(2,1)S(1)}, bf16[384,384]{1,0:T(8,128)(2,1)}, u32[]{:S(2)}) copy-start(bf16[384,384]{1,0:T(8,128)(2,1)} %get-tuple-element.33) | copy-start | bytes 884740
  103.2 2.2 %copy-start.3 = (bf16[384,384]{1,0:T(8,128)(2,1)S(1)}, bf16[384,384]{1,0:T(8,128)(2,1)}, u32[]{:S(2)}) copy-start(bf16[384,384]{1,0:T(8,128)(2,1)} %get-tuple-element.34) | copy-start | bytes 884740
where the time goes:
time: 108 us; the launch traced here: 107 us
  starting transfers between devices  37.4 us (35%)
  waiting for transfers between devices  30.9 us (29%)
  local copies, waits for them, and re-layouts  19 us (18%)
  other arithmetic  9.88 us (9%)
  matrix products  6.41 us (6%)
  between operations  3.46 us (3%)
    ppermute x8, starting transfers between devices, from_partner(): return lax.ppermute(value, axis, pairs)  17.6 us
    all_to_all x1, waiting for transfers between devices, on_device(): lax.all_to_all(send, 'leaf', split_axis=0, concat_axis=0, tiled=True)  16 us
    all_to_all x1, waiting for transfers between devices, on_device(): lax.all_to_all(trace_rows(solved_here, leaf_n, sep_n), 'leaf', split_axis...  10 us
    scatter x1, local copies, waits for them, and re-layouts, on_device(): jnp.zeros((nleaf * capacity, shots, width2), jnp.bfloat16).at[slot].set(rhs)  8.07 us
    all_to_all x1, starting transfers between devices, on_device(): lax.all_to_all(send, 'leaf', split_axis=0, concat_axis=0, tiled=True)  5.95 us
    all_to_all x1, starting transfers between devices, on_device(): lax.all_to_all(trace_rows(solved_here, leaf_n, sep_n), 'leaf', split_axis...  5.47 us
    ppermute x8, waiting for transfers between devices, from_partner(): return lax.ppermute(value, axis, pairs)  4.85 us
    ppermute x1, starting transfers between devices, from_behind(): lax.ppermute(value, axis, [(source, source + steps) for source in range(i...  4.85 us
  transfers between devices with their start and end apart: 12, of which 8 were waited for; matrix products, arithmetic and copies ran while one was open for 10% of the time, Pallas kernels for 0%

commit v1 on v0

v1 whole, which is shorter than its diff:
```python
import functools
import math

import jax
import jax.numpy as jnp
from jax import lax
from jax.experimental import pallas as pl
from jax.experimental.pallas import tpu as pltpu
from jax.sharding import PartitionSpec as P

F32 = jnp.float32
BF16 = jnp.bfloat16
VMEM = pltpu.VMEM


def from_behind(value, axis):
    count = lax.axis_size(axis)
    return lax.ppermute(value, axis, [(at, at + 1) for at in range(count - 1)])


def from_partner(value, axis, bit):
    pairs = [(at, at ^ (1 << bit)) for at in range(lax.axis_size(axis))]
    return lax.ppermute(value, axis, pairs)


def dot(left, right):
    return jnp.dot(left, right, preferred_element_type=F32)


def slot_of(kinds_ref, shots, capacity):
    kinds = kinds_ref[...]
    count = kinds.shape[1]
    before = lax.broadcasted_iota(jnp.int32, (count, count), 0)
    after = lax.broadcasted_iota(jnp.int32, (count, count), 1)
    across = jnp.broadcast_to(kinds, (count, count))
    down_kinds = jnp.sum(jnp.where(before == after, across, 0), axis=1, keepdims=True)
    down = jnp.broadcast_to(down_kinds, (count, count))
    same = (across == down) & (before % shots == after % shots)
    rank_row = jnp.sum((same & (before < after)).astype(jnp.int32), axis=0, keepdims=True)
    rank_col = jnp.sum((same & (after < before)).astype(jnp.int32), axis=1, keepdims=True)
    shot_row = lax.broadcasted_iota(jnp.int32, (1, count), 1) % shots
    shot_col = lax.broadcasted_iota(jnp.int32, (count, 1), 0) % shots
    row = (kinds * shots + shot_row) * capacity + rank_row
    col = (down_kinds * shots + shot_col) * capacity + rank_col
    return row, col


def dispatch_kernel(shots, capacity, front, kinds_ref, rows_ref, arriving_ref, send_ref, rhs_ref):
    width2 = rows_ref.shape[1]
    leaf_n = width2 // 2
    rhs_ref[...] = rows_ref[...]
    for part in range(2):
        face = pl.ds((part + 1) * leaf_n - 2 * front, 2 * front)
        incoming = arriving_ref[...]
        place = lax.broadcasted_iota(jnp.int32, incoming.shape, 1)
        if part == 0:
            incoming = pltpu.roll(incoming, front, 1)
        incoming = jnp.where(place >= front, incoming, 0.0)
        rhs_ref[:, face] = (rows_ref[:, face].astype(F32) + incoming).astype(BF16)
    row, _ = slot_of(kinds_ref, shots, capacity)
    slots = send_ref.shape[0]
    place = lax.broadcasted_iota(jnp.int32, (slots, row.shape[1]), 0)
    pick = (place == row).astype(F32).astype(BF16)
    send_ref[...] = dot(pick, rhs_ref[...]).astype(BF16)


def leaf_kernel(capacity, sep_n, arrived_ref, factor_ref, solved_ref, sums_ref):
    leaf_n = factor_ref.shape[1]
    real, imag = arrived_ref[:, :leaf_n], arrived_ref[:, leaf_n:]
    factor_re, factor_im = factor_ref[0], factor_ref[1]
    solved_ref[:, :leaf_n] = (dot(real, factor_re) - dot(imag, factor_im)).astype(BF16)
    solved_ref[:, leaf_n:] = (dot(real, factor_im) + dot(imag, factor_re)).astype(BF16)
    groups, slots = sums_ref.shape[0], solved_ref.shape[0]
    group = lax.broadcasted_iota(jnp.int32, (groups, slots), 0)
    place = lax.broadcasted_iota(jnp.int32, (groups, slots), 1)
    member = (place // capacity == group).astype(F32).astype(BF16)
    sums_ref[:, :sep_n] = dot(member, solved_ref[:, :sep_n])
    sums_ref[:, sep_n:] = dot(member, solved_ref[:, leaf_n : leaf_n + sep_n])


def tree_kernel(scales, codes_ref, sums_ref, factors_ref, out_ref):
    sep_n = factors_ref.shape[2]
    above = jnp.zeros(out_ref.shape, F32)
    for level in reversed(range(len(scales))):
        operand = (sums_ref[level] * scales[level] - above).astype(BF16)
        real, imag = operand[:, :sep_n], operand[:, sep_n:]
        factor = factors_ref[codes_ref[level]]
        above = jnp.concatenate(
            [
                dot(real, factor[0]) - dot(imag, factor[1]),
                dot(real, factor[1]) + dot(imag, factor[0]),
            ],
            axis=1,
        )
    out_ref[...] = above


def result_kernel(shots, capacity, kinds_ref, back_ref, above_ref, out_ref):
    count, width2 = out_ref.shape
    leaf_n = width2 // 2
    sep_n = above_ref.shape[1] // 2
    _, col = slot_of(kinds_ref, shots, capacity)
    place = lax.broadcasted_iota(jnp.int32, (count, back_ref.shape[0]), 1)
    pick = (place == col).astype(F32).astype(BF16)
    solved = dot(pick, back_ref[...])
    shot = lax.broadcasted_iota(jnp.int32, (count, 2 * sep_n), 0) % shots
    lifted = jnp.zeros((count, 2 * sep_n), F32)
    for at in range(shots):
        lifted = jnp.where(shot == at, above_ref[at : at + 1, :], lifted)
    for part in range(2):
        start = part * leaf_n
        top = solved[:, start : start + sep_n] - lifted[:, part * sep_n : (part + 1) * sep_n]
        out_ref[:, start : start + sep_n] = top.astype(BF16)
        out_ref[:, start + sep_n : start + leaf_n] = solved[:, start + sep_n : start + leaf_n].astype(BF16)


def call(kernel, out_shape, args, smem=(), scratch=(), limit=32):
    return pl.pallas_call(
        kernel,
        out_shape=out_shape,
        in_specs=[
            pl.BlockSpec(memory_space=pltpu.SMEM if at in smem else VMEM) for at in range(len(args))
        ],
        out_specs=jax.tree.map(lambda _: pl.BlockSpec(memory_space=VMEM), out_shape),
        scratch_shapes=list(scratch),
        compiler_params=pltpu.CompilerParams(vmem_limit_bytes=limit * 2**20),
    )(*args)


def node_sums(own_sums, code, levels):
    me = lax.axis_index("leaf")
    positions = own_sums.shape[0]
    mine = jnp.arange(positions, dtype=jnp.int32) == me
    codes = jnp.where(mine, code, 0).astype(F32)
    codes = jnp.broadcast_to(codes[:, None, None], own_sums.shape[:2] + (128,))
    share = jnp.concatenate([own_sums, codes], axis=-1)
    shares = []
    for _ in range(levels):
        share = share.reshape((share.shape[0] // 2, 2) + share.shape[1:]).sum(axis=1)
        shares.append(share)
    for bit in range(levels):
        high = (me >> bit) & 1
        keep, send = [], []
        for level, share in enumerate(shares):
            if level < bit:
                pairs = share.reshape((share.shape[0] // 2, 2) + share.shape[1:])
                keep.append(jnp.where(high == 1, pairs[:, 1], pairs[:, 0]))
                send.append(jnp.where(high == 1, pairs[:, 0], pairs[:, 1]))
            else:
                keep.append(share)
                send.append(share)
        arrived = from_partner(jnp.concatenate(send, axis=0), "leaf", bit)
        ends = [0]
        for share in keep:
            ends.append(ends[-1] + share.shape[0])
        shares = [share + arrived[a:b] for share, a, b in zip(keep, ends[:-1], ends[1:])]
    path = jnp.concatenate(shares, axis=0)
    return path


def on_device(sources, transmission, media, sep_code, leaf_factors, sep_factors):
    leaves, shots, width2 = sources.shape[1:]
    leaf_n = width2 // 2
    front = transmission.shape[2] // 2
    sep_n = sep_factors.shape[2]
    sep_lib = sep_factors.shape[0]
    nleaf = lax.axis_size("leaf")
    levels = nleaf.bit_length() - 1
    capacity = max(2, leaves * 5 // (nleaf * 2))
    slots = nleaf * capacity * shots
    source, tau = sources[0], transmission[0][:, None, :]
    tau_re, tau_im = tau[..., :front], tau[..., front:]
    face_re = source[..., leaf_n - front : leaf_n].astype(F32)
    face_im = source[..., 2 * leaf_n - front :].astype(F32)
    arriving = jnp.zeros((leaves, shots, 2 * front), F32)
    for _ in range(lax.axis_size("panel") - 1):
        real, imag = arriving[..., :front] + face_re, arriving[..., front:] + face_im
        leaving = jnp.concatenate([tau_re * real - tau_im * imag, tau_re * imag + tau_im * real], axis=-1)
        arriving = from_behind(leaving, "panel")
    kinds = jnp.repeat(media[0, :, 0], shots)[None, :]
    rows = leaves * shots
    send = call(
        functools.partial(dispatch_kernel, shots, capacity, front),
        jax.ShapeDtypeStruct((slots, width2), BF16),
        (kinds, source.reshape(rows, width2), arriving.reshape(rows, 2 * front)),
        scratch=[pltpu.VMEM((rows, width2), BF16)],
    )
    split = (nleaf, capacity * shots, width2)
    arrived = lax.all_to_all(send.reshape(split), "leaf", split_axis=0, concat_axis=0, tiled=True)
    solved, sums = call(
        functools.partial(leaf_kernel, capacity, sep_n),
        (
            jax.ShapeDtypeStruct((slots, width2), BF16),
            jax.ShapeDtypeStruct((nleaf * shots, 2 * sep_n), F32),
        ),
        (arrived.reshape(slots, width2), leaf_factors[0]),
    )
    back = lax.all_to_all(solved.reshape(split), "leaf", split_axis=0, concat_axis=0, tiled=True)
    path = node_sums(sums.reshape(nleaf, shots, 2 * sep_n), sep_code[0, 0], levels)
    codes = path[:, 0, 2 * sep_n].astype(jnp.int32) % sep_lib
    scales = [1.0 / math.sqrt(leaves * 2 ** (level + 1)) for level in range(levels)]
    above = call(
        functools.partial(tree_kernel, scales),
        jax.ShapeDtypeStruct((shots, 2 * sep_n), F32),
        (codes, path[..., : 2 * sep_n], sep_factors),
        smem=(0,),
    )
    result = call(
        functools.partial(result_kernel, shots, capacity),
        jax.ShapeDtypeStruct((rows, width2), BF16),
        (kinds, back.reshape(slots, width2), above),
    )
    return result.reshape(1, leaves, shots, width2)


def solution(mesh):
    return jax.shard_map(
        on_device,
        mesh=mesh,
        in_specs=(
            P("panel", "leaf", None, None),
            P("panel", "leaf", None),
            P("panel", "leaf", None),
            P("panel", "leaf"),
            P("leaf", None, None, None),
            P(),
        ),
        out_specs=P("panel", "leaf", None, None),
        check_vma=False,
    )
```

time: 108 us -> 79.3 us (0.73)
  starting transfers between devices: 37.4 us -> 22.1 us
  local copies, waits for them, and re-layouts: 19 us -> 7.9 us
  waiting for transfers between devices: 30.9 us -> 41.3 us
  other arithmetic: 9.88 us -> 1.71 us
  matrix products: 6.41 us -> 0 us
  Pallas kernels: 0 us -> 4.92 us
  between operations: 3.46 us -> 0.94 us
    ppermute x8 -> x4, waiting for transfers between devices: 4.85 us -> 23.2 us  [from_partner(): return lax.ppermute(value, axis, pairs)]
    ppermute x8 -> x4, starting transfers between devices: 17.6 us -> 7.53 us  [from_partner(): return lax.ppermute(value, axis, pairs)]
    scatter x1 -> x0, local copies, waits for them, and re-layouts: 8.07 us -> none  [on_device(): jnp.zeros((nleaf * capacity, shots, width2), jnp.bfloat16).at[slot].set(rhs)]
    all_to_all x3 -> x2, waiting for transfers between devices: 26 us -> 18 us  [the longest x1 18 us: on_device(): lax.all_to_all(send.reshape(split), 'leaf', split_axis=0, concat_axis=0,...]
    dot_general x3 -> x0, matrix products: 6.41 us -> none  [the longest x1 3.72 us: on_device(): jnp.dot(arrived.reshape(-1, width2), big_leaf, preferred_element_type=jnp...]
    all_to_all x3 -> x2, starting transfers between devices: 15 us -> 9.69 us  [the longest x1 5.94 us: on_device(): lax.all_to_all(send.reshape(split), 'leaf', split_axis=0, concat_axis=0,...]
    pallas_call x0 -> x4, Pallas kernels: none -> 4.92 us  [call(): pl.pallas_call(kernel, out_shape=out_shape, in_specs=[pl.BlockSpec(memory...]
    convert_element_type x4 -> x2, other arithmetic: 3.37 us -> 0.17 us  [the longest x1 0.16 us: on_device(): codes = path[:, 0, 2 * sep_n].astype(jnp.int32) % sep_lib]
  transfers between devices with their start and end apart: 12 -> 7, of which waited for: 8 -> 4; matrix products, arithmetic and copies ran while one was open for 10% -> 3% of each run, Pallas kernels for 0% -> 2%
where the time goes in v1:
time: 79.3 us; the launch traced here: 78.8 us
  waiting for transfers between devices  41.3 us (52%)
  starting transfers between devices  22.1 us (28%)
  local copies, waits for them, and re-layouts  7.9 us (10%)
  Pallas kernels  4.92 us (6%)
  other arithmetic  1.71 us (2%)
  between operations  0.94 us (1%)
    ppermute x4, waiting for transfers between devices, from_partner(): return lax.ppermute(value, axis, pairs)  23.2 us
    all_to_all x1, waiting for transfers between devices, on_device(): lax.all_to_all(send.reshape(split), 'leaf', split_axis=0, concat_axis=0,...  18 us
    ppermute x4, starting transfers between devices, from_partner(): return lax.ppermute(value, axis, pairs)  7.53 us
    all_to_all x1, starting transfers between devices, on_device(): lax.all_to_all(send.reshape(split), 'leaf', split_axis=0, concat_axis=0,...  5.94 us
    pallas_call x4, Pallas kernels, call(): pl.pallas_call(kernel, out_shape=out_shape, in_specs=[pl.BlockSpec(memory...  4.92 us
    ppermute x1, starting transfers between devices, from_behind(): return lax.ppermute(value, axis, [(at, at + 1) for at in range(count - 1)])  4.85 us
    all_to_all x1, starting transfers between devices, on_device(): lax.all_to_all(solved.reshape(split), 'leaf', split_axis=0, concat_axis=0...  3.75 us
    unnamed x13, local copies, waits for them, and re-layouts  2.97 us
  transfers between devices with their start and end apart: 7, of which 4 were waited for; matrix products, arithmetic and copies ran while one was open for 3% of the time, Pallas kernels for 2%

profile of v1, /device:TPU:0, one launch (start us, length us, event | category | flops | bytes accessed | tf_op | source)
XLA Modules:
  0.0 78.8 jit_solution(17190670863399326089)
XLA Ops:
  0.0 1.0 %fusion.9 = (f32[52,1,64]{2,1,0:T(1,128)S(1)}, f32[52,1,64]{2,1,0:T(1,128)S(1)}) fusion(f32[52,1,128]{2,1,0:T(1,128)} %bitcast.102), kind=kLoop, calls=%fused_computation.60 | loop fusion | bytes 53248 | tf_op jit(solution)/shard_map/slice | solution.py:172
  1.0 0.9 %fusion = (f32[52,2,64]{2,1,0:T(2,128)S(1)}, f32[52,2,64]{2,1,0:T(2,128)S(1)}) fusion(f32[52,64]{1,0:T(8,128)S(1)} %get-tuple-element.24, f32[52,64]{1,0:T(8,128)S(1)} %get-tuple-element.25, bf16[52,2,1536]{2,1,0:T(2,128)(2,1)} %bitcast.97), kind=kLoop, calls=%fused_computation.9 | loop fusion | flops 53248 | bytes 106496 | tf_op jit(solution)/shard_map/sub | solution.py:178
  2.1 4.8 %collective-permute-start = (f32[52,2,128]{2,1,0:T(2,128)S(1)}, f32[52,2,128]{2,1,0:T(2,128)S(1)}, u32[]{:S(2)}, u32[]{:S(2)}) collective-permute-start(f32[52,2,128]{2,1,0:T(2,128)S(1)} %pad_maximum_fusion.3), channel_id=1, source_target_pairs={{0,16},{1,17},{2,18},{3,19},{4,20},{5,21},{6,22},{7,23},{8,24},{9,... | collective-permute-start | bytes 159752 | tf_op jit(solution)/shard_map/ppermute | solution.py:18
  6.9 1.1 %reshape_squeeze.3.rows_ref = bf16[104,1536]{1,0:T(8,128)(2,1)S(1)} reshape(bf16[1,52,2,1536]{3,2,1,0:T(2,128)(2,1)} %param.6) | data formatting | bytes 638976 | tf_op jit(solution)/shard_map/reshape;squeeze | solution.py:185
  8.0 0.7 broadcast_in_dim.17
  8.9 0.6 copy-done.4
  9.5 0.8 %copy-done.5 = f32[52,2,128]{2,1,0:T(2,128)S(1)} copy-done((f32[52,2,128]{2,1,0:T(2,128)S(1)}, f32[52,2,128]{2,1,0:T(2,128)}, u32[]{:S(2)}) %copy-start.5) | copy-done | bytes 53272
  10.3 1.4 %shard_map.64 = bf16[256,1536]{1,0:T(8,128)(2,1)} custom-call(s32[1,104]{1,0:T(1,128)S(1)} %broadcast_in_dim_reshape.3.kinds_ref, bf16[104,1536]{1,0:T(8,128)(2,1)S(1)} %reshape_squeeze.3.rows_ref, f32[104,128]{1,0:T(8,128)S(1)} %bitcast.94), custom_call_target="tpu_custom_call" | custom-call | tf_op jit(solution)/shard_map/pallas_call | solution.py:118
  11.7 5.9 %all-to-all-start = ((bf16[16,16,1536]{2,1,0:T(8,128)(2,1)}), bf16[16,16,1536]{2,1,0:T(8,128)(2,1)S(1)}, u32[]{:S(2)}, u32[]{:S(2)}) async-start(bf16[16,16,1536]{2,1,0:T(8,128)(2,1)} %bitcast.4), calls=%async_computation | async-start | bytes 1572864 | tf_op jit(solution)/shard_map/all_to_all | solution.py:189
  18.3 18.0 %all-to-all-done = bf16[16,16,1536]{2,1,0:T(8,128)(2,1)S(1)} async-done(((bf16[16,16,1536]{2,1,0:T(8,128)(2,1)}), bf16[16,16,1536]{2,1,0:T(8,128)(2,1)S(1)}, u32[]{:S(2)}, u32[]{:S(2)}) %all-to-all-start) | async-done | bytes 786464 | tf_op jit(solution)/shard_map/all_to_all | solution.py:189
  36.3 1.5 %shard_map.65 = (bf16[256,1536]{1,0:T(8,128)(2,1)S(1)}, f32[32,768]{1,0:T(8,128)S(1)}) custom-call(bf16[256,1536]{1,0:T(8,128)(2,1)S(1)} %bitcast.91, bf16[2,768,768]{2,1,0:T(8,128)(2,1)S(1)} %bitcast.92), custom_call_target="tpu_custom_call" | custom-call | tf_op jit(solution)/shard_map/pallas_call | solution.py:118
  37.8 0.9 %copy-done.2 = bf16[256,1536]{1,0:T(8,128)(2,1)} copy-done((bf16[256,1536]{1,0:T(8,128)(2,1)}, bf16[256,1536]{1,0:T(8,128)(2,1)S(1)}, u32[]{:S(2)}) %copy-start.2) | copy-done | bytes 786456
  38.7 0.6 copy-done.3
  39.4 1.0 %concatenate.25 = f32[8,2,2,768]{3,2,1,0:T(2,128)S(1)} reshape(f32[32,768]{1,0:T(8,128)} %copy-done.3) | data formatting | bytes 196608 | tf_op jit(solution)/shard_map/concatenate | solution.py:136
  41.0 1.1 %collective-permute-done.1 = f32[15,2,896]{2,1,0:T(2,128)S(1)} collective-permute-done((f32[15,2,896]{2,1,0:T(2,128)S(1)}, f32[15,2,896]{2,1,0:T(2,128)S(1)}, u32[]{:S(2)}, u32[]{:S(2)}) %collective-permute-start.1) | collective-permute-done | bytes 107552 | tf_op jit(solution)/shard_map/ppermute | solution.py:23
  42.2 1.6 %collective-permute-start.2 = (f32[11,2,896]{2,1,0:T(2,128)S(1)}, f32[11,2,896]{2,1,0:T(2,128)S(1)}, u32[]{:S(2)}, u32[]{:S(2)}) collective-permute-start(f32[11,2,896]{2,1,0:T(2,128)S(1)} %pad_maximum_fusion.2), channel_id=1, source_target_pairs={{0,2},{1,3},{2,0},{3,1},{4,6},{5,7},{6,4},{7,5},{8,10},{9,11},{10,... | collective-permute-start | bytes 236552 | tf_op jit(solution)/shard_map/ppermute | solution.py:23
  43.8 3.0 %collective-permute-done.2 = f32[11,2,896]{2,1,0:T(2,128)S(1)} collective-permute-done((f32[11,2,896]{2,1,0:T(2,128)S(1)}, f32[11,2,896]{2,1,0:T(2,128)S(1)}, u32[]{:S(2)}, u32[]{:S(2)}) %collective-permute-start.2) | collective-permute-done | bytes 78880 | tf_op jit(solution)/shard_map/ppermute | solution.py:23
  47.0 2.7 %collective-permute-start.3 = (f32[7,2,896]{2,1,0:T(2,128)S(1)}, f32[7,2,896]{2,1,0:T(2,128)S(1)}, u32[]{:S(2)}, u32[]{:S(2)}) collective-permute-start(f32[7,2,896]{2,1,0:T(2,128)S(1)} %pad_maximum_fusion.4), channel_id=1, source_target_pairs={{0,4},{1,5},{2,6},{3,7},{4,0},{5,1},{6,2},{7,3},{8,12},{9,13},{10,... | collective-permute-start | bytes 150536 | tf_op jit(solution)/shard_map/ppermute | solution.py:23
  49.7 3.8 %all-to-all-start.1 = ((bf16[16,16,1536]{2,1,0:T(8,128)(2,1)}), bf16[16,16,1536]{2,1,0:T(8,128)(2,1)S(1)}, u32[]{:S(2)}, u32[]{:S(2)}) async-start(bf16[16,16,1536]{2,1,0:T(8,128)(2,1)} %bitcast.93), calls=%async_computation.1 | async-start | bytes 1572864 | tf_op jit(solution)/shard_map/all_to_all | solution.py:198
  53.6 2.9 %collective-permute-start.4 = (f32[4,2,896]{2,1,0:T(2,128)S(1)}, f32[4,2,896]{2,1,0:T(2,128)S(1)}, u32[]{:S(2)}, u32[]{:S(2)}) collective-permute-start(f32[4,2,896]{2,1,0:T(2,128)S(1)} %pad_maximum_fusion.5), channel_id=1, source_target_pairs={{0,8},{1,9},{2,10},{3,11},{4,12},{5,13},{6,14},{7,15},{8,0},{9,1},... | collective-permute-start | bytes 86024 | tf_op jit(solution)/shard_map/ppermute | solution.py:23
  56.5 19.1 %collective-permute-done.4 = f32[4,2,896]{2,1,0:T(2,128)S(1)} collective-permute-done((f32[4,2,896]{2,1,0:T(2,128)S(1)}, f32[4,2,896]{2,1,0:T(2,128)S(1)}, u32[]{:S(2)}, u32[]{:S(2)}) %collective-permute-start.4) | collective-permute-done | bytes 28704 | tf_op jit(solution)/shard_map/ppermute | solution.py:23
  75.9 1.6 %shard_map.66.above_ref = f32[2,768]{1,0:T(2,128)S(1)} custom-call(s32[4]{0:T(128)S(1)} %and_select_fusion.codes_ref, f32[4,2,768]{2,1,0:T(2,128)S(1)} %pad_maximum_fusion.6.sums_ref, bf16[2,2,384,384]{3,2,1,0:T(8,128)(2,1)S(1)} %copy-done.1), custom_call_target="tpu_custom_call" | custom-call | tf_op jit(solution)/shard_map/pallas_call | solution.py:118
  77.5 0.4 shard_map.67
  78.0 0.8 %reshape.215 = bf16[1,52,2,1536]{3,2,1,0:T(2,128)(2,1)} reshape(bf16[104,1536]{1,0:T(8,128)(2,1)S(1)} %shard_map.67) | data formatting | bytes 638976 | tf_op jit(solution)/shard_map/reshape | solution.py:213
  (43 shorter events, 1.4 us)
Async XLA Ops:
  0.0 36.3 %copy-start = (bf16[1,2,768,768]{3,2,1,0:T(8,128)(2,1)S(1)}, bf16[1,2,768,768]{3,2,1,0:T(8,128)(2,1)}, u32[]{:S(2)}) copy-start(bf16[1,2,768,768]{3,2,1,0:T(8,128)(2,1)} %param.10) | copy-start | bytes 7077892
  2.1 6.8 %collective-permute-start = (f32[52,2,128]{2,1,0:T(2,128)S(1)}, f32[52,2,128]{2,1,0:T(2,128)S(1)}, u32[]{:S(2)}, u32[]{:S(2)}) collective-permute-start(f32[52,2,128]{2,1,0:T(2,128)S(1)} %pad_maximum_fusion.3), channel_id=1, source_target_pairs={{0,16},{1,17},{2,18},{3,19},{4,20},{5,21},{6,22},{7,23},{8,24},{9,... | collective-permute-start | bytes 159752 | tf_op jit(solution)/shard_map/ppermute | solution.py:18
  8.9 0.6 copy-start.4
  9.5 0.8 %copy-start.5 = (f32[52,2,128]{2,1,0:T(2,128)S(1)}, f32[52,2,128]{2,1,0:T(2,128)}, u32[]{:S(2)}) copy-start(f32[52,2,128]{2,1,0:T(2,128)} %copy-done.4) | copy-start | bytes 159748
  11.7 24.7 %all-to-all-start = ((bf16[16,16,1536]{2,1,0:T(8,128)(2,1)}), bf16[16,16,1536]{2,1,0:T(8,128)(2,1)S(1)}, u32[]{:S(2)}, u32[]{:S(2)}) async-start(bf16[16,16,1536]{2,1,0:T(8,128)(2,1)} %bitcast.4), calls=%async_computation | async-start | bytes 1572864 | tf_op jit(solution)/shard_map/all_to_all | solution.py:189
  37.8 0.9 %copy-start.2 = (bf16[256,1536]{1,0:T(8,128)(2,1)}, bf16[256,1536]{1,0:T(8,128)(2,1)S(1)}, u32[]{:S(2)}) copy-start(bf16[256,1536]{1,0:T(8,128)(2,1)S(1)} %get-tuple-element.7) | copy-start | bytes 2359300
  38.7 0.6 copy-start.3
  39.4 36.5 %copy-start.1 = (bf16[2,2,384,384]{3,2,1,0:T(8,128)(2,1)S(1)}, bf16[2,2,384,384]{3,2,1,0:T(8,128)(2,1)}, u32[]{:S(2)}) copy-start(bf16[2,2,384,384]{3,2,1,0:T(8,128)(2,1)} %factors_ref.1) | copy-start | bytes 3538948
  40.7 1.4 %collective-permute-start.1 = (f32[15,2,896]{2,1,0:T(2,128)S(1)}, f32[15,2,896]{2,1,0:T(2,128)S(1)}, u32[]{:S(2)}, u32[]{:S(2)}) collective-permute-start(f32[15,2,896]{2,1,0:T(2,128)S(1)} %pad_maximum_fusion.1), channel_id=1, source_target_pairs={{0,1},{1,0},{2,3},{3,2},{4,5},{5,4},{6,7},{7,6},{8,9},{9,8},{10,11... | collective-permute-start | bytes 322568 | tf_op jit(solution)/shard_map/ppermute | solution.py:23
  42.2 4.6 %collective-permute-start.2 = (f32[11,2,896]{2,1,0:T(2,128)S(1)}, f32[11,2,896]{2,1,0:T(2,128)S(1)}, u32[]{:S(2)}, u32[]{:S(2)}) collective-permute-start(f32[11,2,896]{2,1,0:T(2,128)S(1)} %pad_maximum_fusion.2), channel_id=1, source_target_pairs={{0,2},{1,3},{2,0},{3,1},{4,6},{5,7},{6,4},{7,5},{8,10},{9,11},{10,... | collective-permute-start | bytes 236552 | tf_op jit(solution)/shard_map/ppermute | solution.py:23
  47.0 6.5 %collective-permute-start.3 = (f32[7,2,896]{2,1,0:T(2,128)S(1)}, f32[7,2,896]{2,1,0:T(2,128)S(1)}, u32[]{:S(2)}, u32[]{:S(2)}) collective-permute-start(f32[7,2,896]{2,1,0:T(2,128)S(1)} %pad_maximum_fusion.4), channel_id=1, source_target_pairs={{0,4},{1,5},{2,6},{3,7},{4,0},{5,1},{6,2},{7,3},{8,12},{9,13},{10,... | collective-permute-start | bytes 150536 | tf_op jit(solution)/shard_map/ppermute | solution.py:23
  49.7 27.8 %all-to-all-start.1 = ((bf16[16,16,1536]{2,1,0:T(8,128)(2,1)}), bf16[16,16,1536]{2,1,0:T(8,128)(2,1)S(1)}, u32[]{:S(2)}, u32[]{:S(2)}) async-start(bf16[16,16,1536]{2,1,0:T(8,128)(2,1)} %bitcast.93), calls=%async_computation.1 | async-start | bytes 1572864 | tf_op jit(solution)/shard_map/all_to_all | solution.py:198
  53.6 22.0 %collective-permute-start.4 = (f32[4,2,896]{2,1,0:T(2,128)S(1)}, f32[4,2,896]{2,1,0:T(2,128)S(1)}, u32[]{:S(2)}, u32[]{:S(2)}) collective-permute-start(f32[4,2,896]{2,1,0:T(2,128)S(1)} %pad_maximum_fusion.5), channel_id=1, source_target_pairs={{0,8},{1,9},{2,10},{3,11},{4,12},{5,13},{6,14},{7,15},{8,0},{9,1},... | collective-permute-start | bytes 86024 | tf_op jit(solution)/shard_map/ppermute | solution.py:23

commit v2 on v1

v2 whole, which is shorter than its diff:
```python
import functools
import math

import jax
import jax.numpy as jnp
from jax import lax
from jax.experimental import pallas as pl
from jax.experimental.pallas import tpu as pltpu
from jax.sharding import PartitionSpec as P

F32 = jnp.float32
BF16 = jnp.bfloat16
VMEM = pltpu.VMEM
LANES = 128


def from_behind(value, axis):
    count = lax.axis_size(axis)
    return lax.ppermute(value, axis, [(at, at + 1) for at in range(count - 1)])


def dot(left, right):
    return jnp.dot(left, right, preferred_element_type=F32)


def slot_of(kinds_ref, shots, capacity):
    kinds = kinds_ref[...]
    count = kinds.shape[1]
    before = lax.broadcasted_iota(jnp.int32, (count, count), 0)
    after = lax.broadcasted_iota(jnp.int32, (count, count), 1)
    across = jnp.broadcast_to(kinds, (count, count))
    down_kinds = jnp.sum(jnp.where(before == after, across, 0), axis=1, keepdims=True)
    down = jnp.broadcast_to(down_kinds, (count, count))
    same = (across == down) & (before % shots == after % shots)
    rank_row = jnp.sum((same & (before < after)).astype(jnp.int32), axis=0, keepdims=True)
    rank_col = jnp.sum((same & (after < before)).astype(jnp.int32), axis=1, keepdims=True)
    shot_row = lax.broadcasted_iota(jnp.int32, (1, count), 1) % shots
    shot_col = lax.broadcasted_iota(jnp.int32, (count, 1), 0) % shots
    row = (kinds * shots + shot_row) * capacity + rank_row
    col = (down_kinds * shots + shot_col) * capacity + rank_col
    return row, col


def dispatch_kernel(shots, capacity, front, kinds_ref, rows_ref, arriving_ref, out_ref, rhs_ref, send_ref, sems):
    width2 = rows_ref.shape[1]
    leaf_n = width2 // 2
    rhs_ref[...] = rows_ref[...]
    for part in range(2):
        face = pl.ds((part + 1) * leaf_n - 2 * front, 2 * front)
        incoming = arriving_ref[...]
        place = lax.broadcasted_iota(jnp.int32, incoming.shape, 1)
        if part == 0:
            incoming = pltpu.roll(incoming, front, 1)
        incoming = jnp.where(place >= front, incoming, 0.0)
        rhs_ref[:, face] = (rows_ref[:, face].astype(F32) + incoming).astype(BF16)
    row, _ = slot_of(kinds_ref, shots, capacity)
    slots = send_ref.shape[0]
    place = lax.broadcasted_iota(jnp.int32, (slots, row.shape[1]), 0)
    pick = (place == row).astype(F32).astype(BF16)
    copies = []
    for part in range(2):
        columns = pl.ds(part * leaf_n, leaf_n)
        send_ref[:, columns] = dot(pick, rhs_ref[:, columns]).astype(BF16)
        copies.append(pltpu.make_async_copy(send_ref.at[:, columns], out_ref.at[:, columns], sems.at[part]))
        copies[part].start()
    for copy in copies:
        copy.wait()


def leaf_kernel(capacity, shots, levels, sep_n, place_ref, arrived_ref, factor_ref, out_ref, solved_ref, sems):
    leaf_n = factor_ref.shape[1]
    block = capacity * shots
    slots = solved_ref.shape[0]
    real, imag = arrived_ref[:, :leaf_n], arrived_ref[:, leaf_n:]
    factor_re, factor_im = factor_ref[0], factor_ref[1]

    def leave(part, start, size):
        columns = pl.ds(start, size)
        copy = pltpu.make_async_copy(solved_ref.at[:, columns], out_ref.at[:, columns], sems.at[part])
        copy.start()
        return copy

    solved_ref[:, :leaf_n] = (dot(real, factor_re) - dot(imag, factor_im)).astype(BF16)
    copies = [leave(0, 0, leaf_n)]
    solved_ref[:, leaf_n : 2 * leaf_n] = (dot(real, factor_im) + dot(imag, factor_re)).astype(BF16)
    copies.append(leave(1, leaf_n, leaf_n))
    row = lax.broadcasted_iota(jnp.int32, (slots, slots), 0)
    col = lax.broadcasted_iota(jnp.int32, (slots, slots), 1)
    col_shot = col // capacity % shots
    first = 2 * leaf_n
    for start in range(0, 2 * levels * shots, block):
        entry = start + row % block
        level = entry // shots % levels
        near = (row // block) >> (level + 1) == (col // block) >> (level + 1)
        member = near & (entry % shots == col_shot) & (entry < 2 * levels * shots)
        total = jnp.zeros((slots, sep_n), F32)
        for part in range(2):
            pick = (member & (entry // (levels * shots) == part)).astype(F32).astype(BF16)
            total = total + dot(pick, solved_ref[:, part * leaf_n : part * leaf_n + sep_n])
        solved_ref[:, first : first + sep_n] = total.astype(BF16)
        first = first + sep_n
    row = lax.broadcasted_iota(jnp.int32, (slots, LANES), 0)
    level = lax.broadcasted_iota(jnp.int32, (slots, LANES), 1)
    me, code = place_ref[0], place_ref[1]
    near = ((row // block) >> (level + 1) == me >> (level + 1)) & (level < levels)
    solved_ref[:, first:] = jnp.where(near, code, 0).astype(F32).astype(BF16)
    copies.append(leave(2, 2 * leaf_n, solved_ref.shape[1] - 2 * leaf_n))
    for copy in copies:
        copy.wait()


def result_kernel(shots, capacity, scales, kinds_ref, back_ref, factors_ref, out_ref):
    count, width2 = out_ref.shape
    leaf_n = width2 // 2
    sep_lib, sep_n = factors_ref.shape[0], factors_ref.shape[2]
    slots, block, levels = back_ref.shape[0], capacity * shots, len(scales)
    row = lax.broadcasted_iota(jnp.int32, (block, slots), 0)
    col = lax.broadcasted_iota(jnp.int32, (block, slots), 1)
    same = (col % block == row).astype(F32).astype(BF16)
    sums = dot(same, back_ref[:, width2:])
    codes = sums[0:1, sums.shape[1] - LANES :]
    lane = lax.broadcasted_iota(jnp.int32, codes.shape, 1)
    codes = [jnp.sum(jnp.where(lane == level, codes, 0.0)).astype(jnp.int32) % sep_lib for level in range(levels)]

    def path_sum(part, level):
        entry = (part * levels + level) * shots
        rows, cols = entry % block, entry // block * sep_n
        return sums[rows : rows + shots, cols : cols + sep_n]

    above = jnp.zeros((2 * shots, sep_n), F32)
    for level in reversed(range(levels)):
        path = jnp.concatenate([path_sum(0, level), path_sum(1, level)], axis=0)
        operand = (path * scales[level] - above).astype(BF16)
        factor = factors_ref[codes[level]]
        by_re, by_im = dot(operand, factor[0]), dot(operand, factor[1])
        above = jnp.concatenate([by_re[:shots] - by_im[shots:], by_im[:shots] + by_re[shots:]], axis=0)
    _, col = slot_of(kinds_ref, shots, capacity)
    place = lax.broadcasted_iota(jnp.int32, (count, slots), 1)
    pick = (place == col).astype(F32).astype(BF16)
    shot = lax.broadcasted_iota(jnp.int32, (count, sep_n), 0) % shots
    for part in range(2):
        start = part * leaf_n
        solved = dot(pick, back_ref[:, start : start + leaf_n])
        lifted = jnp.zeros((count, sep_n), F32)
        for at in range(shots):
            here = part * shots + at
            lifted = jnp.where(shot == at, above[here : here + 1], lifted)
        out_ref[:, start : start + sep_n] = (solved[:, :sep_n] - lifted).astype(BF16)
        out_ref[:, start + sep_n : start + leaf_n] = solved[:, sep_n:].astype(BF16)


def face_kernel(front, source_ref, tau_ref, out_ref):
    leaf_n = source_ref.shape[2] // 2
    both = 2 * front
    face_re = source_ref[:, :, leaf_n - both : leaf_n].astype(F32)
    face_im = source_ref[:, :, 2 * leaf_n - both :].astype(F32)
    tau = tau_ref[...]
    first = lax.broadcasted_iota(jnp.int32, tau.shape, 2) < front
    turned = pltpu.roll(tau, front, 2)
    by_same, by_other = jnp.where(first, tau, turned), jnp.where(first, -turned, tau)
    first = lax.broadcasted_iota(jnp.int32, face_re.shape, 2) < front
    face = jnp.where(first, pltpu.roll(face_re, front, 2), face_im)
    other = jnp.where(first, pltpu.roll(face_im, front, 2), face_re)
    out_ref[...] = by_same * face + by_other * other


def call(kernel, out_shape, args, smem=(), scratch=(), to_hbm=False, limit=32):
    return pl.pallas_call(
        kernel,
        out_shape=out_shape,
        in_specs=[
            pl.BlockSpec(memory_space=pltpu.SMEM if at in smem else VMEM) for at in range(len(args))
        ],
        out_specs=pl.BlockSpec(memory_space=pl.ANY if to_hbm else VMEM),
        scratch_shapes=list(scratch),
        compiler_params=pltpu.CompilerParams(vmem_limit_bytes=limit * 2**20),
    )(*args)


def on_device(sources, transmission, media, sep_code, leaf_factors, sep_factors):
    leaves, shots, width2 = sources.shape[1:]
    leaf_n = width2 // 2
    front = transmission.shape[2] // 2
    sep_n = sep_factors.shape[2]
    nleaf = lax.axis_size("leaf")
    levels = nleaf.bit_length() - 1
    capacity = max(2, leaves * 5 // (nleaf * 2))
    block = capacity * shots
    slots = nleaf * block
    source, tau = sources[0], transmission[0][:, None, :]
    leaving = call(
        functools.partial(face_kernel, front),
        jax.ShapeDtypeStruct((leaves, shots, 2 * front), F32),
        (source, tau),
    )
    arriving = from_behind(leaving, "panel")
    tau_re, tau_im = tau[..., :front], tau[..., front:]
    for _ in range(lax.axis_size("panel") - 2):
        real = arriving[..., :front] + source[..., leaf_n - front : leaf_n].astype(F32)
        imag = arriving[..., front:] + source[..., 2 * leaf_n - front :].astype(F32)
        leaving = jnp.concatenate([tau_re * real - tau_im * imag, tau_re * imag + tau_im * real], axis=-1)
        arriving = from_behind(leaving, "panel")
    kinds = jnp.repeat(media[0, :, 0], shots)[None, :]
    rows = leaves * shots
    send = call(
        functools.partial(dispatch_kernel, shots, capacity, front),
        jax.ShapeDtypeStruct((slots, width2), BF16),
        (kinds, source.reshape(rows, width2), arriving.reshape(rows, 2 * front)),
        scratch=[VMEM((rows, width2), BF16), VMEM((slots, width2), BF16), pltpu.SemaphoreType.DMA((2,))],
        to_hbm=True,
    )
    arrived = lax.all_to_all(send.reshape(nleaf, block, width2), "leaf", split_axis=0, concat_axis=0, tiled=True)
    wide = width2 + -(-2 * levels // capacity) * sep_n + LANES
    place = jnp.stack([lax.axis_index("leaf"), sep_code[0, 0]])
    solved = call(
        functools.partial(leaf_kernel, capacity, shots, levels, sep_n),
        jax.ShapeDtypeStruct((slots, wide), BF16),
        (place, arrived.reshape(slots, width2), leaf_factors[0]),
        smem=(0,),
        scratch=[VMEM((slots, wide), BF16), pltpu.SemaphoreType.DMA((3,))],
        to_hbm=True,
    )
    back = lax.all_to_all(solved.reshape(nleaf, block, wide), "leaf", split_axis=0, concat_axis=0, tiled=True)
    scales = [1.0 / math.sqrt(leaves * 2 ** (level + 1)) for level in range(levels)]
    result = call(
        functools.partial(result_kernel, shots, capacity, scales),
        jax.ShapeDtypeStruct((rows, width2), BF16),
        (kinds, back.reshape(slots, wide), sep_factors),
    )
    return result.reshape(1, leaves, shots, width2)


def solution(mesh):
    return jax.shard_map(
        on_device,
        mesh=mesh,
        in_specs=(
            P("panel", "leaf", None, None),
            P("panel", "leaf", None),
            P("panel", "leaf", None),
            P("panel", "leaf"),
            P("leaf", None, None, None),
            P(),
        ),
        out_specs=P("panel", "leaf", None, None),
        check_vma=False,
    )
```

time: 79.3 us -> 70.9 us (0.89)
  blocking collectives: 0 us -> 30.1 us
  waiting for transfers between devices: 41.3 us -> 18 us
  starting transfers between devices: 22.1 us -> 10.8 us
  local copies, waits for them, and re-layouts: 7.9 us -> 4.66 us
  other arithmetic: 1.71 us -> 0.08 us
  Pallas kernels: 4.92 us -> 5.75 us
    all_to_all x0 -> x1, blocking collectives: none -> 30.1 us  [on_device(): lax.all_to_all(solved.reshape(nleaf, block, wide), 'leaf', split_axis=0,...]
    ppermute x4 -> x0, waiting for transfers between devices: 23.2 us -> none  [from_partner(): return lax.ppermute(value, axis, pairs)]
    ppermute x4 -> x0, starting transfers between devices: 7.53 us -> none  [from_partner(): return lax.ppermute(value, axis, pairs)]
    all_to_all x2 -> x1, starting transfers between devices: 9.69 us -> 5.95 us  [on_device(): lax.all_to_all(send.reshape(nleaf, block, width2), 'leaf', split_axis=0,...]
    unnamed x13 -> x8, local copies, waits for them, and re-layouts: 2.97 us -> 1.87 us
    concatenate x1 -> x0, local copies, waits for them, and re-layouts: 1.04 us -> none  [node_sums(): share = jnp.concatenate([own_sums, codes], axis=-1)]
    slice x1 -> x0, local copies, waits for them, and re-layouts: 1.02 us -> none  [on_device(): tau_re, tau_im = (tau[..., :front], tau[..., front:])]
    sub x1 -> x0, other arithmetic: 0.89 us -> none  [on_device(): tau_re * real - tau_im * imag]
  transfers between devices with their start and end apart: 7 -> 2, of which waited for: 4 -> 1; matrix products, arithmetic and copies ran while one was open for 3% -> 3% of each run, Pallas kernels for 2% -> 0%
where the time goes in v2:
time: 70.9 us; the launch traced here: 70.1 us
  blocking collectives  30.1 us (42%)
  waiting for transfers between devices  18 us (25%)
  starting transfers between devices  10.8 us (15%)
  Pallas kernels  5.75 us (8%)
  local copies, waits for them, and re-layouts  4.66 us (7%)
  between operations  0.72 us (1%)
    all_to_all x1, blocking collectives, on_device(): lax.all_to_all(solved.reshape(nleaf, block, wide), 'leaf', split_axis=0,...  30.1 us
    all_to_all x1, waiting for transfers between devices, on_device(): lax.all_to_all(send.reshape(nleaf, block, width2), 'leaf', split_axis=0,...  18 us
    all_to_all x1, starting transfers between devices, on_device(): lax.all_to_all(send.reshape(nleaf, block, width2), 'leaf', split_axis=0,...  5.95 us
    pallas_call x4, Pallas kernels, call(): pl.pallas_call(kernel, out_shape=out_shape, in_specs=[pl.BlockSpec(memory...  5.75 us
    ppermute x1, starting transfers between devices, from_behind(): return lax.ppermute(value, axis, [(at, at + 1) for at in range(count - 1)])  4.85 us
    unnamed x8, local copies, waits for them, and re-layouts  1.87 us
  transfers between devices with their start and end apart: 2, of which 1 were waited for; matrix products, arithmetic and copies ran while one was open for 3% of the time, Pallas kernels for 0%

profile of v2, /device:TPU:0, one launch (start us, length us, event | category | flops | bytes accessed | tf_op | source)
XLA Modules:
  0.0 70.1 jit_solution(9907219894849232926)
XLA Ops:
  0.0 0.0 copy-start
  0.0 0.0 copy-start.1
  0.0 1.1 %copy-done.1 = bf16[1,52,2,1536]{3,2,1,0:T(2,128)(2,1)S(1)} copy-done((bf16[1,52,2,1536]{3,2,1,0:T(2,128)(2,1)S(1)}, bf16[1,52,2,1536]{3,2,1,0:T(2,128)(2,1)}, u32[]{:S(2)}) %copy-start.1) | copy-done | bytes 319512
  1.1 0.0 copy-start.3
  1.1 0.7 %copy-done.3 = f32[1,52,128]{2,0,1:T(1,128)S(1)} copy-done((f32[1,52,128]{2,0,1:T(1,128)S(1)}, f32[1,52,128]{2,0,1:T(1,128)}, u32[]{:S(2)}) %copy-start.3) | copy-done | bytes 26648
  1.9 0.2 shard_map.64
  2.1 4.8 %collective-permute-start = (f32[52,2,128]{2,1,0:T(2,128)S(1)}, f32[52,2,128]{2,1,0:T(2,128)S(1)}, u32[]{:S(2)}, u32[]{:S(2)}) collective-permute-start(f32[52,2,128]{2,1,0:T(2,128)S(1)} %shard_map.64), channel_id=1, source_target_pairs={{0,16},{1,17},{2,18},{3,19},{4,20},{5,21},{6,22},{7,23},{8,24},{9,... | collective-permute-start | bytes 159752 | tf_op jit(solution)/shard_map/ppermute | solution.py:19
  6.9 1.1 %reshape_squeeze.3.rows_ref = bf16[104,1536]{1,0:T(8,128)(2,1)S(1)} reshape(bf16[1,52,2,1536]{3,2,1,0:T(2,128)(2,1)} %param.6) | data formatting | bytes 638976 | tf_op jit(solution)/shard_map/reshape;squeeze | solution.py:208
  8.0 0.7 %broadcast_in_dim.3 = s32[52,2]{1,0:T(8,128)S(1)} broadcast(s32[52]{0:T(128)} %bitcast.19), dimensions={0} | broadcast | bytes 624 | tf_op jit(solution)/shard_map/broadcast_in_dim | solution.py:203
  8.8 0.1 broadcast_in_dim_reshape.3.kinds_ref
  8.9 0.0 collective-permute-done
  8.9 1.3 %shard_map.65 = bf16[256,1536]{1,0:T(8,128)(2,1)} custom-call(s32[1,104]{1,0:T(1,128)S(1)} %broadcast_in_dim_reshape.3.kinds_ref, bf16[104,1536]{1,0:T(8,128)(2,1)S(1)} %reshape_squeeze.3.rows_ref, f32[104,128]{1,0:T(8,128)S(1)} %bitcast.17), custom_call_target="tpu_custom_call" | custom-call | tf_op jit(solution)/shard_map/pallas_call | solution.py:168
  10.2 6.0 %all-to-all-start = ((bf16[16,16,1536]{2,1,0:T(8,128)(2,1)}), bf16[16,16,1536]{2,1,0:T(8,128)(2,1)S(1)}, u32[]{:S(2)}, u32[]{:S(2)}) async-start(bf16[16,16,1536]{2,1,0:T(8,128)(2,1)} %bitcast.6), calls=%async_computation | async-start | bytes 1572864 | tf_op jit(solution)/shard_map/all_to_all | solution.py:212
  16.8 0.1 pad_add_fusion.place_ref
  16.9 18.0 %all-to-all-done = bf16[16,16,1536]{2,1,0:T(8,128)(2,1)S(1)} async-done(((bf16[16,16,1536]{2,1,0:T(8,128)(2,1)}), bf16[16,16,1536]{2,1,0:T(8,128)(2,1)S(1)}, u32[]{:S(2)}, u32[]{:S(2)}) %all-to-all-start) | async-done | bytes 786464 | tf_op jit(solution)/shard_map/all_to_all | solution.py:212
  34.9 0.0 copy-done
  34.9 0.0 copy-start.2
  34.9 3.0 %shard_map.66 = bf16[256,2048]{1,0:T(8,128)(2,1)S(1)} custom-call(s32[2]{0:T(128)S(1)} %pad_add_fusion.place_ref, bf16[256,1536]{1,0:T(8,128)(2,1)S(1)} %bitcast.14, bf16[2,768,768]{2,1,0:T(8,128)(2,1)S(1)} %bitcast.15), custom_call_target="tpu_custom_call" | custom-call | tf_op jit(solution)/shard_map/pallas_call | solution.py:168
  38.0 30.1 %all_to_all.10 = bf16[16,16,2048]{2,1,0:T(8,128)(2,1)S(1)} all-to-all(bf16[16,16,2048]{2,1,0:T(8,128)(2,1)S(1)} %bitcast.12), channel_id=1, replica_groups=mesh['panel'=2,'leaf'=16] {'leaf'}, dimensions={0} | all-to-all | bytes 2097152 | tf_op jit(solution)/shard_map/all_to_all | solution.py:223
  68.1 0.0 copy-done.2
  68.1 1.2 %shard_map.67 = bf16[104,1536]{1,0:T(8,128)(2,1)S(1)} custom-call(s32[1,104]{1,0:T(1,128)S(1)} %broadcast_in_dim_reshape.3.kinds_ref, bf16[256,2048]{1,0:T(8,128)(2,1)S(1)} %bitcast.13, bf16[2,2,384,384]{3,2,1,0:T(8,128)(2,1)S(1)} %copy-done.2), custom_call_target="tpu_custom_call" | custom-call | tf_op jit(solution)/shard_map/pallas_call | solution.py:168
  69.3 0.8 %reshape.23 = bf16[1,52,2,1536]{3,2,1,0:T(2,128)(2,1)} reshape(bf16[104,1536]{1,0:T(8,128)(2,1)S(1)} %shard_map.67) | data formatting | bytes 638976 | tf_op jit(solution)/shard_map/reshape | solution.py:230
Async XLA Ops:
  0.0 34.9 %copy-start = (bf16[1,2,768,768]{3,2,1,0:T(8,128)(2,1)S(1)}, bf16[1,2,768,768]{3,2,1,0:T(8,128)(2,1)}, u32[]{:S(2)}) copy-start(bf16[1,2,768,768]{3,2,1,0:T(8,128)(2,1)} %param.10) | copy-start | bytes 7077892
  0.0 1.1 %copy-start.1 = (bf16[1,52,2,1536]{3,2,1,0:T(2,128)(2,1)S(1)}, bf16[1,52,2,1536]{3,2,1,0:T(2,128)(2,1)}, u32[]{:S(2)}) copy-start(bf16[1,52,2,1536]{3,2,1,0:T(2,128)(2,1)} %param.6) | copy-start | bytes 958468
  1.1 0.7 %copy-start.3 = (f32[1,52,128]{2,0,1:T(1,128)S(1)}, f32[1,52,128]{2,0,1:T(1,128)}, u32[]{:S(2)}) copy-start(f32[1,52,128]{2,0,1:T(1,128)} %param.7) | copy-start | bytes 79876
  2.1 6.8 %collective-permute-start = (f32[52,2,128]{2,1,0:T(2,128)S(1)}, f32[52,2,128]{2,1,0:T(2,128)S(1)}, u32[]{:S(2)}, u32[]{:S(2)}) collective-permute-start(f32[52,2,128]{2,1,0:T(2,128)S(1)} %shard_map.64), channel_id=1, source_target_pairs={{0,16},{1,17},{2,18},{3,19},{4,20},{5,21},{6,22},{7,23},{8,24},{9,... | collective-permute-start | bytes 159752 | tf_op jit(solution)/shard_map/ppermute | solution.py:19
  10.2 24.7 %all-to-all-start = ((bf16[16,16,1536]{2,1,0:T(8,128)(2,1)}), bf16[16,16,1536]{2,1,0:T(8,128)(2,1)S(1)}, u32[]{:S(2)}, u32[]{:S(2)}) async-start(bf16[16,16,1536]{2,1,0:T(8,128)(2,1)} %bitcast.6), calls=%async_computation | async-start | bytes 1572864 | tf_op jit(solution)/shard_map/all_to_all | solution.py:212
  34.9 33.2 %copy-start.2 = (bf16[2,2,384,384]{3,2,1,0:T(8,128)(2,1)S(1)}, bf16[2,2,384,384]{3,2,1,0:T(8,128)(2,1)}, u32[]{:S(2)}) copy-start(bf16[2,2,384,384]{3,2,1,0:T(8,128)(2,1)} %factors_ref.1) | copy-start | bytes 3538948

commit v3 on v1

v3 whole, which is shorter than its diff:
```python
import functools
import math

import jax
import jax.numpy as jnp
from jax import lax
from jax.experimental import pallas as pl
from jax.experimental.pallas import tpu as pltpu
from jax.sharding import PartitionSpec as P

F32 = jnp.float32
BF16 = jnp.bfloat16
VMEM = pltpu.VMEM
LANES = 128


def from_behind(value, axis):
    count = lax.axis_size(axis)
    return lax.ppermute(value, axis, [(at, at + 1) for at in range(count - 1)])


def exchange(value, distance):
    pairs = [(at, at ^ distance) for at in range(lax.axis_size("leaf"))]
    return lax.ppermute(value, "leaf", pairs)


def after(value, *others):
    return lax.optimization_barrier((value, *others))[0]


def dot(left, right):
    return jnp.dot(left, right, preferred_element_type=F32)


def one_hot(mask):
    return mask.astype(F32).astype(BF16)


def slot_of(place_ref, kinds_ref, shots, capacity):
    kinds = kinds_ref[...]
    count = kinds.shape[1]
    before = lax.broadcasted_iota(jnp.int32, (count, count), 0)
    later = lax.broadcasted_iota(jnp.int32, (count, count), 1)
    across = jnp.broadcast_to(kinds, (count, count))
    kinds_down = jnp.sum(jnp.where(before == later, across, 0), axis=1, keepdims=True)
    down = jnp.broadcast_to(kinds_down, (count, count))
    same = (across == down) & (before % shots == later % shots)
    rank_row = jnp.sum((same & (before < later)).astype(jnp.int32), axis=0, keepdims=True)
    rank_col = jnp.sum((same & (later < before)).astype(jnp.int32), axis=1, keepdims=True)
    shot_row = lax.broadcasted_iota(jnp.int32, (1, count), 1) % shots
    shot_col = lax.broadcasted_iota(jnp.int32, (count, 1), 0) % shots
    me = place_ref[0]
    row = ((kinds ^ me) * shots + shot_row) * capacity + rank_row
    col = ((kinds_down ^ me) * shots + shot_col) * capacity + rank_col
    return row, col


def face_kernel(front, source_ref, tau_ref, out_ref, re_ref, im_ref, through_ref, sems):
    leaf_n = source_ref.shape[2] // 2
    both = 2 * front
    copies = [
        pltpu.make_async_copy(source_ref.at[:, :, pl.ds(leaf_n - both, both)], re_ref, sems.at[0]),
        pltpu.make_async_copy(source_ref.at[:, :, pl.ds(2 * leaf_n - both, both)], im_ref, sems.at[1]),
        pltpu.make_async_copy(tau_ref, through_ref, sems.at[2]),
    ]
    for copy in copies:
        copy.start()
    for copy in copies:
        copy.wait()
    face_re, face_im = re_ref[...].astype(F32), im_ref[...].astype(F32)
    tau = through_ref[...]
    first = lax.broadcasted_iota(jnp.int32, tau.shape, 2) < front
    turned = pltpu.roll(tau, front, 2)
    by_same, by_other = jnp.where(first, tau, turned), jnp.where(first, -turned, tau)
    first = lax.broadcasted_iota(jnp.int32, face_re.shape, 2) < front
    face = jnp.where(first, pltpu.roll(face_re, front, 2), face_im)
    other = jnp.where(first, pltpu.roll(face_im, front, 2), face_re)
    out_ref[...] = by_same * face + by_other * other


def dispatch_kernel(shots, capacity, front, place_ref, kinds_ref, rows_ref, arriving_ref, *refs):
    out_refs, rhs_ref = refs[:-1], refs[-1]
    leaf_n = rows_ref.shape[1] // 2
    rhs_ref[...] = rows_ref[...]
    for part in range(2):
        face = pl.ds((part + 1) * leaf_n - 2 * front, 2 * front)
        incoming = arriving_ref[...]
        lane = lax.broadcasted_iota(jnp.int32, incoming.shape, 1)
        if part == 0:
            incoming = pltpu.roll(incoming, front, 1)
        incoming = jnp.where(lane >= front, incoming, 0.0)
        rhs_ref[:, face] = (rows_ref[:, face].astype(F32) + incoming).astype(BF16)
    row, _ = slot_of(place_ref, kinds_ref, shots, capacity)
    size = out_refs[0].shape[0]
    slots = size * len(out_refs)
    place = lax.broadcasted_iota(jnp.int32, (slots, row.shape[1]), 0)
    send = dot(one_hot(place == row), rhs_ref[...]).astype(BF16)
    for at, out_ref in enumerate(out_refs):
        out_ref[...] = send[at * size : (at + 1) * size]


def leaf_kernel(count, capacity, shots, sep_n, own_ref, sibling_ref, *refs):
    blocks, out_refs, sums_ref = refs[:count], refs[count : 2 * count], refs[2 * count]
    rows_ref, top_ref = refs[2 * count + 1 :]
    leaf_n = own_ref.shape[1]
    size = capacity * shots
    half = count * size
    for entry, factor_ref in enumerate((own_ref, sibling_ref)):
        for at, block in enumerate(blocks):
            for part in range(2):
                rows_ref[part * half + at * size : part * half + (at + 1) * size] = block[
                    entry * size : (entry + 1) * size, part * leaf_n : (part + 1) * leaf_n
                ]
        by_re, by_im = dot(rows_ref[...], factor_ref[0]), dot(rows_ref[...], factor_ref[1])
        solved = ((by_re[:half] - by_im[half:]).astype(BF16), (by_im[:half] + by_re[half:]).astype(BF16))
        for part in range(2):
            for at, out_ref in enumerate(out_refs):
                out_ref[entry * size : (entry + 1) * size, part * leaf_n : (part + 1) * leaf_n] = solved[part][
                    at * size : (at + 1) * size
                ]
            top_ref[entry * half : (entry + 1) * half, part * sep_n : (part + 1) * sep_n] = solved[part][:, :sep_n]
    group = lax.broadcasted_iota(jnp.int32, (sums_ref.shape[0], 2 * half), 0)
    place = lax.broadcasted_iota(jnp.int32, (sums_ref.shape[0], 2 * half), 1)
    member = one_hot(place % half // capacity == group)
    sums_ref[...] = dot(member, top_ref[...])


def tree_kernel(scales, codes_ref, sums_ref, factors_ref, out_ref):
    sep_n = factors_ref.shape[2]
    shots = out_ref.shape[0] // 2
    above = jnp.zeros(out_ref.shape, F32)
    for level in reversed(range(len(scales))):
        here = sums_ref[level * shots : (level + 1) * shots]
        path = jnp.concatenate([here[:, :sep_n], here[:, sep_n : 2 * sep_n]], axis=0)
        operand = (path * scales[level] - above).astype(BF16)
        factor = factors_ref[codes_ref[level]]
        by_re, by_im = dot(operand, factor[0]), dot(operand, factor[1])
        above = jnp.concatenate([by_re[:shots] - by_im[shots:], by_im[:shots] + by_re[shots:]], axis=0)
    out_ref[...] = above


def result_kernel(shots, capacity, place_ref, kinds_ref, above_ref, *refs):
    blocks, out_ref, back_ref = refs[:-2], refs[-2], refs[-1]
    size = blocks[0].shape[0]
    for at, block in enumerate(blocks):
        back_ref[at * size : (at + 1) * size] = block[...]
    count, width2 = out_ref.shape
    leaf_n = width2 // 2
    sep_n = above_ref.shape[1]
    _, col = slot_of(place_ref, kinds_ref, shots, capacity)
    place = lax.broadcasted_iota(jnp.int32, (count, back_ref.shape[0]), 1)
    pick = one_hot(place == col)
    shot = lax.broadcasted_iota(jnp.int32, (count, sep_n), 0) % shots
    for part in range(2):
        start = part * leaf_n
        solved = dot(pick, back_ref[:, start : start + leaf_n])
        lifted = jnp.zeros((count, sep_n), F32)
        for at in range(shots):
            here = part * shots + at
            lifted = jnp.where(shot == at, above_ref[here : here + 1], lifted)
        out_ref[:, start : start + sep_n] = (solved[:, :sep_n] - lifted).astype(BF16)
        out_ref[:, start + sep_n : start + leaf_n] = solved[:, sep_n:].astype(BF16)


def call(kernel, out_shape, args, smem=(), hbm=(), scratch=(), limit=32):
    spaces = [pltpu.SMEM if at in smem else pl.ANY if at in hbm else VMEM for at in range(len(args))]
    return pl.pallas_call(
        kernel,
        out_shape=out_shape,
        in_specs=[pl.BlockSpec(memory_space=space) for space in spaces],
        out_specs=jax.tree.map(lambda _: pl.BlockSpec(memory_space=VMEM), out_shape),
        scratch_shapes=list(scratch),
        compiler_params=pltpu.CompilerParams(vmem_limit_bytes=limit * 2**20),
    )(*args)


def on_device(sources, transmission, media, sep_code, leaf_factors, sep_factors):
    leaves, shots, width2 = sources.shape[1:]
    leaf_n = width2 // 2
    front = transmission.shape[2] // 2
    sep_lib, sep_n = sep_factors.shape[0], sep_factors.shape[2]
    nleaf = lax.axis_size("leaf")
    levels = nleaf.bit_length() - 1
    capacity = max(2, leaves * 5 // (nleaf * 2))
    pairs = nleaf // 2
    block = jax.ShapeDtypeStruct((2 * capacity * shots, width2), BF16)
    source, tau = sources[0], transmission[0][:, None, :]
    place = lax.axis_index("leaf").astype(jnp.int32).reshape(1)
    own = leaf_factors[0]
    sibling = exchange(own, 1)

    face = jax.ShapeDtypeStruct((leaves, shots, 2 * front), BF16)
    leaving = call(
        functools.partial(face_kernel, front),
        jax.ShapeDtypeStruct((leaves, shots, 2 * front), F32),
        (source, tau),
        hbm=(0, 1),
        scratch=[VMEM(face.shape, BF16)] * 2 + [VMEM(tau.shape, F32), pltpu.SemaphoreType.DMA((3,))],
    )
    arriving = from_behind(leaving, "panel")
    tau_re, tau_im = tau[..., :front], tau[..., front:]
    for _ in range(lax.axis_size("panel") - 2):
        real = arriving[..., :front] + source[..., leaf_n - front : leaf_n].astype(F32)
        imag = arriving[..., front:] + source[..., 2 * leaf_n - front :].astype(F32)
        leaving = jnp.concatenate([tau_re * real - tau_im * imag, tau_re * imag + tau_im * real], axis=-1)
        arriving = from_behind(leaving, "panel")
    arriving = after(arriving, sibling)

    kinds = jnp.repeat(media[0, :, 0], shots)[None, :]
    rows = leaves * shots
    sent = call(
        functools.partial(dispatch_kernel, shots, capacity, front),
        [block] * pairs,
        (place, kinds, source.reshape(rows, width2), arriving.reshape(rows, 2 * front)),
        smem=(0,),
        scratch=[VMEM((rows, width2), BF16)],
    )

    far = list(range(pairs // 2, pairs))
    early, late = far[: len(far) // 2], far[len(far) // 2 :]
    under_way = []

    def cross(value, at):
        if len(under_way) >= 2:
            value = after(value, under_way[-2])
        under_way.append(exchange(value, 2 * at))
        return under_way[-1]

    def solve(group, arrived):
        count = len(group)
        half = count * capacity * shots
        *solved, sums = call(
            functools.partial(leaf_kernel, count, capacity, shots, sep_n),
            [block] * count + [jax.ShapeDtypeStruct((count * shots, 2 * sep_n), F32)],
            (own, sibling, *(arrived[at] for at in group)),
            scratch=[VMEM((2 * half, leaf_n), BF16), VMEM((2 * half, 2 * sep_n), BF16)],
        )
        return dict(zip(group, solved)), sums.reshape(count, shots, 2 * sep_n)

    arrived = {0: sent[0]}
    for at in far:
        arrived[at] = cross(sent[at], at)
    near = list(range(1, pairs // 2))
    for at in near:
        arrived[at] = exchange(sent[at], 2 * at)
    solved, sums = solve([0] + near + early, arrived)
    solved_late, sums_late = solve(late, arrived)
    solved.update(solved_late)

    back = {0: solved[0]}
    for at in near:
        back[at] = exchange(solved[at], 2 * at)
    for at in far:
        back[at] = cross(solved[at], at)

    sums = jnp.concatenate([sums, sums_late], axis=0)
    code = jnp.where(jnp.arange(pairs) == 0, sep_code[0, 0], 0).astype(F32)
    share = jnp.concatenate([sums, jnp.broadcast_to(code[:, None, None], (pairs, shots, LANES))], axis=-1)
    nodes = [share]
    for _ in range(levels - 1):
        share = share.reshape((share.shape[0] // 2, 2) + share.shape[1:]).sum(axis=1)
        nodes.append(share)
    for bit in reversed(range(levels)):
        if bit:
            cut = [part.shape[0] // 2 for part in nodes]
            keep = [part[: max(1, at)] for part, at in zip(nodes, cut)]
            send = [part[at:] for part, at in zip(nodes, cut)]
        else:
            keep, send = nodes, nodes
        part = exchange(jnp.concatenate(send, axis=0), 1 << bit)
        nodes, start = [], 0
        for mine in keep:
            nodes.append(mine + part[start : start + mine.shape[0]])
            start += mine.shape[0]
    path = jnp.concatenate(nodes, axis=0)
    codes = path[:, 0, 2 * sep_n].astype(jnp.int32) % sep_lib
    scales = [1.0 / math.sqrt(leaves * 2 ** (level + 1)) for level in range(levels)]
    above = call(
        functools.partial(tree_kernel, scales),
        jax.ShapeDtypeStruct((2 * shots, sep_n), F32),
        (codes, path.reshape(levels * shots, -1), sep_factors),
        smem=(0,),
    )
    result = call(
        functools.partial(result_kernel, shots, capacity),
        jax.ShapeDtypeStruct((rows, width2), BF16),
        (place, kinds, above, *(back[at] for at in range(pairs))),
        smem=(0,),
        scratch=[VMEM((pairs * block.shape[0], width2), BF16)],
    )
    return result.reshape(1, leaves, shots, width2)


def solution(mesh):
    return jax.shard_map(
        on_device,
        mesh=mesh,
        in_specs=(
            P("panel", "leaf", None, None),
            P("panel", "leaf", None),
            P("panel", "leaf", None),
            P("panel", "leaf"),
            P("leaf", None, None, None),
            P(),
        ),
        out_specs=P("panel", "leaf", None, None),
        check_vma=False,
    )
```

time: 79.3 us -> 80.5 us (1.015)
  waiting for transfers between devices: 41.3 us -> 14.9 us
  starting transfers between devices: 22.1 us -> 37.1 us
  local copies, waits for them, and re-layouts: 7.9 us -> 20.5 us
    ppermute x4 -> x19, starting transfers between devices: 7.53 us -> 32.7 us  [exchange(): return lax.ppermute(value, 'leaf', pairs)]
    all_to_all x2 -> x0, waiting for transfers between devices: 18 us -> none  [the longest x1 18 us: on_device(): lax.all_to_all(send.reshape(split), 'leaf', split_axis=0, concat_axis=0,...]
    unnamed x13 -> x42, local copies, waits for them, and re-layouts: 2.97 us -> 16.3 us
    all_to_all x2 -> x0, starting transfers between devices: 9.69 us -> none  [the longest x1 5.94 us: on_device(): lax.all_to_all(send.reshape(split), 'leaf', split_axis=0, concat_axis=0,...]
    ppermute x4 -> x19, waiting for transfers between devices: 23.2 us -> 14.9 us  [exchange(): return lax.ppermute(value, 'leaf', pairs)]
    concatenate x1 -> x0, local copies, waits for them, and re-layouts: 1.04 us -> none  [node_sums(): share = jnp.concatenate([own_sums, codes], axis=-1)]
    slice x1 -> x6, local copies, waits for them, and re-layouts: 1.02 us -> 0.02 us  [on_device(): send = [part[at:] for part, at in zip(nodes, cut)]]
    sub x1 -> x0, other arithmetic: 0.89 us -> none  [on_device(): tau_re * real - tau_im * imag]
  transfers between devices with their start and end apart: 7 -> 20, of which waited for: 4 -> 5; matrix products, arithmetic and copies ran while one was open for 3% -> 4% of each run, Pallas kernels for 2% -> 4%
where the time goes in v3:
time: 80.5 us; the launch traced here: 80 us
  starting transfers between devices  37.1 us (46%)
  local copies, waits for them, and re-layouts  20.5 us (25%)
  waiting for transfers between devices  14.9 us (19%)
  Pallas kernels  4.72 us (6%)
  other arithmetic  1.82 us (2%)
  between operations  0.96 us (1%)
    ppermute x19, starting transfers between devices, exchange(): return lax.ppermute(value, 'leaf', pairs)  32.7 us
    unnamed x42, local copies, waits for them, and re-layouts  16.3 us
    ppermute x19, waiting for transfers between devices, exchange(): return lax.ppermute(value, 'leaf', pairs)  14.9 us
    pallas_call x6, Pallas kernels, call(): pl.pallas_call(kernel, out_shape=out_shape, in_specs=[pl.BlockSpec(memory...  4.72 us
    ppermute x1, starting transfers between devices, from_behind(): return lax.ppermute(value, axis, [(at, at + 1) for at in range(count - 1)])  4.4 us
  transfers between devices with their start and end apart: 20, of which 5 were waited for; matrix products, arithmetic and copies ran while one was open for 4% of the time, Pallas kernels for 4%

profile of v3, /device:TPU:0, one launch (start us, length us, event | category | flops | bytes accessed | tf_op | source)
XLA Modules:
  0.0 80.0 jit_solution(15633868590011895549)
XLA Ops:
  2.5 4.4 %collective-permute-start.1 = (f32[52,2,128]{2,1,0:T(2,128)S(1)}, f32[52,2,128]{2,1,0:T(2,128)S(1)}, u32[]{:S(2)}, u32[]{:S(2)}) collective-permute-start(f32[52,2,128]{2,1,0:T(2,128)S(1)} %shard_map.64), channel_id=1, source_target_pairs={{0,16},{1,17},{2,18},{3,19},{4,20},{5,21},{6,22},{7,23},{8,24},{9,... | collective-permute-start | bytes 159752 | tf_op jit(solution)/shard_map/ppermute | solution.py:19
  6.9 1.1 %reshape_squeeze.3.rows_ref = bf16[104,1536]{1,0:T(8,128)(2,1)S(1)} reshape(bf16[1,52,2,1536]{3,2,1,0:T(2,128)(2,1)} %param.6) | data formatting | bytes 638976 | tf_op jit(solution)/shard_map/reshape;squeeze | solution.py:214
  8.9 1.4 %copy-done.2 = bf16[2,768,768]{2,1,0:T(8,128)(2,1)} copy-done((bf16[2,768,768]{2,1,0:T(8,128)(2,1)}, bf16[2,768,768]{2,1,0:T(8,128)(2,1)S(1)}, u32[]{:S(2)}) %copy-start.2) | copy-done | bytes 2359320
  10.7 3.6 %collective-permute-start.6 = (bf16[32,1536]{1,0:T(8,128)(2,1)S(1)}, bf16[32,1536]{1,0:T(8,128)(2,1)S(1)}, u32[]{:S(2)}, u32[]{:S(2)}) collective-permute-start(bf16[32,1536]{1,0:T(8,128)(2,1)S(1)} %get-tuple-element.36), channel_id=1, source_target_pairs={{0,10},{1,11},{2,8},{3,9},{4,14},{5,15},{6,12},{7,13},{8,2},{9,3},... | collective-permute-start | bytes 294920 | tf_op jit(solution)/shard_map/ppermute | solution.py:24
  15.9 1.6 %collective-permute-start.3 = (bf16[32,1536]{1,0:T(8,128)(2,1)S(1)}, bf16[32,1536]{1,0:T(8,128)(2,1)S(1)}, u32[]{:S(2)}, u32[]{:S(2)}) collective-permute-start(bf16[32,1536]{1,0:T(8,128)(2,1)S(1)} %get-tuple-element.33), channel_id=1, source_target_pairs={{0,4},{1,5},{2,6},{3,7},{4,0},{5,1},{6,2},{7,3},{8,12},{9,13},{10,... | collective-permute-start | bytes 294920 | tf_op jit(solution)/shard_map/ppermute | solution.py:24
  17.5 1.4 %collective-permute-start.4 = (bf16[32,1536]{1,0:T(8,128)(2,1)S(1)}, bf16[32,1536]{1,0:T(8,128)(2,1)S(1)}, u32[]{:S(2)}, u32[]{:S(2)}) collective-permute-start(bf16[32,1536]{1,0:T(8,128)(2,1)S(1)} %get-tuple-element.34), channel_id=1, source_target_pairs={{0,6},{1,7},{2,4},{3,5},{4,2},{5,3},{6,0},{7,1},{8,14},{9,15},{10,... | collective-permute-start | bytes 294920 | tf_op jit(solution)/shard_map/ppermute | solution.py:24
  18.9 3.7 %collective-permute-done.6.refs_5_ = bf16[32,1536]{1,0:T(8,128)(2,1)S(1)} collective-permute-done((bf16[32,1536]{1,0:T(8,128)(2,1)S(1)}, bf16[32,1536]{1,0:T(8,128)(2,1)S(1)}, u32[]{:S(2)}, u32[]{:S(2)}) %collective-permute-start.6) | collective-permute-done | bytes 98336 | tf_op jit(solution)/shard_map/ppermute | solution.py:24
  22.5 3.8 %collective-permute-start.8 = (bf16[32,1536]{1,0:T(8,128)(2,1)S(1)}, bf16[32,1536]{1,0:T(8,128)(2,1)S(1)}, u32[]{:S(2)}, u32[]{:S(2)}) collective-permute-start(bf16[32,1536]{1,0:T(8,128)(2,1)S(1)} %get-tuple-element.41), channel_id=1, source_target_pairs={{0,14},{1,15},{2,12},{3,13},{4,10},{5,11},{6,8},{7,9},{8,6},{9,7},... | collective-permute-start | bytes 294920 | tf_op jit(solution)/shard_map/ppermute | solution.py:24
  26.3 1.1 %collective-permute-start.7 = (bf16[32,1536]{1,0:T(8,128)(2,1)S(1)}, bf16[32,1536]{1,0:T(8,128)(2,1)S(1)}, u32[]{:S(2)}, u32[]{:S(2)}) collective-permute-start(bf16[32,1536]{1,0:T(8,128)(2,1)S(1)} %get-tuple-element.39), channel_id=1, source_target_pairs={{0,12},{1,13},{2,14},{3,15},{4,8},{5,9},{6,10},{7,11},{8,4},{9,5},... | collective-permute-start | bytes 294920 | tf_op jit(solution)/shard_map/ppermute | solution.py:24
  28.1 1.7 %copy-done = bf16[1,2,768,768]{3,2,1,0:T(8,128)(2,1)S(1)} copy-done((bf16[1,2,768,768]{3,2,1,0:T(8,128)(2,1)S(1)}, bf16[1,2,768,768]{3,2,1,0:T(8,128)(2,1)}, u32[]{:S(2)}) %copy-start) | copy-done | bytes 2359320
  29.8 1.7 %copy-done.3 = bf16[2,768,768]{2,1,0:T(8,128)(2,1)S(1)} copy-done((bf16[2,768,768]{2,1,0:T(8,128)(2,1)S(1)}, bf16[2,768,768]{2,1,0:T(8,128)(2,1)}, u32[]{:S(2)}) %copy-start.3) | copy-done | bytes 2359320
  31.4 1.2 %shard_map.66 = (bf16[32,1536]{1,0:T(8,128)(2,1)S(1)}, bf16[32,1536]{1,0:T(8,128)(2,1)S(1)}, bf16[32,1536]{1,0:T(8,128)(2,1)S(1)}, bf16[32,1536]{1,0:T(8,128)(2,...) custom-call(bf16[2,768,768]{2,1,0:T(8,128)(2,1)S(1)} %bitcast.15, ...), custom_call_target="tpu_custom_call" | custom-call | tf_op jit(solution)/shard_map/pallas_call | solution.py:167
  38.4 1.7 %copy-done.4 = bf16[2,768,768]{2,1,0:T(8,128)(2,1)S(1)} copy-done((bf16[2,768,768]{2,1,0:T(8,128)(2,1)S(1)}, bf16[2,768,768]{2,1,0:T(8,128)(2,1)}, u32[]{:S(2)}) %copy-start.4) | copy-done | bytes 2359320
  41.8 1.0 %shard_map.67 = (bf16[32,1536]{1,0:T(8,128)(2,1)S(1)}, bf16[32,1536]{1,0:T(8,128)(2,1)S(1)}, f32[4,768]{1,0:T(4,128)S(1)}) custom-call(bf16[2,768,768]{2,1,0:T(8,128)(2,1)S(1)} %bitcast.16, bf16[2,768,768]{2,1,0:T(8,128)(2,1)S(1)} %copy-done.4, bf16[32,1536]{1,0:T(8,128)(2,1)S(1)} %copy-done.12, bf16[32,1536]{1,0:T(8,128)(2,1)S(1)} %copy-done.10), custom_call_target="tpu_custom_call" | custom-call | tf_op jit(solution)/shard_map/pallas_call | solution.py:167
  46.0 5.1 %collective-permute-done.9 = f32[8,2,896]{2,1,0:T(2,128)S(1)} collective-permute-done((f32[8,2,896]{2,1,0:T(2,128)S(1)}, f32[8,2,896]{2,1,0:T(2,128)S(1)}, u32[]{:S(2)}, u32[]{:S(2)}) %collective-permute-start.9) | collective-permute-done | bytes 57376 | tf_op jit(solution)/shard_map/ppermute | solution.py:24
  51.2 4.6 %collective-permute-start.10 = (f32[5,2,896]{2,1,0:T(2,128)S(1)}, f32[5,2,896]{2,1,0:T(2,128)S(1)}, u32[]{:S(2)}, u32[]{:S(2)}) collective-permute-start(f32[5,2,896]{2,1,0:T(2,128)S(1)} %pad_maximum_fusion.2), channel_id=1, source_target_pairs={{0,4},{1,5},{2,6},{3,7},{4,0},{5,1},{6,2},{7,3},{8,12},{9,13},{10,... | collective-permute-start | bytes 107528 | tf_op jit(solution)/shard_map/ppermute | solution.py:24
  55.8 1.9 %collective-permute-done.10 = f32[5,2,896]{2,1,0:T(2,128)S(1)} collective-permute-done((f32[5,2,896]{2,1,0:T(2,128)S(1)}, f32[5,2,896]{2,1,0:T(2,128)S(1)}, u32[]{:S(2)}, u32[]{:S(2)}) %collective-permute-start.10) | collective-permute-done | bytes 35872 | tf_op jit(solution)/shard_map/ppermute | solution.py:24
  57.8 4.4 %collective-permute-start.17 = (bf16[32,1536]{1,0:T(8,128)(2,1)}, bf16[32,1536]{1,0:T(8,128)(2,1)S(1)}, u32[]{:S(2)}, u32[]{:S(2)}) collective-permute-start(bf16[32,1536]{1,0:T(8,128)(2,1)} %copy-done.20), channel_id=1, source_target_pairs={{0,10},{1,11},{2,8},{3,9},{4,14},{5,15},{6,12},{7,13},{8,2},{9,3},... | collective-permute-start | bytes 294920 | tf_op jit(solution)/shard_map/ppermute | solution.py:24
  63.0 2.0 %collective-permute-start.14 = (bf16[32,1536]{1,0:T(8,128)(2,1)}, bf16[32,1536]{1,0:T(8,128)(2,1)S(1)}, u32[]{:S(2)}, u32[]{:S(2)}) collective-permute-start(bf16[32,1536]{1,0:T(8,128)(2,1)} %copy-done.15), channel_id=1, source_target_pairs={{0,4},{1,5},{2,6},{3,7},{4,0},{5,1},{6,2},{7,3},{8,12},{9,13},{10,... | collective-permute-start | bytes 294920 | tf_op jit(solution)/shard_map/ppermute | solution.py:24
  65.0 3.1 %collective-permute-start.15 = (bf16[32,1536]{1,0:T(8,128)(2,1)}, bf16[32,1536]{1,0:T(8,128)(2,1)S(1)}, u32[]{:S(2)}, u32[]{:S(2)}) collective-permute-start(bf16[32,1536]{1,0:T(8,128)(2,1)} %copy-done.14), channel_id=1, source_target_pairs={{0,6},{1,7},{2,4},{3,5},{4,2},{5,3},{6,0},{7,1},{8,14},{9,15},{10,... | collective-permute-start | bytes 294920 | tf_op jit(solution)/shard_map/ppermute | solution.py:24
  68.1 3.9 %collective-permute-start.19 = (bf16[32,1536]{1,0:T(8,128)(2,1)}, bf16[32,1536]{1,0:T(8,128)(2,1)S(1)}, u32[]{:S(2)}, u32[]{:S(2)}) collective-permute-start(bf16[32,1536]{1,0:T(8,128)(2,1)} %copy-done.18), channel_id=1, source_target_pairs={{0,14},{1,15},{2,12},{3,13},{4,10},{5,11},{6,8},{7,9},{8,6},{9,7},... | collective-permute-start | bytes 294920 | tf_op jit(solution)/shard_map/ppermute | solution.py:24
  73.2 1.3 %shard_map.68.above_ref = f32[4,384]{1,0:T(4,128)S(1)} custom-call(s32[4]{0:T(128)S(1)} %and_select_fusion.codes_ref, f32[8,896]{1,0:T(8,128)S(1)} %reshape.39.sums_ref, bf16[2,2,384,384]{3,2,1,0:T(8,128)(2,1)S(1)} %copy-done.6), custom_call_target="tpu_custom_call" | custom-call | tf_op jit(solution)/shard_map/pallas_call | solution.py:167
  74.5 2.1 %collective-permute-done.19.refs_7_ = bf16[32,1536]{1,0:T(8,128)(2,1)S(1)} collective-permute-done((bf16[32,1536]{1,0:T(8,128)(2,1)}, bf16[32,1536]{1,0:T(8,128)(2,1)S(1)}, u32[]{:S(2)}, u32[]{:S(2)}) %collective-permute-start.19) | collective-permute-done | bytes 98336 | tf_op jit(solution)/shard_map/ppermute | solution.py:24
  76.6 2.1 %collective-permute-done.18.refs_6_ = bf16[32,1536]{1,0:T(8,128)(2,1)S(1)} collective-permute-done((bf16[32,1536]{1,0:T(8,128)(2,1)}, bf16[32,1536]{1,0:T(8,128)(2,1)S(1)}, u32[]{:S(2)}, u32[]{:S(2)}) %collective-permute-start.18) | collective-permute-done | bytes 98336 | tf_op jit(solution)/shard_map/ppermute | solution.py:24
  (96 shorter events, 19.3 us)
Async XLA Ops:
  0.0 8.8 %collective-permute-start = (bf16[2,768,768]{2,1,0:T(8,128)(2,1)}, bf16[2,768,768]{2,1,0:T(8,128)(2,1)S(1)}, u32[]{:S(2)}, u32[]{:S(2)}) collective-permute-start(bf16[2,768,768]{2,1,0:T(8,128)(2,1)} %bitcast.14), channel_id=1, source_target_pairs={{0,1},{1,0},{2,3},{3,2},{4,5},{5,4},{6,7},{7,6},{8,9},{9,8},{10,11... | collective-permute-start | bytes 7077896 | tf_op jit(solution)/shard_map/ppermute | solution.py:24
  2.5 6.4 %collective-permute-start.1 = (f32[52,2,128]{2,1,0:T(2,128)S(1)}, f32[52,2,128]{2,1,0:T(2,128)S(1)}, u32[]{:S(2)}, u32[]{:S(2)}) collective-permute-start(f32[52,2,128]{2,1,0:T(2,128)S(1)} %shard_map.64), channel_id=1, source_target_pairs={{0,16},{1,17},{2,18},{3,19},{4,20},{5,21},{6,22},{7,23},{8,24},{9,... | collective-permute-start | bytes 159752 | tf_op jit(solution)/shard_map/ppermute | solution.py:19
  10.7 11.8 %collective-permute-start.6 = (bf16[32,1536]{1,0:T(8,128)(2,1)S(1)}, bf16[32,1536]{1,0:T(8,128)(2,1)S(1)}, u32[]{:S(2)}, u32[]{:S(2)}) collective-permute-start(bf16[32,1536]{1,0:T(8,128)(2,1)S(1)} %get-tuple-element.36), channel_id=1, source_target_pairs={{0,10},{1,11},{2,8},{3,9},{4,14},{5,15},{6,12},{7,13},{8,2},{9,3},... | collective-permute-start | bytes 294920 | tf_op jit(solution)/shard_map/ppermute | solution.py:24
  14.3 12.0 %collective-permute-start.5 = (bf16[32,1536]{1,0:T(8,128)(2,1)S(1)}, bf16[32,1536]{1,0:T(8,128)(2,1)S(1)}, u32[]{:S(2)}, u32[]{:S(2)}) collective-permute-start(bf16[32,1536]{1,0:T(8,128)(2,1)S(1)} %get-tuple-element.35), channel_id=1, source_target_pairs={{0,8},{1,9},{2,10},{3,11},{4,12},{5,13},{6,14},{7,15},{8,0},{9,1},... | collective-permute-start | bytes 294920 | tf_op jit(solution)/shard_map/ppermute | solution.py:24
  15.3 12.7 %collective-permute-start.2 = (bf16[32,1536]{1,0:T(8,128)(2,1)S(1)}, bf16[32,1536]{1,0:T(8,128)(2,1)S(1)}, u32[]{:S(2)}, u32[]{:S(2)}) collective-permute-start(bf16[32,1536]{1,0:T(8,128)(2,1)S(1)} %get-tuple-element.32), channel_id=1, source_target_pairs={{0,2},{1,3},{2,0},{3,1},{4,6},{5,7},{6,4},{7,5},{8,10},{9,11},{10,... | collective-permute-start | bytes 294920 | tf_op jit(solution)/shard_map/ppermute | solution.py:24
  15.9 12.2 %collective-permute-start.3 = (bf16[32,1536]{1,0:T(8,128)(2,1)S(1)}, bf16[32,1536]{1,0:T(8,128)(2,1)S(1)}, u32[]{:S(2)}, u32[]{:S(2)}) collective-permute-start(bf16[32,1536]{1,0:T(8,128)(2,1)S(1)} %get-tuple-element.33), channel_id=1, source_target_pairs={{0,4},{1,5},{2,6},{3,7},{4,0},{5,1},{6,2},{7,3},{8,12},{9,13},{10,... | collective-permute-start | bytes 294920 | tf_op jit(solution)/shard_map/ppermute | solution.py:24
  17.5 10.6 %collective-permute-start.4 = (bf16[32,1536]{1,0:T(8,128)(2,1)S(1)}, bf16[32,1536]{1,0:T(8,128)(2,1)S(1)}, u32[]{:S(2)}, u32[]{:S(2)}) collective-permute-start(bf16[32,1536]{1,0:T(8,128)(2,1)S(1)} %get-tuple-element.34), channel_id=1, source_target_pairs={{0,6},{1,7},{2,4},{3,5},{4,2},{5,3},{6,0},{7,1},{8,14},{9,15},{10,... | collective-permute-start | bytes 294920 | tf_op jit(solution)/shard_map/ppermute | solution.py:24
  22.5 14.6 %collective-permute-start.8 = (bf16[32,1536]{1,0:T(8,128)(2,1)S(1)}, bf16[32,1536]{1,0:T(8,128)(2,1)S(1)}, u32[]{:S(2)}, u32[]{:S(2)}) collective-permute-start(bf16[32,1536]{1,0:T(8,128)(2,1)S(1)} %get-tuple-element.41), channel_id=1, source_target_pairs={{0,14},{1,15},{2,12},{3,13},{4,10},{5,11},{6,8},{7,9},{8,6},{9,7},... | collective-permute-start | bytes 294920 | tf_op jit(solution)/shard_map/ppermute | solution.py:24
  26.3 11.4 %collective-permute-start.7 = (bf16[32,1536]{1,0:T(8,128)(2,1)S(1)}, bf16[32,1536]{1,0:T(8,128)(2,1)S(1)}, u32[]{:S(2)}, u32[]{:S(2)}) collective-permute-start(bf16[32,1536]{1,0:T(8,128)(2,1)S(1)} %get-tuple-element.39), channel_id=1, source_target_pairs={{0,12},{1,13},{2,14},{3,15},{4,8},{5,9},{6,10},{7,11},{8,4},{9,5},... | collective-permute-start | bytes 294920 | tf_op jit(solution)/shard_map/ppermute | solution.py:24
  28.1 1.7 %copy-start = (bf16[1,2,768,768]{3,2,1,0:T(8,128)(2,1)S(1)}, bf16[1,2,768,768]{3,2,1,0:T(8,128)(2,1)}, u32[]{:S(2)}) copy-start(bf16[1,2,768,768]{3,2,1,0:T(8,128)(2,1)} %param.10) | copy-start | bytes 7077892
  31.4 7.0 %copy-start.1 = (bf16[1,2,768,768]{3,2,1,0:T(8,128)(2,1)S(1)}, bf16[1,2,768,768]{3,2,1,0:T(8,128)(2,1)}, u32[]{:S(2)}) copy-start(bf16[1,2,768,768]{3,2,1,0:T(8,128)(2,1)} %param.10) | copy-start | bytes 7077892
  41.8 31.4 %copy-start.6 = (bf16[2,2,384,384]{3,2,1,0:T(8,128)(2,1)S(1)}, bf16[2,2,384,384]{3,2,1,0:T(8,128)(2,1)}, u32[]{:S(2)}) copy-start(bf16[2,2,384,384]{3,2,1,0:T(8,128)(2,1)} %factors_ref.1) | copy-start | bytes 3538948
  44.2 34.6 %copy-start.8 = (bf16[32,1536]{1,0:T(8,128)(2,1)S(1)}, bf16[32,1536]{1,0:T(8,128)(2,1)}, u32[]{:S(2)}) copy-start(bf16[32,1536]{1,0:T(8,128)(2,1)} %copy-done.7) | copy-start | bytes 294916
  45.9 5.1 %collective-permute-start.9 = (f32[8,2,896]{2,1,0:T(2,128)S(1)}, f32[8,2,896]{2,1,0:T(2,128)S(1)}, u32[]{:S(2)}, u32[]{:S(2)}) collective-permute-start(f32[8,2,896]{2,1,0:T(2,128)S(1)} %pad_maximum_fusion.1), channel_id=1, source_target_pairs={{0,8},{1,9},{2,10},{3,11},{4,12},{5,13},{6,14},{7,15},{8,0},{9,1},... | collective-permute-start | bytes 172040 | tf_op jit(solution)/shard_map/ppermute | solution.py:24
  51.2 6.5 %collective-permute-start.10 = (f32[5,2,896]{2,1,0:T(2,128)S(1)}, f32[5,2,896]{2,1,0:T(2,128)S(1)}, u32[]{:S(2)}, u32[]{:S(2)}) collective-permute-start(f32[5,2,896]{2,1,0:T(2,128)S(1)} %pad_maximum_fusion.2), channel_id=1, source_target_pairs={{0,4},{1,5},{2,6},{3,7},{4,0},{5,1},{6,2},{7,3},{8,12},{9,13},{10,... | collective-permute-start | bytes 107528 | tf_op jit(solution)/shard_map/ppermute | solution.py:24
  57.8 4.5 %collective-permute-start.11 = (f32[4,2,896]{2,1,0:T(2,128)S(1)}, f32[4,2,896]{2,1,0:T(2,128)S(1)}, u32[]{:S(2)}, u32[]{:S(2)}) collective-permute-start(f32[4,2,896]{2,1,0:T(2,128)S(1)} %pad_maximum_fusion.3), channel_id=1, source_target_pairs={{0,2},{1,3},{2,0},{3,1},{4,6},{5,7},{6,4},{7,5},{8,10},{9,11},{10,... | collective-permute-start | bytes 86024 | tf_op jit(solution)/shard_map/ppermute | solution.py:24
  57.8 7.2 %collective-permute-start.17 = (bf16[32,1536]{1,0:T(8,128)(2,1)}, bf16[32,1536]{1,0:T(8,128)(2,1)S(1)}, u32[]{:S(2)}, u32[]{:S(2)}) collective-permute-start(bf16[32,1536]{1,0:T(8,128)(2,1)} %copy-done.20), channel_id=1, source_target_pairs={{0,10},{1,11},{2,8},{3,9},{4,14},{5,15},{6,12},{7,13},{8,2},{9,3},... | collective-permute-start | bytes 294920 | tf_op jit(solution)/shard_map/ppermute | solution.py:24
  62.2 5.9 %collective-permute-start.16 = (bf16[32,1536]{1,0:T(8,128)(2,1)}, bf16[32,1536]{1,0:T(8,128)(2,1)S(1)}, u32[]{:S(2)}, u32[]{:S(2)}) collective-permute-start(bf16[32,1536]{1,0:T(8,128)(2,1)} %copy-done.19), channel_id=1, source_target_pairs={{0,8},{1,9},{2,10},{3,11},{4,12},{5,13},{6,14},{7,15},{8,0},{9,1},... | collective-permute-start | bytes 294920 | tf_op jit(solution)/shard_map/ppermute | solution.py:24
  62.3 9.7 %collective-permute-start.12 = (f32[4,2,896]{2,1,0:T(2,128)S(1)}, f32[4,2,896]{2,1,0:T(2,128)S(1)}, u32[]{:S(2)}, u32[]{:S(2)}) collective-permute-start(f32[4,2,896]{2,1,0:T(2,128)S(1)} %pad_maximum_fusion.4), channel_id=1, source_target_pairs={{0,1},{1,0},{2,3},{3,2},{4,5},{5,4},{6,7},{7,6},{8,9},{9,8},{10,11... | collective-permute-start | bytes 86024 | tf_op jit(solution)/shard_map/ppermute | solution.py:24
  62.3 12.2 %collective-permute-start.13 = (bf16[32,1536]{1,0:T(8,128)(2,1)}, bf16[32,1536]{1,0:T(8,128)(2,1)S(1)}, u32[]{:S(2)}, u32[]{:S(2)}) collective-permute-start(bf16[32,1536]{1,0:T(8,128)(2,1)} %copy-done.16), channel_id=1, source_target_pairs={{0,2},{1,3},{2,0},{3,1},{4,6},{5,7},{6,4},{7,5},{8,10},{9,11},{10,... | collective-permute-start | bytes 294920 | tf_op jit(solution)/shard_map/ppermute | solution.py:24
  63.0 11.6 %collective-permute-start.14 = (bf16[32,1536]{1,0:T(8,128)(2,1)}, bf16[32,1536]{1,0:T(8,128)(2,1)S(1)}, u32[]{:S(2)}, u32[]{:S(2)}) collective-permute-start(bf16[32,1536]{1,0:T(8,128)(2,1)} %copy-done.15), channel_id=1, source_target_pairs={{0,4},{1,5},{2,6},{3,7},{4,0},{5,1},{6,2},{7,3},{8,12},{9,13},{10,... | collective-permute-start | bytes 294920 | tf_op jit(solution)/shard_map/ppermute | solution.py:24
  65.0 9.5 %collective-permute-start.15 = (bf16[32,1536]{1,0:T(8,128)(2,1)}, bf16[32,1536]{1,0:T(8,128)(2,1)S(1)}, u32[]{:S(2)}, u32[]{:S(2)}) collective-permute-start(bf16[32,1536]{1,0:T(8,128)(2,1)} %copy-done.14), channel_id=1, source_target_pairs={{0,6},{1,7},{2,4},{3,5},{4,2},{5,3},{6,0},{7,1},{8,14},{9,15},{10,... | collective-permute-start | bytes 294920 | tf_op jit(solution)/shard_map/ppermute | solution.py:24
  68.1 8.5 %collective-permute-start.19 = (bf16[32,1536]{1,0:T(8,128)(2,1)}, bf16[32,1536]{1,0:T(8,128)(2,1)S(1)}, u32[]{:S(2)}, u32[]{:S(2)}) collective-permute-start(bf16[32,1536]{1,0:T(8,128)(2,1)} %copy-done.18), channel_id=1, source_target_pairs={{0,14},{1,15},{2,12},{3,13},{4,10},{5,11},{6,8},{7,9},{8,6},{9,7},... | collective-permute-start | bytes 294920 | tf_op jit(solution)/shard_map/ppermute | solution.py:24
  72.0 6.7 %collective-permute-start.18 = (bf16[32,1536]{1,0:T(8,128)(2,1)}, bf16[32,1536]{1,0:T(8,128)(2,1)S(1)}, u32[]{:S(2)}, u32[]{:S(2)}) collective-permute-start(bf16[32,1536]{1,0:T(8,128)(2,1)} %copy-done.17), channel_id=1, source_target_pairs={{0,12},{1,13},{2,14},{3,15},{4,8},{5,9},{6,10},{7,11},{8,4},{9,5},... | collective-permute-start | bytes 294920 | tf_op jit(solution)/shard_map/ppermute | solution.py:24
  (17 other events, 14.6 us)

commit v4 on v3

v4 whole, which is shorter than its diff:
```python
import functools
import math

import jax
import jax.numpy as jnp
from jax import lax
from jax.experimental import pallas as pl
from jax.experimental.pallas import tpu as pltpu
from jax.sharding import PartitionSpec as P

F32 = jnp.float32
BF16 = jnp.bfloat16
VMEM = pltpu.VMEM
LANES = 128


def from_behind(value, axis):
    count = lax.axis_size(axis)
    return lax.ppermute(value, axis, [(at, at + 1) for at in range(count - 1)])


def exchange(value, distance):
    pairs = [(at, at ^ distance) for at in range(lax.axis_size("leaf"))]
    return lax.ppermute(value, "leaf", pairs)


def dot(left, right):
    return jnp.dot(left, right, preferred_element_type=F32)


def one_hot(mask):
    return mask.astype(F32).astype(BF16)


def slot_of(place_ref, kinds_ref, shots, capacity):
    kinds = kinds_ref[...]
    count = kinds.shape[1]
    before = lax.broadcasted_iota(jnp.int32, (count, count), 0)
    later = lax.broadcasted_iota(jnp.int32, (count, count), 1)
    across = jnp.broadcast_to(kinds, (count, count))
    kinds_down = jnp.sum(jnp.where(before == later, across, 0), axis=1, keepdims=True)
    down = jnp.broadcast_to(kinds_down, (count, count))
    same = (across == down) & (before % shots == later % shots)
    rank_row = jnp.sum((same & (before < later)).astype(jnp.int32), axis=0, keepdims=True)
    rank_col = jnp.sum((same & (later < before)).astype(jnp.int32), axis=1, keepdims=True)
    shot_row = lax.broadcasted_iota(jnp.int32, (1, count), 1) % shots
    shot_col = lax.broadcasted_iota(jnp.int32, (count, 1), 0) % shots
    parity = place_ref[0] & 1
    row = ((kinds ^ parity) * shots + shot_row) * capacity + rank_row
    col = ((kinds_down ^ parity) * shots + shot_col) * capacity + rank_col
    return row, col


def face_kernel(front, source_ref, tau_ref, out_ref, re_ref, im_ref, through_ref, sems):
    leaf_n = source_ref.shape[2] // 2
    both = 2 * front
    copies = [
        pltpu.make_async_copy(source_ref.at[:, :, pl.ds(leaf_n - both, both)], re_ref, sems.at[0]),
        pltpu.make_async_copy(source_ref.at[:, :, pl.ds(2 * leaf_n - both, both)], im_ref, sems.at[1]),
        pltpu.make_async_copy(tau_ref, through_ref, sems.at[2]),
    ]
    for copy in copies:
        copy.start()
    for copy in copies:
        copy.wait()
    face_re, face_im = re_ref[...].astype(F32), im_ref[...].astype(F32)
    tau = through_ref[...]
    first = lax.broadcasted_iota(jnp.int32, tau.shape, 2) < front
    turned = pltpu.roll(tau, front, 2)
    by_same, by_other = jnp.where(first, tau, turned), jnp.where(first, -turned, tau)
    first = lax.broadcasted_iota(jnp.int32, face_re.shape, 2) < front
    face = jnp.where(first, pltpu.roll(face_re, front, 2), face_im)
    other = jnp.where(first, pltpu.roll(face_im, front, 2), face_re)
    out_ref[...] = by_same * face + by_other * other


def dispatch_kernel(shots, capacity, front, place_ref, kinds_ref, rows_ref, arriving_ref, out_ref, rhs_ref, send_ref, sems):
    leaf_n = rows_ref.shape[1] // 2
    rhs_ref[...] = rows_ref[...]
    for part in range(2):
        face = pl.ds((part + 1) * leaf_n - 2 * front, 2 * front)
        incoming = arriving_ref[...]
        lane = lax.broadcasted_iota(jnp.int32, incoming.shape, 1)
        if part == 0:
            incoming = pltpu.roll(incoming, front, 1)
        incoming = jnp.where(lane >= front, incoming, 0.0)
        rhs_ref[:, face] = (rows_ref[:, face].astype(F32) + incoming).astype(BF16)
    row, _ = slot_of(place_ref, kinds_ref, shots, capacity)
    place = lax.broadcasted_iota(jnp.int32, (send_ref.shape[0], row.shape[1]), 0)
    pick = one_hot(place == row)
    copies = []
    for part in range(2):
        columns = pl.ds(part * leaf_n, leaf_n)
        send_ref[:, columns] = dot(pick, rhs_ref[:, columns]).astype(BF16)
        copies.append(pltpu.make_async_copy(send_ref.at[:, columns], out_ref.at[:, columns], sems.at[part]))
        copies[part].start()
    for copy in copies:
        copy.wait()


def leaf_kernel(capacity, shots, sep_n, place_ref, arrived_ref, own_ref, sibling_ref, out_ref, keep_ref, send_ref, *refs):
    rows_ref, solved_ref, top_ref, sems = refs
    leaf_n = own_ref.shape[1]
    size = capacity * shots
    pairs = arrived_ref.shape[0] // (2 * size)
    half = pairs * size
    copies = []
    for entry, factor_ref in enumerate((own_ref, sibling_ref)):
        for at in range(pairs):
            first = (2 * at + entry) * size
            for part in range(2):
                rows_ref[part * half + at * size : part * half + (at + 1) * size] = arrived_ref[
                    first : first + size, part * leaf_n : (part + 1) * leaf_n
                ]
        by_re, by_im = dot(rows_ref[...], factor_ref[0]), dot(rows_ref[...], factor_ref[1])
        solved = ((by_re[:half] - by_im[half:]).astype(BF16), (by_im[:half] + by_re[half:]).astype(BF16))
        for part in range(2):
            for at in range(pairs):
                first = (2 * at + entry) * size
                solved_ref[first : first + size, part * leaf_n : (part + 1) * leaf_n] = solved[part][
                    at * size : (at + 1) * size
                ]
            top_ref[entry * half : (entry + 1) * half, part * sep_n : (part + 1) * sep_n] = solved[part][:, :sep_n]
    out = pltpu.make_async_copy(solved_ref, out_ref, sems.at[0])
    out.start()
    own_pair = place_ref[0] >> 1
    code = place_ref[1].astype(F32)
    bits = pairs.bit_length() - 1
    for other, ref in enumerate((keep_ref, send_ref)):
        count = ref.shape[0]
        row = lax.broadcasted_iota(jnp.int32, (count, 2 * half), 0)
        place = lax.broadcasted_iota(jnp.int32, (count, 2 * half), 1)
        distance = (place % half // size) ^ own_pair
        member = row < 0
        here = lax.broadcasted_iota(jnp.int32, (count, LANES), 0) < 0
        first = 0
        for level in range(bits + 1):
            nodes = max(1, 1 << bits - 1 - level) if level < bits else 1
            node = (row - first) // shots + (other * nodes if level < bits else 0)
            inside = (row >= first) & (row < first + nodes * shots)
            member |= inside & (distance >> level == node)
            if not (other and level < bits):
                lead = lax.broadcasted_iota(jnp.int32, (count, LANES), 0)
                here |= (lead >= first) & (lead < first + shots)
            first += nodes * shots
        member &= place % size // capacity == row % shots
        ref[:, : 2 * sep_n] = dot(one_hot(member), top_ref[...]).astype(ref.dtype)
        ref[:, 2 * sep_n :] = jnp.where(here, code, 0.0).astype(ref.dtype)
    out.wait()


def tree_kernel(scales, keep_ref, arrived_ref, factors_ref, out_ref):
    sep_lib, sep_n = factors_ref.shape[0], factors_ref.shape[2]
    shots = out_ref.shape[0] // 2
    sums = keep_ref[...] + arrived_ref[...].astype(F32)
    above = jnp.zeros(out_ref.shape, F32)
    for level in reversed(range(len(scales))):
        here = sums[level * shots : (level + 1) * shots]
        code = jnp.max(here[0:1, 2 * sep_n :]).astype(jnp.int32) % sep_lib
        path = jnp.concatenate([here[:, :sep_n], here[:, sep_n : 2 * sep_n]], axis=0)
        operand = (path * scales[level] - above).astype(BF16)
        factor = factors_ref[code]
        by_re, by_im = dot(operand, factor[0]), dot(operand, factor[1])
        above = jnp.concatenate([by_re[:shots] - by_im[shots:], by_im[:shots] + by_re[shots:]], axis=0)
    out_ref[...] = above


def result_kernel(shots, capacity, place_ref, kinds_ref, above_ref, back_ref, out_ref):
    count, width2 = out_ref.shape
    leaf_n = width2 // 2
    sep_n = above_ref.shape[1]
    _, col = slot_of(place_ref, kinds_ref, shots, capacity)
    place = lax.broadcasted_iota(jnp.int32, (count, back_ref.shape[0]), 1)
    pick = one_hot(place == col)
    shot = lax.broadcasted_iota(jnp.int32, (count, sep_n), 0) % shots
    for part in range(2):
        start = part * leaf_n
        solved = dot(pick, back_ref[:, start : start + leaf_n])
        lifted = jnp.zeros((count, sep_n), F32)
        for at in range(shots):
            here = part * shots + at
            lifted = jnp.where(shot == at, above_ref[here : here + 1], lifted)
        out_ref[:, start : start + sep_n] = (solved[:, :sep_n] - lifted).astype(BF16)
        out_ref[:, start + sep_n : start + leaf_n] = solved[:, sep_n:].astype(BF16)


def call(kernel, out_shape, args, smem=(), hbm=(), hbm_out=(), scratch=(), cost=None, limit=16):
    spaces = [pltpu.SMEM if at in smem else pltpu.HBM if at in hbm else VMEM for at in range(len(args))]
    shapes = out_shape if isinstance(out_shape, list) else [out_shape]
    out_specs = [pl.BlockSpec(memory_space=pltpu.HBM if at in hbm_out else VMEM) for at in range(len(shapes))]
    return pl.pallas_call(
        kernel,
        out_shape=out_shape,
        in_specs=[pl.BlockSpec(memory_space=space) for space in spaces],
        out_specs=out_specs if isinstance(out_shape, list) else out_specs[0],
        scratch_shapes=list(scratch),
        cost_estimate=cost and pl.CostEstimate(flops=cost[0], bytes_accessed=cost[1], transcendentals=0),
        compiler_params=pltpu.CompilerParams(vmem_limit_bytes=limit * 2**20),
    )(*args)


def to_pairs(value):
    groups = [list(range(parity, lax.axis_size("leaf"), 2)) for parity in range(2)]
    return lax.all_to_all(value, "leaf", 0, 0, tiled=True, axis_index_groups=groups)


def path_sums(keep, send, shots, levels):
    bits = levels - 1
    sizes = [1 << bits - 1 - level for level in range(bits)] + [1]
    arrived = exchange(send, 1 << bits)
    for bit in range(-1, bits - 1):
        sums = keep + arrived.astype(F32)
        mine, other, start = [], [], 0
        for level, count in enumerate(sizes):
            for node in range(count):
                rows = sums[start * shots : (start + 1) * shots]
                start += 1
                if level > bit or bit < 0:
                    mine.append(rows)
                    other.append(rows)
                else:
                    (other if node % 2 else mine).append(rows)
            if level <= bit:
                sizes[level] //= 2
        keep = jnp.concatenate(mine)
        arrived = exchange(jnp.concatenate(other).astype(BF16), 2 << bit if bit >= 0 else 1)
    return keep, arrived


def on_device(sources, transmission, media, sep_code, leaf_factors, sep_factors):
    leaves, shots, width2 = sources.shape[1:]
    leaf_n = width2 // 2
    front = transmission.shape[2] // 2
    sep_lib, sep_n = sep_factors.shape[0], sep_factors.shape[2]
    nleaf = lax.axis_size("leaf")
    levels = nleaf.bit_length() - 1
    capacity = max(2, leaves * 5 // (nleaf * 2))
    size = 2 * capacity * shots
    pairs = nleaf // 2
    slots = pairs * size
    source, tau = sources[0], transmission[0][:, None, :]
    place = jnp.stack([lax.axis_index("leaf").astype(jnp.int32), sep_code[0, 0] % sep_lib])
    own = leaf_factors[0]
    sibling = exchange(own, 1)

    face = jax.ShapeDtypeStruct((leaves, shots, 2 * front), BF16)
    leaving = call(
        functools.partial(face_kernel, front),
        jax.ShapeDtypeStruct((leaves, shots, 2 * front), F32),
        (source, tau),
        hbm=(0, 1),
        scratch=[VMEM(face.shape, BF16)] * 2 + [VMEM(tau.shape, F32), pltpu.SemaphoreType.DMA((3,))],
    )
    arriving = from_behind(leaving, "panel")
    tau_re, tau_im = tau[..., :front], tau[..., front:]
    for _ in range(lax.axis_size("panel") - 2):
        real = arriving[..., :front] + source[..., leaf_n - front : leaf_n].astype(F32)
        imag = arriving[..., front:] + source[..., 2 * leaf_n - front :].astype(F32)
        leaving = jnp.concatenate([tau_re * real - tau_im * imag, tau_re * imag + tau_im * real], axis=-1)
        arriving = from_behind(leaving, "panel")

    kinds = jnp.repeat(media[0, :, 0], shots)[None, :]
    rows = leaves * shots
    blocks = jax.ShapeDtypeStruct((slots, width2), BF16)
    sent = call(
        functools.partial(dispatch_kernel, shots, capacity, front),
        blocks,
        (place, kinds, source.reshape(rows, width2), arriving.reshape(rows, 2 * front)),
        smem=(0,),
        hbm_out=(0,),
        scratch=[VMEM((rows, width2), BF16), VMEM((slots, width2), BF16), pltpu.SemaphoreType.DMA((2,))],
    )
    arrived = to_pairs(sent.reshape(pairs, size, width2)).reshape(slots, width2)
    nodes = jax.ShapeDtypeStruct((pairs * shots, 2 * sep_n + LANES), F32)
    solved, keep, send = call(
        functools.partial(leaf_kernel, capacity, shots, sep_n),
        [blocks, nodes, jax.ShapeDtypeStruct(nodes.shape, BF16)],
        (place, arrived, own, sibling),
        smem=(0,),
        hbm_out=(0,),
        scratch=[
            VMEM((slots, leaf_n), BF16),
            VMEM((slots, width2), BF16),
            VMEM((slots, 2 * sep_n), BF16),
            pltpu.SemaphoreType.DMA((1,)),
        ],
    )
    back = to_pairs(solved.reshape(pairs, size, width2)).reshape(slots, width2)
    keep, arrived = path_sums(keep, send, shots, levels)
    scales = [1.0 / math.sqrt(leaves * 2 ** (level + 1)) for level in range(levels)]
    above = call(
        functools.partial(tree_kernel, scales),
        jax.ShapeDtypeStruct((2 * shots, sep_n), F32),
        (keep, arrived, sep_factors),
        cost=(1, 1),
    )
    result = call(
        functools.partial(result_kernel, shots, capacity),
        jax.ShapeDtypeStruct((rows, width2), BF16),
        (place, kinds, above, back),
        smem=(0,),
    )
    return result.reshape(1, leaves, shots, width2)


def solution(mesh):
    return jax.shard_map(
        on_device,
        mesh=mesh,
        in_specs=(
            P("panel", "leaf", None, None),
            P("panel", "leaf", None),
            P("panel", "leaf", None),
            P("panel", "leaf"),
            P("leaf", None, None, None),
            P(),
        ),
        out_specs=P("panel", "leaf", None, None),
        check_vma=False,
    )
```

time: 80.5 us -> 67.4 us (0.84)
  blocking collectives: 0 us -> 26 us
  starting transfers between devices: 37.1 us -> 12.9 us
  local copies, waits for them, and re-layouts: 20.5 us -> 4.8 us
  Pallas kernels: 4.72 us -> 7.41 us
  other arithmetic: 1.82 us -> 0.17 us
    ppermute x19 -> x5, starting transfers between devices: 32.7 us -> 4.53 us  [exchange(): return lax.ppermute(value, 'leaf', pairs)]
    all_to_all x0 -> x1, blocking collectives: none -> 26 us  [to_pairs(): lax.all_to_all(value, 'leaf', 0, 0, tiled=True, axis_index_groups=groups)]
    unnamed x42 -> x8, local copies, waits for them, and re-layouts: 16.3 us -> 1.95 us
    all_to_all x0 -> x1, waiting for transfers between devices: none -> 6.08 us  [to_pairs(): lax.all_to_all(value, 'leaf', 0, 0, tiled=True, axis_index_groups=groups)]
    ppermute x19 -> x5, waiting for transfers between devices: 14.9 us -> 8.87 us  [exchange(): return lax.ppermute(value, 'leaf', pairs)]
    all_to_all x0 -> x1, starting transfers between devices: none -> 3.99 us  [to_pairs(): lax.all_to_all(value, 'leaf', 0, 0, tiled=True, axis_index_groups=groups)]
    pallas_call x6 -> x5, Pallas kernels: 4.72 us -> 7.41 us  [call(): pl.pallas_call(kernel, out_shape=out_shape, in_specs=[pl.BlockSpec(memory...]
    reduce_sum x3 -> x0, other arithmetic: 0.88 us -> none  [on_device(): share.reshape((share.shape[0] // 2, 2) + share.shape[1:]).sum(axis=1)]
  transfers between devices with their start and end apart: 20 -> 7, of which waited for: 5 -> 4; matrix products, arithmetic and copies ran while one was open for 4% -> 3% of each run, Pallas kernels for 4% -> 4%
where the time goes in v4:
time: 67.4 us; the launch traced here: 67 us
  blocking collectives  26 us (39%)
  waiting for transfers between devices  15 us (22%)
  starting transfers between devices  12.9 us (19%)
  Pallas kernels  7.41 us (11%)
  local copies, waits for them, and re-layouts  4.8 us (7%)
  between operations  0.81 us (1%)
    all_to_all x1, blocking collectives, to_pairs(): lax.all_to_all(value, 'leaf', 0, 0, tiled=True, axis_index_groups=groups)  26 us
    ppermute x5, waiting for transfers between devices, exchange(): return lax.ppermute(value, 'leaf', pairs)  8.87 us
    pallas_call x5, Pallas kernels, call(): pl.pallas_call(kernel, out_shape=out_shape, in_specs=[pl.BlockSpec(memory...  7.41 us
    all_to_all x1, waiting for transfers between devices, to_pairs(): lax.all_to_all(value, 'leaf', 0, 0, tiled=True, axis_index_groups=groups)  6.08 us
    ppermute x5, starting transfers between devices, exchange(): return lax.ppermute(value, 'leaf', pairs)  4.53 us
    ppermute x1, starting transfers between devices, from_behind(): return lax.ppermute(value, axis, [(at, at + 1) for at in range(count - 1)])  4.35 us
    all_to_all x1, starting transfers between devices, to_pairs(): lax.all_to_all(value, 'leaf', 0, 0, tiled=True, axis_index_groups=groups)  3.99 us
    unnamed x8, local copies, waits for them, and re-layouts  1.95 us
  transfers between devices with their start and end apart: 7, of which 4 were waited for; matrix products, arithmetic and copies ran while one was open for 3% of the time, Pallas kernels for 4%

profile of v4, /device:TPU:0, one launch (start us, length us, event | category | flops | bytes accessed | tf_op | source)
XLA Modules:
  0.0 67.0 jit_solution(5040381131030172278)
XLA Ops:
  0.0 0.5 collective-permute-start.1
  0.5 1.2 %copy-done.1 = bf16[1,52,2,1536]{3,2,1,0:T(2,128)(2,1)S(1)} copy-done((bf16[1,52,2,1536]{3,2,1,0:T(2,128)(2,1)S(1)}, bf16[1,52,2,1536]{3,2,1,0:T(2,128)(2,1)}, u32[]{:S(2)}) %copy-start.1) | copy-done | bytes 319512
  1.7 0.7 %copy-done.3 = f32[1,52,128]{2,0,1:T(1,128)S(1)} copy-done((f32[1,52,128]{2,0,1:T(1,128)S(1)}, f32[1,52,128]{2,0,1:T(1,128)}, u32[]{:S(2)}) %copy-start.3) | copy-done | bytes 26648
  2.4 0.3 shard_map.64
  2.7 4.3 %collective-permute-start = (f32[52,2,128]{2,1,0:T(2,128)S(1)}, f32[52,2,128]{2,1,0:T(2,128)S(1)}, u32[]{:S(2)}, u32[]{:S(2)}) collective-permute-start(f32[52,2,128]{2,1,0:T(2,128)S(1)} %shard_map.64), channel_id=1, source_target_pairs={{0,16},{1,17},{2,18},{3,19},{4,20},{5,21},{6,22},{7,23},{8,24},{9,... | collective-permute-start | bytes 159752 | tf_op jit(solution)/shard_map/ppermute | solution.py:19
  7.7 0.1 pad_add_fusion.place_ref
  7.8 1.1 %reshape_squeeze.3.rows_ref = bf16[104,1536]{1,0:T(8,128)(2,1)S(1)} reshape(bf16[1,52,2,1536]{3,2,1,0:T(2,128)(2,1)} %param.6) | data formatting | bytes 638976 | tf_op jit(solution)/shard_map/reshape;squeeze | solution.py:268
  8.9 0.7 %broadcast_in_dim.3 = s32[52,2]{1,0:T(8,128)S(1)} broadcast(s32[52]{0:T(128)} %bitcast.23), dimensions={0} | broadcast | bytes 624 | tf_op jit(solution)/shard_map/broadcast_in_dim | solution.py:262
  9.6 0.1 broadcast_in_dim_reshape.3.kinds_ref
  9.8 1.3 %shard_map.65 = bf16[256,1536]{1,0:T(8,128)(2,1)S(1)} custom-call(s32[2]{0:T(128)S(1)} %pad_add_fusion.place_ref, s32[1,104]{1,0:T(1,128)S(1)} %broadcast_in_dim_reshape.3.kinds_ref, bf16[104,1536]{1,0:T(8,128)(2,1)S(1)} %reshape_squeeze.3.rows_ref, f32[104,128]{1,0:T(8,128)S(1)} %bitcast.21), custom_call_target="tpu_custom_call" | custom-call | tf_op jit(solution)/shard_map/pallas_call | solution.py:191
  11.0 26.0 %all_to_all.10 = bf16[8,32,1536]{2,1,0:T(8,128)(2,1)S(1)} all-to-all(bf16[8,32,1536]{2,1,0:T(8,128)(2,1)S(1)} %bitcast.16), channel_id=1, replica_groups={{0,2,4,6,8,10,12,14},{1,3,5,7,9,11,13,15},{16,18,20,22,24,26,28,30},{17..., dimensions={0} | all-to-all | bytes 1572864 | tf_op jit(solution)/shard_map/all_to_all | solution.py:204
  37.0 4.0 %shard_map.66 = (bf16[256,1536]{1,0:T(8,128)(2,1)}, f32[16,896]{1,0:T(8,128)S(1)}, bf16[16,896]{1,0:T(8,128)(2,1)S(1)}) custom-call(s32[2]{0:T(128)S(1)} %pad_add_fusion.place_ref, bf16[256,1536]{1,0:T(8,128)(2,1)S(1)} %bitcast.17, bf16[2,768,768]{2,1,0:T(8,128)(2,1)S(1)} %bitcast.19, bf16[2,768,768]{2,1,0:T(8,128)(2,1)} %collective-permute-done.1.sibling_ref), custom_call_target="tpu_custom_call" | custom-call | tf_op jit(solution)/shard_map/pallas_call | solution.py:191
  41.0 1.2 %collective-permute-start.2 = (bf16[16,896]{1,0:T(8,128)(2,1)S(1)}, bf16[16,896]{1,0:T(8,128)(2,1)S(1)}, u32[]{:S(2)}, u32[]{:S(2)}) collective-permute-start(bf16[16,896]{1,0:T(8,128)(2,1)S(1)} %get-tuple-element.9), channel_id=1, source_target_pairs={{0,8},{1,9},{2,10},{3,11},{4,12},{5,13},{6,14},{7,15},{8,0},{9,1},... | collective-permute-start | bytes 86024 | tf_op jit(solution)/shard_map/ppermute | solution.py:24
  42.2 4.0 %all-to-all-start.1 = ((bf16[8,32,1536]{2,1,0:T(8,128)(2,1)}), bf16[8,32,1536]{2,1,0:T(8,128)(2,1)S(1)}, u32[]{:S(2)}, u32[]{:S(2)}) async-start(bf16[8,32,1536]{2,1,0:T(8,128)(2,1)} %bitcast.10), calls=%async_computation.1 | async-start | bytes 1572864 | tf_op jit(solution)/shard_map/all_to_all | solution.py:204
  46.2 0.1 collective-permute-start.3
  46.3 1.2 %collective-permute-done.3 = bf16[16,896]{1,0:T(8,128)(2,1)S(1)} collective-permute-done((bf16[16,896]{1,0:T(8,128)(2,1)S(1)}, bf16[16,896]{1,0:T(8,128)(2,1)S(1)}, u32[]{:S(2)}, u32[]{:S(2)}) %collective-permute-start.3) | collective-permute-done | bytes 28704 | tf_op jit(solution)/shard_map/ppermute | solution.py:24
  47.6 2.1 %collective-permute-start.4 = (bf16[12,896]{1,0:T(8,128)(2,1)S(1)}, bf16[12,896]{1,0:T(8,128)(2,1)S(1)}, u32[]{:S(2)}, u32[]{:S(2)}) collective-permute-start(bf16[12,896]{1,0:T(8,128)(2,1)S(1)} %pad_maximum_fusion), channel_id=1, source_target_pairs={{0,2},{1,3},{2,0},{3,1},{4,6},{5,7},{6,4},{7,5},{8,10},{9,11},{10,... | collective-permute-start | bytes 64520 | tf_op jit(solution)/shard_map/ppermute | solution.py:24
  49.7 3.5 %collective-permute-done.4 = bf16[12,896]{1,0:T(8,128)(2,1)S(1)} collective-permute-done((bf16[12,896]{1,0:T(8,128)(2,1)S(1)}, bf16[12,896]{1,0:T(8,128)(2,1)S(1)}, u32[]{:S(2)}, u32[]{:S(2)}) %collective-permute-start.4) | collective-permute-done | bytes 21536 | tf_op jit(solution)/shard_map/ppermute | solution.py:24
  53.3 0.7 %collective-permute-start.5 = (bf16[8,896]{1,0:T(8,128)(2,1)S(1)}, bf16[8,896]{1,0:T(8,128)(2,1)S(1)}, u32[]{:S(2)}, u32[]{:S(2)}) collective-permute-start(bf16[8,896]{1,0:T(8,128)(2,1)S(1)} %pad_maximum_fusion.2), channel_id=1, source_target_pairs={{0,4},{1,5},{2,6},{3,7},{4,0},{5,1},{6,2},{7,3},{8,12},{9,13},{10,... | collective-permute-start | bytes 43016 | tf_op jit(solution)/shard_map/ppermute | solution.py:24
  54.1 4.2 %collective-permute-done.5.arrived_ref = bf16[8,896]{1,0:T(8,128)(2,1)S(1)} collective-permute-done((bf16[8,896]{1,0:T(8,128)(2,1)S(1)}, bf16[8,896]{1,0:T(8,128)(2,1)S(1)}, u32[]{:S(2)}, u32[]{:S(2)}) %collective-permute-start.5) | collective-permute-done | bytes 14368 | tf_op jit(solution)/shard_map/ppermute | solution.py:24
  58.2 0.9 %shard_map.67.above_ref = f32[4,384]{1,0:T(4,128)S(1)} custom-call(f32[8,896]{1,0:T(8,128)S(1)} %pad_maximum_fusion.1.keep_ref, bf16[8,896]{1,0:T(8,128)(2,1)S(1)} %collective-permute-done.5.arrived_ref, bf16[2,2,384,384]{3,2,1,0:T(8,128)(2,1)S(1)} %copy-done.2), custom_call_target="tpu_custom_call" | custom-call | flops 1 | bytes 1 | tf_op jit(solution)/shard_map/pallas_call | solution.py:191
  59.1 6.1 %all-to-all-done.1 = bf16[8,32,1536]{2,1,0:T(8,128)(2,1)S(1)} async-done(((bf16[8,32,1536]{2,1,0:T(8,128)(2,1)}), bf16[8,32,1536]{2,1,0:T(8,128)(2,1)S(1)}, u32[]{:S(2)}, u32[]{:S(2)}) %all-to-all-start.1) | async-done | bytes 786464 | tf_op jit(solution)/shard_map/all_to_all | solution.py:204
  65.2 0.9 %shard_map.68 = bf16[104,1536]{1,0:T(8,128)(2,1)S(1)} custom-call(s32[2]{0:T(128)S(1)} %pad_add_fusion.place_ref, s32[1,104]{1,0:T(1,128)S(1)} %broadcast_in_dim_reshape.3.kinds_ref, f32[4,384]{1,0:T(4,128)S(1)} %shard_map.67.above_ref, bf16[256,1536]{1,0:T(8,128)(2,1)S(1)} %bitcast.15), custom_call_target="tpu_custom_call" | custom-call | tf_op jit(solution)/shard_map/pallas_call | solution.py:191
  66.1 0.8 %reshape.23 = bf16[1,52,2,1536]{3,2,1,0:T(2,128)(2,1)} reshape(bf16[104,1536]{1,0:T(8,128)(2,1)S(1)} %shard_map.68) | data formatting | bytes 638976 | tf_op jit(solution)/shard_map/reshape | solution.py:303
  (23 shorter events, 0.2 us)
Async XLA Ops:
  0.0 37.0 %copy-start = (bf16[1,2,768,768]{3,2,1,0:T(8,128)(2,1)S(1)}, bf16[1,2,768,768]{3,2,1,0:T(8,128)(2,1)}, u32[]{:S(2)}) copy-start(bf16[1,2,768,768]{3,2,1,0:T(8,128)(2,1)} %param.10) | copy-start | bytes 7077892
  0.0 37.0 %collective-permute-start.1 = (bf16[2,768,768]{2,1,0:T(8,128)(2,1)}, bf16[2,768,768]{2,1,0:T(8,128)(2,1)}, u32[]{:S(2)}, u32[]{:S(2)}) collective-permute-start(bf16[2,768,768]{2,1,0:T(8,128)(2,1)} %bitcast.18), channel_id=1, source_target_pairs={{0,1},{1,0},{2,3},{3,2},{4,5},{5,4},{6,7},{7,6},{8,9},{9,8},{10,11... | collective-permute-start | bytes 7077896 | tf_op jit(solution)/shard_map/ppermute | solution.py:24
  0.5 1.2 %copy-start.1 = (bf16[1,52,2,1536]{3,2,1,0:T(2,128)(2,1)S(1)}, bf16[1,52,2,1536]{3,2,1,0:T(2,128)(2,1)}, u32[]{:S(2)}) copy-start(bf16[1,52,2,1536]{3,2,1,0:T(2,128)(2,1)} %param.6) | copy-start | bytes 958468
  1.7 0.7 %copy-start.3 = (f32[1,52,128]{2,0,1:T(1,128)S(1)}, f32[1,52,128]{2,0,1:T(1,128)}, u32[]{:S(2)}) copy-start(f32[1,52,128]{2,0,1:T(1,128)} %param.7) | copy-start | bytes 79876
  2.7 7.1 %collective-permute-start = (f32[52,2,128]{2,1,0:T(2,128)S(1)}, f32[52,2,128]{2,1,0:T(2,128)S(1)}, u32[]{:S(2)}, u32[]{:S(2)}) collective-permute-start(f32[52,2,128]{2,1,0:T(2,128)S(1)} %shard_map.64), channel_id=1, source_target_pairs={{0,16},{1,17},{2,18},{3,19},{4,20},{5,21},{6,22},{7,23},{8,24},{9,... | collective-permute-start | bytes 159752 | tf_op jit(solution)/shard_map/ppermute | solution.py:19
  41.0 17.2 %copy-start.2 = (bf16[2,2,384,384]{3,2,1,0:T(8,128)(2,1)S(1)}, bf16[2,2,384,384]{3,2,1,0:T(8,128)(2,1)}, u32[]{:S(2)}) copy-start(bf16[2,2,384,384]{3,2,1,0:T(8,128)(2,1)} %factors_ref.1) | copy-start | bytes 3538948
  41.0 5.2 %collective-permute-start.2 = (bf16[16,896]{1,0:T(8,128)(2,1)S(1)}, bf16[16,896]{1,0:T(8,128)(2,1)S(1)}, u32[]{:S(2)}, u32[]{:S(2)}) collective-permute-start(bf16[16,896]{1,0:T(8,128)(2,1)S(1)} %get-tuple-element.9), channel_id=1, source_target_pairs={{0,8},{1,9},{2,10},{3,11},{4,12},{5,13},{6,14},{7,15},{8,0},{9,1},... | collective-permute-start | bytes 86024 | tf_op jit(solution)/shard_map/ppermute | solution.py:24
  42.2 23.0 %all-to-all-start.1 = ((bf16[8,32,1536]{2,1,0:T(8,128)(2,1)}), bf16[8,32,1536]{2,1,0:T(8,128)(2,1)S(1)}, u32[]{:S(2)}, u32[]{:S(2)}) async-start(bf16[8,32,1536]{2,1,0:T(8,128)(2,1)} %bitcast.10), calls=%async_computation.1 | async-start | bytes 1572864 | tf_op jit(solution)/shard_map/all_to_all | solution.py:204
  46.2 1.3 %collective-permute-start.3 = (bf16[16,896]{1,0:T(8,128)(2,1)S(1)}, bf16[16,896]{1,0:T(8,128)(2,1)S(1)}, u32[]{:S(2)}, u32[]{:S(2)}) collective-permute-start(bf16[16,896]{1,0:T(8,128)(2,1)S(1)} %fusion), channel_id=1, source_target_pairs={{0,1},{1,0},{2,3},{3,2},{4,5},{5,4},{6,7},{7,6},{8,9},{9,8},{10,11... | collective-permute-start | bytes 86024 | tf_op jit(solution)/shard_map/ppermute | solution.py:24
  47.6 5.6 %collective-permute-start.4 = (bf16[12,896]{1,0:T(8,128)(2,1)S(1)}, bf16[12,896]{1,0:T(8,128)(2,1)S(1)}, u32[]{:S(2)}, u32[]{:S(2)}) collective-permute-start(bf16[12,896]{1,0:T(8,128)(2,1)S(1)} %pad_maximum_fusion), channel_id=1, source_target_pairs={{0,2},{1,3},{2,0},{3,1},{4,6},{5,7},{6,4},{7,5},{8,10},{9,11},{10,... | collective-permute-start | bytes 64520 | tf_op jit(solution)/shard_map/ppermute | solution.py:24
  53.3 4.9 %collective-permute-start.5 = (bf16[8,896]{1,0:T(8,128)(2,1)S(1)}, bf16[8,896]{1,0:T(8,128)(2,1)S(1)}, u32[]{:S(2)}, u32[]{:S(2)}) collective-permute-start(bf16[8,896]{1,0:T(8,128)(2,1)S(1)} %pad_maximum_fusion.2), channel_id=1, source_target_pairs={{0,4},{1,5},{2,6},{3,7},{4,0},{5,1},{6,2},{7,3},{8,12},{9,13},{10,... | collective-permute-start | bytes 43016 | tf_op jit(solution)/shard_map/ppermute | solution.py:24

commit v5 on v4

--- a/solution.py
+++ b/solution.py
@@ -32,9 +32,12 @@
     return mask.astype(F32).astype(BF16)
 
 
-def slot_of(place_ref, kinds_ref, shots, capacity):
-    kinds = kinds_ref[...]
-    count = kinds.shape[1]
+def slot_kernel(shots, capacity, media_ref, to_slots_ref, from_slots_ref):
+    slots, count = to_slots_ref.shape
+    leaves = media_ref.shape[1]
+    leaf = lax.broadcasted_iota(jnp.int32, (leaves, count), 0)
+    of_row = one_hot(lax.broadcasted_iota(jnp.int32, (leaves, count), 1) // shots == leaf)
+    kinds = dot(media_ref[...].astype(F32).astype(BF16), of_row).astype(jnp.int32)
     before = lax.broadcasted_iota(jnp.int32, (count, count), 0)
     later = lax.broadcasted_iota(jnp.int32, (count, count), 1)
     across = jnp.broadcast_to(kinds, (count, count))
@@ -45,10 +48,12 @@
     rank_col = jnp.sum((same & (later < before)).astype(jnp.int32), axis=1, keepdims=True)
     shot_row = lax.broadcasted_iota(jnp.int32, (1, count), 1) % shots
     shot_col = lax.broadcasted_iota(jnp.int32, (count, 1), 0) % shots
-    parity = place_ref[0] & 1
-    row = ((kinds ^ parity) * shots + shot_row) * capacity + rank_row
+    me = lax.axis_index("leaf")
+    parity = me % 2
+    row = ((kinds ^ me) * shots + shot_row) * capacity + rank_row
     col = ((kinds_down ^ parity) * shots + shot_col) * capacity + rank_col
-    return row, col
+    to_slots_ref[...] = one_hot(lax.broadcasted_iota(jnp.int32, (slots, count), 0) == row)
+    from_slots_ref[...] = one_hot(lax.broadcasted_iota(jnp.int32, (count, slots), 1) == col)
 
 
 def face_kernel(front, source_ref, tau_ref, out_ref, re_ref, im_ref, through_ref, sems):
@@ -74,7 +79,8 @@
     out_ref[...] = by_same * face + by_other * other
 
 
-def dispatch_kernel(shots, capacity, front, place_ref, kinds_ref, rows_ref, arriving_ref, out_ref, rhs_ref, send_ref, sems):
+def dispatch_kernel(front, pick_ref, rows_ref, arriving_ref, _, *refs):
+    out_refs, rhs_ref = refs[:-1], refs[-1]
     leaf_n = rows_ref.shape[1] // 2
     rhs_ref[...] = rows_ref[...]
     for part in range(2):
@@ -85,68 +91,81 @@
             incoming = pltpu.roll(incoming, front, 1)
         incoming = jnp.where(lane >= front, incoming, 0.0)
         rhs_ref[:, face] = (rows_ref[:, face].astype(F32) + incoming).astype(BF16)
-    row, _ = slot_of(place_ref, kinds_ref, shots, capacity)
-    place = lax.broadcasted_iota(jnp.int32, (send_ref.shape[0], row.shape[1]), 0)
-    pick = one_hot(place == row)
-    copies = []
-    for part in range(2):
-        columns = pl.ds(part * leaf_n, leaf_n)
-        send_ref[:, columns] = dot(pick, rhs_ref[:, columns]).astype(BF16)
-        copies.append(pltpu.make_async_copy(send_ref.at[:, columns], out_ref.at[:, columns], sems.at[part]))
-        copies[part].start()
-    for copy in copies:
-        copy.wait()
-
-
-def leaf_kernel(capacity, shots, sep_n, place_ref, arrived_ref, own_ref, sibling_ref, out_ref, keep_ref, send_ref, *refs):
-    rows_ref, solved_ref, top_ref, sems = refs
+    size = out_refs[0].shape[0]
+    send = dot(pick_ref[...], rhs_ref[...]).astype(BF16)
+    for at, out_ref in enumerate(out_refs):
+        out_ref[...] = send[at * size : (at + 1) * size]
+
+
+def stage_kernel(from_ref, _, to_ref):
+    to_ref[...] = from_ref[...]
+
+
+def leaf_kernel(shots, sep_n, order, code_ref, own_ref, sibling_ref, *refs):
+    blocks, (out_ref, keep_ref, send_ref) = dict(zip(order, refs[:-8])), refs[-8:-5]
+    factor_ref, rows_ref, solved_ref, load_sems, sems = refs[-5:]
     leaf_n = own_ref.shape[1]
-    size = capacity * shots
-    pairs = arrived_ref.shape[0] // (2 * size)
+    loads = []
+    for at in range(4):
+        rows = (at // 2, pl.ds(at % 2 * (leaf_n // 2), leaf_n // 2))
+        loads.append(pltpu.make_async_copy(sibling_ref.at[rows], factor_ref.at[rows], load_sems.at[at]))
+        loads[at].start()
+    pairs, _, size, _ = solved_ref.shape
+    capacity = size // shots
     half = pairs * size
-    copies = []
-    for entry, factor_ref in enumerate((own_ref, sibling_ref)):
-        for at in range(pairs):
-            first = (2 * at + entry) * size
-            for part in range(2):
-                rows_ref[part * half + at * size : part * half + (at + 1) * size] = arrived_ref[
-                    first : first + size, part * leaf_n : (part + 1) * leaf_n
-                ]
-        by_re, by_im = dot(rows_ref[...], factor_ref[0]), dot(rows_ref[...], factor_ref[1])
-        solved = ((by_re[:half] - by_im[half:]).astype(BF16), (by_im[:half] + by_re[half:]).astype(BF16))
-        for part in range(2):
-            for at in range(pairs):
-                first = (2 * at + entry) * size
-                solved_ref[first : first + size, part * leaf_n : (part + 1) * leaf_n] = solved[part][
-                    at * size : (at + 1) * size
-                ]
-            top_ref[entry * half : (entry + 1) * half, part * sep_n : (part + 1) * sep_n] = solved[part][:, :sep_n]
-    out = pltpu.make_async_copy(solved_ref, out_ref, sems.at[0])
-    out.start()
-    own_pair = place_ref[0] >> 1
-    code = place_ref[1].astype(F32)
+    count = keep_ref.shape[0]
+    own_pair = lax.axis_index("leaf") // 2
     bits = pairs.bit_length() - 1
-    for other, ref in enumerate((keep_ref, send_ref)):
-        count = ref.shape[0]
-        row = lax.broadcasted_iota(jnp.int32, (count, 2 * half), 0)
-        place = lax.broadcasted_iota(jnp.int32, (count, 2 * half), 1)
-        distance = (place % half // size) ^ own_pair
-        member = row < 0
-        here = lax.broadcasted_iota(jnp.int32, (count, LANES), 0) < 0
-        first = 0
+    row = lax.broadcasted_iota(jnp.int32, (2 * count, half), 0)
+    place = lax.broadcasted_iota(jnp.int32, (2 * count, half), 1)
+    lead = lax.broadcasted_iota(jnp.int32, (2 * count, LANES), 0)
+    distance = place // size
+    member, here, first = row < 0, lead < 0, 0
+    for other in range(2):
         for level in range(bits + 1):
-            nodes = max(1, 1 << bits - 1 - level) if level < bits else 1
+            nodes = 1 << bits - 1 - level if level < bits else 1
             node = (row - first) // shots + (other * nodes if level < bits else 0)
             inside = (row >= first) & (row < first + nodes * shots)
             member |= inside & (distance >> level == node)
             if not (other and level < bits):
-                lead = lax.broadcasted_iota(jnp.int32, (count, LANES), 0)
                 here |= (lead >= first) & (lead < first + shots)
             first += nodes * shots
-        member &= place % size // capacity == row % shots
-        ref[:, : 2 * sep_n] = dot(one_hot(member), top_ref[...]).astype(ref.dtype)
-        ref[:, 2 * sep_n :] = jnp.where(here, code, 0.0).astype(ref.dtype)
-    out.wait()
+    member = one_hot(member & (place % size // capacity == row % shots))
+    codes = jnp.where(here, code_ref[0, 0].astype(F32), 0.0)
+
+    copies, sums = [], [0.0, 0.0]
+    for entry in range(2):
+        for at in range(pairs):
+            real = blocks[at][entry * size : (entry + 1) * size, :leaf_n]
+            imag = blocks[at][entry * size : (entry + 1) * size, leaf_n:]
+            first = at * size
+            rows_ref[first : first + size, :leaf_n] = real
+            rows_ref[first : first + size, leaf_n:] = -imag
+            rows_ref[half + first : half + first + size, :leaf_n] = imag
+            rows_ref[half + first : half + first + size, leaf_n:] = real
+        if entry:
+            for load in loads:
+                load.wait()
+        factor = (factor_ref if entry else own_ref)[...].reshape(2 * leaf_n, leaf_n)
+        for part in range(2):
+            solved = dot(rows_ref[part * half : (part + 1) * half], factor).astype(BF16)
+            columns = pl.ds(part * leaf_n, leaf_n)
+            for at in range(pairs):
+                solved_ref[at, entry, :, columns] = solved[at * size : (at + 1) * size]
+            sums[part] += dot(member, solved[:, :sep_n])
+        for at in range(pairs):
+            copies.append(
+                pltpu.make_async_copy(
+                    solved_ref.at[at, entry], out_ref.at[own_pair ^ at, entry], sems.at[entry * pairs + at]
+                )
+            )
+            copies[-1].start()
+    for ref, rows in ((keep_ref, slice(0, count)), (send_ref, slice(count, 2 * count))):
+        for part in range(2):
+            ref[:, part * sep_n : (part + 1) * sep_n] = sums[part][rows].astype(ref.dtype)
+        ref[:, 2 * sep_n :] = codes[rows].astype(ref.dtype)
+    for copy in copies:
+        copy.wait()
 
 
 def tree_kernel(scales, keep_ref, arrived_ref, factors_ref, out_ref):
@@ -165,26 +184,24 @@
     out_ref[...] = above
 
 
-def result_kernel(shots, capacity, place_ref, kinds_ref, above_ref, back_ref, out_ref):
-    count, width2 = out_ref.shape
+def result_kernel(shots, pick_ref, above_ref, back_ref, out_ref):
+    leaves, _, width2 = out_ref.shape
+    count = leaves * shots
     leaf_n = width2 // 2
     sep_n = above_ref.shape[1]
-    _, col = slot_of(place_ref, kinds_ref, shots, capacity)
-    place = lax.broadcasted_iota(jnp.int32, (count, back_ref.shape[0]), 1)
-    pick = one_hot(place == col)
     shot = lax.broadcasted_iota(jnp.int32, (count, sep_n), 0) % shots
     for part in range(2):
         start = part * leaf_n
-        solved = dot(pick, back_ref[:, start : start + leaf_n])
+        solved = dot(pick_ref[...], back_ref[:, start : start + leaf_n])
         lifted = jnp.zeros((count, sep_n), F32)
         for at in range(shots):
             here = part * shots + at
             lifted = jnp.where(shot == at, above_ref[here : here + 1], lifted)
-        out_ref[:, start : start + sep_n] = (solved[:, :sep_n] - lifted).astype(BF16)
-        out_ref[:, start + sep_n : start + leaf_n] = solved[:, sep_n:].astype(BF16)
-
-
-def call(kernel, out_shape, args, smem=(), hbm=(), hbm_out=(), scratch=(), cost=None, limit=16):
+        solved = jnp.concatenate([solved[:, :sep_n] - lifted, solved[:, sep_n:]], axis=1).astype(BF16)
+        out_ref[:, :, start : start + leaf_n] = solved.reshape(leaves, shots, leaf_n)
+
+
+def call(kernel, out_shape, args, smem=(), hbm=(), hbm_out=(), aliases={}, scratch=(), cost=None, limit=16):
     spaces = [pltpu.SMEM if at in smem else pltpu.HBM if at in hbm else VMEM for at in range(len(args))]
     shapes = out_shape if isinstance(out_shape, list) else [out_shape]
     out_specs = [pl.BlockSpec(memory_space=pltpu.HBM if at in hbm_out else VMEM) for at in range(len(shapes))]
@@ -194,6 +211,7 @@
         in_specs=[pl.BlockSpec(memory_space=space) for space in spaces],
         out_specs=out_specs if isinstance(out_shape, list) else out_specs[0],
         scratch_shapes=list(scratch),
+        input_output_aliases=aliases,
         cost_estimate=cost and pl.CostEstimate(flops=cost[0], bytes_accessed=cost[1], transcendentals=0),
         compiler_params=pltpu.CompilerParams(vmem_limit_bytes=limit * 2**20),
     )(*args)
@@ -239,7 +257,6 @@
     pairs = nleaf // 2
     slots = pairs * size
     source, tau = sources[0], transmission[0][:, None, :]
-    place = jnp.stack([lax.axis_index("leaf").astype(jnp.int32), sep_code[0, 0] % sep_lib])
     own = leaf_factors[0]
     sibling = exchange(own, 1)
 
@@ -250,6 +267,7 @@
         (source, tau),
         hbm=(0, 1),
         scratch=[VMEM(face.shape, BF16)] * 2 + [VMEM(tau.shape, F32), pltpu.SemaphoreType.DMA((3,))],
+        limit=60,
     )
     arriving = from_behind(leaving, "panel")
     tau_re, tau_im = tau[..., :front], tau[..., front:]
@@ -259,30 +277,39 @@
         leaving = jnp.concatenate([tau_re * real - tau_im * imag, tau_re * imag + tau_im * real], axis=-1)
         arriving = from_behind(leaving, "panel")
 
-    kinds = jnp.repeat(media[0, :, 0], shots)[None, :]
     rows = leaves * shots
-    blocks = jax.ShapeDtypeStruct((slots, width2), BF16)
+    to_slots, from_slots = call(
+        functools.partial(slot_kernel, shots, capacity),
+        [jax.ShapeDtypeStruct((slots, rows), BF16), jax.ShapeDtypeStruct((rows, slots), BF16)],
+        (media[0].reshape(1, leaves),),
+    )
+    block = jax.ShapeDtypeStruct((size, width2), BF16)
     sent = call(
-        functools.partial(dispatch_kernel, shots, capacity, front),
-        blocks,
-        (place, kinds, source.reshape(rows, width2), arriving.reshape(rows, 2 * front)),
+        functools.partial(dispatch_kernel, front),
+        [block] * pairs,
+        (to_slots, source.reshape(rows, width2), arriving.reshape(rows, 2 * front), sibling),
+        hbm=(3,),
+        scratch=[VMEM((rows, width2), BF16)],
+    )
+    far, near = list(range(pairs // 2, pairs)), list(range(1, pairs // 2))
+    order = far[-1:] + near + far[-2::-1] + [0]
+    arrived = {at: exchange(sent[at], 2 * at) if at else sent[at] for at in order}
+    own = call(stage_kernel, jax.ShapeDtypeStruct(own.shape, BF16), (own, sent[0]), hbm=(1,))
+    nodes = jax.ShapeDtypeStruct((pairs * shots, 2 * sep_n + LANES), F32)
+    halves = (pairs, 2, size // 2, width2)
+    solved, keep, send = call(
+        functools.partial(leaf_kernel, shots, sep_n, order),
+        [jax.ShapeDtypeStruct(halves, BF16), nodes, jax.ShapeDtypeStruct(nodes.shape, BF16)],
+        (sep_code % sep_lib, own, sibling, *(arrived[at] for at in order)),
         smem=(0,),
-        hbm_out=(0,),
-        scratch=[VMEM((rows, width2), BF16), VMEM((slots, width2), BF16), pltpu.SemaphoreType.DMA((2,))],
-    )
-    arrived = to_pairs(sent.reshape(pairs, size, width2)).reshape(slots, width2)
-    nodes = jax.ShapeDtypeStruct((pairs * shots, 2 * sep_n + LANES), F32)
-    solved, keep, send = call(
-        functools.partial(leaf_kernel, capacity, shots, sep_n),
-        [blocks, nodes, jax.ShapeDtypeStruct(nodes.shape, BF16)],
-        (place, arrived, own, sibling),
-        smem=(0,),
+        hbm=(2,),
         hbm_out=(0,),
         scratch=[
-            VMEM((slots, leaf_n), BF16),
+            VMEM(own.shape, BF16),
             VMEM((slots, width2), BF16),
-            VMEM((slots, 2 * sep_n), BF16),
-            pltpu.SemaphoreType.DMA((1,)),
+            VMEM(halves, BF16),
+            pltpu.SemaphoreType.DMA((4,)),
+            pltpu.SemaphoreType.DMA((2 * pairs,)),
         ],
     )
     back = to_pairs(solved.reshape(pairs, size, width2)).reshape(slots, width2)
@@ -295,12 +322,11 @@
         cost=(1, 1),
     )
     result = call(
-        functools.partial(result_kernel, shots, capacity),
-        jax.ShapeDtypeStruct((rows, width2), BF16),
-        (place, kinds, above, back),
-        smem=(0,),
-    )
-    return result.reshape(1, leaves, shots, width2)
+        functools.partial(result_kernel, shots),
+        jax.ShapeDtypeStruct((leaves, shots, width2), BF16),
+        (from_slots, above, back),
+    )
+    return result[None]
 
 
 def solution(mesh):

time: 67.4 us -> 60.7 us (0.901)
  blocking collectives: 26 us -> 0 us
  starting transfers between devices: 12.9 us -> 24.8 us
  waiting for transfers between devices: 15 us -> 25 us
  local copies, waits for them, and re-layouts: 4.8 us -> 1.96 us
    all_to_all x1 -> x0, blocking collectives: 26 us -> none  [to_pairs(): lax.all_to_all(value, 'leaf', 0, 0, tiled=True, axis_index_groups=groups)]
    ppermute x5 -> x12, starting transfers between devices: 4.53 us -> 15.7 us  [exchange(): return lax.ppermute(value, 'leaf', pairs)]
    ppermute x5 -> x12, waiting for transfers between devices: 8.87 us -> 18.9 us  [exchange(): return lax.ppermute(value, 'leaf', pairs)]
    unnamed x8 -> x6, local copies, waits for them, and re-layouts: 1.95 us -> 0.81 us
    reshape x1 -> x0, local copies, waits for them, and re-layouts: 0.85 us -> none  [on_device(): return result.reshape(1, leaves, shots, width2)]
    broadcast_in_dim x1 -> x0, local copies, waits for them, and re-layouts: 0.73 us -> none  [on_device(): kinds = jnp.repeat(media[0, :, 0], shots)[None, :]]
    all_to_all x1, starting transfers between devices: 3.99 us -> 4.7 us  [to_pairs(): lax.all_to_all(value, 'leaf', 0, 0, tiled=True, axis_index_groups=groups)]
    pallas_call x5 -> x7, Pallas kernels: 7.41 us -> 7.6 us  [call(): pl.pallas_call(kernel, out_shape=out_shape, in_specs=[pl.BlockSpec(memory...]
  transfers between devices with their start and end apart: 7 -> 14, of which waited for: 4 -> 10; matrix products, arithmetic and copies ran while one was open for 3% -> 2% of each run, Pallas kernels for 4% -> 5%
where the time goes in v5:
time: 60.7 us; the launch traced here: 60.4 us
  waiting for transfers between devices  25 us (41%)
  starting transfers between devices  24.8 us (41%)
  Pallas kernels  7.6 us (13%)
  local copies, waits for them, and re-layouts  1.96 us (3%)
  between operations  0.87 us (1%)
    ppermute x12, waiting for transfers between devices, exchange(): return lax.ppermute(value, 'leaf', pairs)  18.9 us
    ppermute x12, starting transfers between devices, exchange(): return lax.ppermute(value, 'leaf', pairs)  15.7 us
    pallas_call x7, Pallas kernels, call(): pl.pallas_call(kernel, out_shape=out_shape, in_specs=[pl.BlockSpec(memory...  7.6 us
    all_to_all x1, waiting for transfers between devices, to_pairs(): lax.all_to_all(value, 'leaf', 0, 0, tiled=True, axis_index_groups=groups)  6.16 us
    all_to_all x1, starting transfers between devices, to_pairs(): lax.all_to_all(value, 'leaf', 0, 0, tiled=True, axis_index_groups=groups)  4.7 us
    ppermute x1, starting transfers between devices, from_behind(): return lax.ppermute(value, axis, [(at, at + 1) for at in range(count - 1)])  4.4 us
  transfers between devices with their start and end apart: 14, of which 10 were waited for; matrix products, arithmetic and copies ran while one was open for 2% of the time, Pallas kernels for 5%

profile of v5, /device:TPU:0, one launch (start us, length us, event | category | flops | bytes accessed | tf_op | source)
XLA Modules:
  0.0 60.4 jit_solution(12429828612676611053)
XLA Ops:
  0.0 0.5 collective-permute-start.1
  0.5 1.6 %shard_map.65 = f32[52,2,128]{2,1,0:T(2,128)} custom-call(bf16[52,2,1536]{2,1,0:T(2,128)(2,1)} %bitcast.13, f32[52,1,128]{2,1,0:T(1,128)} %bitcast.14), custom_call_target="tpu_custom_call" | custom-call | tf_op jit(solution)/shard_map/pallas_call | solution.py:208
  2.1 4.4 %collective-permute-start = (f32[52,2,128]{2,1,0:T(2,128)}, f32[52,2,128]{2,1,0:T(2,128)S(1)}, u32[]{:S(2)}, u32[]{:S(2)}) collective-permute-start(f32[52,2,128]{2,1,0:T(2,128)} %shard_map.65), channel_id=1, source_target_pairs={{0,16},{1,17},{2,18},{3,19},{4,20},{5,21},{6,22},{7,23},{8,24},{9,... | collective-permute-start | bytes 159752 | tf_op jit(solution)/shard_map/ppermute | solution.py:19
  6.5 1.1 %reshape_squeeze.7.rows_ref = bf16[104,1536]{1,0:T(8,128)(2,1)S(1)} reshape(bf16[1,52,2,1536]{3,2,1,0:T(2,128)(2,1)} %param.6) | data formatting | bytes 638976 | tf_op jit(solution)/shard_map/reshape;squeeze | solution.py:290
  7.6 0.8 %copy-done.2 = s32[1,52,1]{1,2,0:T(1,128)S(1)} copy-done((s32[1,52,1]{1,2,0:T(1,128)S(1)}, s32[1,52,1]{1,2,0:T(1,128)}, u32[]{:S(2)}) %copy-start.2) | copy-done | bytes 232
  9.1 4.6 %collective-permute-start.2 = (bf16[32,1536]{1,0:T(8,128)(2,1)S(1)}, bf16[32,1536]{1,0:T(8,128)(2,1)S(1)}, u32[]{:S(2)}, u32[]{:S(2)}) collective-permute-start(bf16[32,1536]{1,0:T(8,128)(2,1)S(1)} %get-tuple-element.21), channel_id=1, source_target_pairs={{0,14},{1,15},{2,12},{3,13},{4,10},{5,11},{6,8},{7,9},{8,6},{9,7},... | collective-permute-start | bytes 294920 | tf_op jit(solution)/shard_map/ppermute | solution.py:24
  13.8 0.5 collective-permute-start.3
  14.3 3.0 %collective-permute-start.5 = (bf16[32,1536]{1,0:T(8,128)(2,1)S(1)}, bf16[32,1536]{1,0:T(8,128)(2,1)S(1)}, u32[]{:S(2)}, u32[]{:S(2)}) collective-permute-start(bf16[32,1536]{1,0:T(8,128)(2,1)S(1)} %get-tuple-element.24), channel_id=1, source_target_pairs={{0,6},{1,7},{2,4},{3,5},{4,2},{5,3},{6,0},{7,1},{8,14},{9,15},{10,... | collective-permute-start | bytes 294920 | tf_op jit(solution)/shard_map/ppermute | solution.py:24
  17.6 2.8 %collective-permute-start.7 = (bf16[32,1536]{1,0:T(8,128)(2,1)S(1)}, bf16[32,1536]{1,0:T(8,128)(2,1)S(1)}, u32[]{:S(2)}, u32[]{:S(2)}) collective-permute-start(bf16[32,1536]{1,0:T(8,128)(2,1)S(1)} %get-tuple-element.26), channel_id=1, source_target_pairs={{0,10},{1,11},{2,8},{3,9},{4,14},{5,15},{6,12},{7,13},{8,2},{9,3},... | collective-permute-start | bytes 294920 | tf_op jit(solution)/shard_map/ppermute | solution.py:24
  20.4 1.1 %collective-permute-start.8 = (bf16[32,1536]{1,0:T(8,128)(2,1)S(1)}, bf16[32,1536]{1,0:T(8,128)(2,1)S(1)}, u32[]{:S(2)}, u32[]{:S(2)}) collective-permute-start(bf16[32,1536]{1,0:T(8,128)(2,1)S(1)} %get-tuple-element.27), channel_id=1, source_target_pairs={{0,8},{1,9},{2,10},{3,11},{4,12},{5,13},{6,14},{7,15},{8,0},{9,1},... | collective-permute-start | bytes 294920 | tf_op jit(solution)/shard_map/ppermute | solution.py:24
  22.3 1.1 %collective-permute-done.5.refs_3_ = bf16[32,1536]{1,0:T(8,128)(2,1)S(1)} collective-permute-done((bf16[32,1536]{1,0:T(8,128)(2,1)S(1)}, bf16[32,1536]{1,0:T(8,128)(2,1)S(1)}, u32[]{:S(2)}, u32[]{:S(2)}) %collective-permute-start.5) | collective-permute-done | bytes 98336 | tf_op jit(solution)/shard_map/ppermute | solution.py:24
  23.4 1.3 %collective-permute-done.6.refs_4_ = bf16[32,1536]{1,0:T(8,128)(2,1)S(1)} collective-permute-done((bf16[32,1536]{1,0:T(8,128)(2,1)S(1)}, bf16[32,1536]{1,0:T(8,128)(2,1)S(1)}, u32[]{:S(2)}, u32[]{:S(2)}) %collective-permute-start.6) | collective-permute-done | bytes 98336 | tf_op jit(solution)/shard_map/ppermute | solution.py:24
  24.7 5.6 %collective-permute-done.7.refs_5_ = bf16[32,1536]{1,0:T(8,128)(2,1)S(1)} collective-permute-done((bf16[32,1536]{1,0:T(8,128)(2,1)S(1)}, bf16[32,1536]{1,0:T(8,128)(2,1)S(1)}, u32[]{:S(2)}, u32[]{:S(2)}) %collective-permute-start.7) | collective-permute-done | bytes 98336 | tf_op jit(solution)/shard_map/ppermute | solution.py:24
  30.2 1.6 %collective-permute-done.8.refs_6_ = bf16[32,1536]{1,0:T(8,128)(2,1)S(1)} collective-permute-done((bf16[32,1536]{1,0:T(8,128)(2,1)S(1)}, bf16[32,1536]{1,0:T(8,128)(2,1)S(1)}, u32[]{:S(2)}, u32[]{:S(2)}) %collective-permute-start.8) | collective-permute-done | bytes 98336 | tf_op jit(solution)/shard_map/ppermute | solution.py:24
  31.8 3.2 %shard_map.68 = (bf16[8,2,16,1536]{3,2,1,0:T(8,128)(2,1)}, f32[16,896]{1,0:T(8,128)S(1)}, bf16[16,896]{1,0:T(8,128)(2,1)S(1)}) custom-call(s32[1,1]{1,0:T(1,128)S(6)} %select_n.7.code_ref, bf16[2,768,768]{2,1,0:T(8,128)(2,1)S(1)} %shard_map.67.own_ref, bf16[2,768,768]{2,1,0:T(8,128)(2,1)S(1)} %collective-permute-done.1._.sibling_ref, ...), custom_call_target="tpu_custom_call" | custom-call | tf_op jit(solution)/shard_map/pallas_call | solution.py:208
  35.2 4.7 %all-to-all-start = ((bf16[8,32,1536]{2,1,0:T(8,128)(2,1)}), bf16[8,32,1536]{2,1,0:T(8,128)(2,1)S(1)}, u32[]{:S(2)}, u32[]{:S(2)}) async-start(bf16[8,32,1536]{2,1,0:T(8,128)(2,1)} %bitcast.5), calls=%async_computation | async-start | bytes 1572864 | tf_op jit(solution)/shard_map/all_to_all | solution.py:222
  40.3 1.2 %collective-permute-done.10 = bf16[16,896]{1,0:T(8,128)(2,1)S(1)} collective-permute-done((bf16[16,896]{1,0:T(8,128)(2,1)S(1)}, bf16[16,896]{1,0:T(8,128)(2,1)S(1)}, u32[]{:S(2)}, u32[]{:S(2)}) %collective-permute-start.10) | collective-permute-done | bytes 28704 | tf_op jit(solution)/shard_map/ppermute | solution.py:24
  41.5 1.8 %collective-permute-start.11 = (bf16[12,896]{1,0:T(8,128)(2,1)S(1)}, bf16[12,896]{1,0:T(8,128)(2,1)S(1)}, u32[]{:S(2)}, u32[]{:S(2)}) collective-permute-start(bf16[12,896]{1,0:T(8,128)(2,1)S(1)} %pad_maximum_fusion), channel_id=1, source_target_pairs={{0,2},{1,3},{2,0},{3,1},{4,6},{5,7},{6,4},{7,5},{8,10},{9,11},{10,... | collective-permute-start | bytes 64520 | tf_op jit(solution)/shard_map/ppermute | solution.py:24
  43.3 4.3 %collective-permute-done.11 = bf16[12,896]{1,0:T(8,128)(2,1)S(1)} collective-permute-done((bf16[12,896]{1,0:T(8,128)(2,1)S(1)}, bf16[12,896]{1,0:T(8,128)(2,1)S(1)}, u32[]{:S(2)}, u32[]{:S(2)}) %collective-permute-start.11) | collective-permute-done | bytes 21536 | tf_op jit(solution)/shard_map/ppermute | solution.py:24
  47.7 1.2 %collective-permute-start.12 = (bf16[8,896]{1,0:T(8,128)(2,1)S(1)}, bf16[8,896]{1,0:T(8,128)(2,1)S(1)}, u32[]{:S(2)}, u32[]{:S(2)}) collective-permute-start(bf16[8,896]{1,0:T(8,128)(2,1)S(1)} %pad_maximum_fusion.2), channel_id=1, source_target_pairs={{0,4},{1,5},{2,6},{3,7},{4,0},{5,1},{6,2},{7,3},{8,12},{9,13},{10,... | collective-permute-start | bytes 43016 | tf_op jit(solution)/shard_map/ppermute | solution.py:24
  48.9 3.4 %collective-permute-done.12.arrived_ref = bf16[8,896]{1,0:T(8,128)(2,1)S(1)} collective-permute-done((bf16[8,896]{1,0:T(8,128)(2,1)S(1)}, bf16[8,896]{1,0:T(8,128)(2,1)S(1)}, u32[]{:S(2)}, u32[]{:S(2)}) %collective-permute-start.12) | collective-permute-done | bytes 14368 | tf_op jit(solution)/shard_map/ppermute | solution.py:24
  52.3 0.9 %shard_map.69.above_ref = f32[4,384]{1,0:T(4,128)S(1)} custom-call(f32[8,896]{1,0:T(8,128)S(1)} %pad_maximum_fusion.1.keep_ref, bf16[8,896]{1,0:T(8,128)(2,1)S(1)} %collective-permute-done.12.arrived_ref, bf16[2,2,384,384]{3,2,1,0:T(8,128)(2,1)S(1)} %copy-done.1), custom_call_target="tpu_custom_call" | custom-call | flops 1 | bytes 1 | tf_op jit(solution)/shard_map/pallas_call | solution.py:208
  53.2 6.2 %all-to-all-done = bf16[8,32,1536]{2,1,0:T(8,128)(2,1)S(1)} async-done(((bf16[8,32,1536]{2,1,0:T(8,128)(2,1)}), bf16[8,32,1536]{2,1,0:T(8,128)(2,1)S(1)}, u32[]{:S(2)}, u32[]{:S(2)}) %all-to-all-start) | async-done | bytes 786464 | tf_op jit(solution)/shard_map/all_to_all | solution.py:222
  59.4 1.0 %shard_map.70 = bf16[52,2,1536]{2,1,0:T(2,128)(2,1)} custom-call(bf16[104,256]{1,0:T(8,128)(2,1)S(1)} %get-tuple-element.18.pick_ref, f32[4,384]{1,0:T(4,128)S(1)} %shard_map.69.above_ref, bf16[256,1536]{1,0:T(8,128)(2,1)S(1)} %bitcast.8), custom_call_target="tpu_custom_call" | custom-call | tf_op jit(solution)/shard_map/pallas_call | solution.py:208
  (32 shorter events, 1.8 us)
Async XLA Ops:
  0.0 8.8 %collective-permute-start.1 = (bf16[2,768,768]{2,1,0:T(8,128)(2,1)}, bf16[2,768,768]{2,1,0:T(8,128)(2,1)S(1)}, u32[]{:S(2)}, u32[]{:S(2)}) collective-permute-start(bf16[2,768,768]{2,1,0:T(8,128)(2,1)} %bitcast.9), channel_id=1, source_target_pairs={{0,1},{1,0},{2,3},{3,2},{4,5},{5,4},{6,7},{7,6},{8,9},{9,8},{10,11... | collective-permute-start | bytes 7077896 | tf_op jit(solution)/shard_map/ppermute | solution.py:24
  2.1 6.7 %collective-permute-start = (f32[52,2,128]{2,1,0:T(2,128)}, f32[52,2,128]{2,1,0:T(2,128)S(1)}, u32[]{:S(2)}, u32[]{:S(2)}) collective-permute-start(f32[52,2,128]{2,1,0:T(2,128)} %shard_map.65), channel_id=1, source_target_pairs={{0,16},{1,17},{2,18},{3,19},{4,20},{5,21},{6,22},{7,23},{8,24},{9,... | collective-permute-start | bytes 159752 | tf_op jit(solution)/shard_map/ppermute | solution.py:19
  7.6 14.5 %copy-start = (bf16[1,2,768,768]{3,2,1,0:T(8,128)(2,1)S(1)}, bf16[1,2,768,768]{3,2,1,0:T(8,128)(2,1)}, u32[]{:S(2)}) copy-start(bf16[1,2,768,768]{3,2,1,0:T(8,128)(2,1)} %param.10) | copy-start | bytes 7077892
  7.6 0.8 %copy-start.2 = (s32[1,52,1]{1,2,0:T(1,128)S(1)}, s32[1,52,1]{1,2,0:T(1,128)}, u32[]{:S(2)}) copy-start(s32[1,52,1]{1,2,0:T(1,128)} %param.8) | copy-start | bytes 628
  9.1 8.4 %collective-permute-start.2 = (bf16[32,1536]{1,0:T(8,128)(2,1)S(1)}, bf16[32,1536]{1,0:T(8,128)(2,1)S(1)}, u32[]{:S(2)}, u32[]{:S(2)}) collective-permute-start(bf16[32,1536]{1,0:T(8,128)(2,1)S(1)} %get-tuple-element.21), channel_id=1, source_target_pairs={{0,14},{1,15},{2,12},{3,13},{4,10},{5,11},{6,8},{7,9},{8,6},{9,7},... | collective-permute-start | bytes 294920 | tf_op jit(solution)/shard_map/ppermute | solution.py:24
  13.8 6.6 %collective-permute-start.3 = (bf16[32,1536]{1,0:T(8,128)(2,1)S(1)}, bf16[32,1536]{1,0:T(8,128)(2,1)S(1)}, u32[]{:S(2)}, u32[]{:S(2)}) collective-permute-start(bf16[32,1536]{1,0:T(8,128)(2,1)S(1)} %get-tuple-element.22), channel_id=1, source_target_pairs={{0,2},{1,3},{2,0},{3,1},{4,6},{5,7},{6,4},{7,5},{8,10},{9,11},{10,... | collective-permute-start | bytes 294920 | tf_op jit(solution)/shard_map/ppermute | solution.py:24
  14.3 8.0 %collective-permute-start.4 = (bf16[32,1536]{1,0:T(8,128)(2,1)S(1)}, bf16[32,1536]{1,0:T(8,128)(2,1)S(1)}, u32[]{:S(2)}, u32[]{:S(2)}) collective-permute-start(bf16[32,1536]{1,0:T(8,128)(2,1)S(1)} %get-tuple-element.23), channel_id=1, source_target_pairs={{0,4},{1,5},{2,6},{3,7},{4,0},{5,1},{6,2},{7,3},{8,12},{9,13},{10,... | collective-permute-start | bytes 294920 | tf_op jit(solution)/shard_map/ppermute | solution.py:24
  14.3 9.1 %collective-permute-start.5 = (bf16[32,1536]{1,0:T(8,128)(2,1)S(1)}, bf16[32,1536]{1,0:T(8,128)(2,1)S(1)}, u32[]{:S(2)}, u32[]{:S(2)}) collective-permute-start(bf16[32,1536]{1,0:T(8,128)(2,1)S(1)} %get-tuple-element.24), channel_id=1, source_target_pairs={{0,6},{1,7},{2,4},{3,5},{4,2},{5,3},{6,0},{7,1},{8,14},{9,15},{10,... | collective-permute-start | bytes 294920 | tf_op jit(solution)/shard_map/ppermute | solution.py:24
  17.2 7.4 %collective-permute-start.6 = (bf16[32,1536]{1,0:T(8,128)(2,1)S(1)}, bf16[32,1536]{1,0:T(8,128)(2,1)S(1)}, u32[]{:S(2)}, u32[]{:S(2)}) collective-permute-start(bf16[32,1536]{1,0:T(8,128)(2,1)S(1)} %get-tuple-element.25), channel_id=1, source_target_pairs={{0,12},{1,13},{2,14},{3,15},{4,8},{5,9},{6,10},{7,11},{8,4},{9,5},... | collective-permute-start | bytes 294920 | tf_op jit(solution)/shard_map/ppermute | solution.py:24
  17.6 12.7 %collective-permute-start.7 = (bf16[32,1536]{1,0:T(8,128)(2,1)S(1)}, bf16[32,1536]{1,0:T(8,128)(2,1)S(1)}, u32[]{:S(2)}, u32[]{:S(2)}) collective-permute-start(bf16[32,1536]{1,0:T(8,128)(2,1)S(1)} %get-tuple-element.26), channel_id=1, source_target_pairs={{0,10},{1,11},{2,8},{3,9},{4,14},{5,15},{6,12},{7,13},{8,2},{9,3},... | collective-permute-start | bytes 294920 | tf_op jit(solution)/shard_map/ppermute | solution.py:24
  20.4 11.5 %collective-permute-start.8 = (bf16[32,1536]{1,0:T(8,128)(2,1)S(1)}, bf16[32,1536]{1,0:T(8,128)(2,1)S(1)}, u32[]{:S(2)}, u32[]{:S(2)}) collective-permute-start(bf16[32,1536]{1,0:T(8,128)(2,1)S(1)} %get-tuple-element.27), channel_id=1, source_target_pairs={{0,8},{1,9},{2,10},{3,11},{4,12},{5,13},{6,14},{7,15},{8,0},{9,1},... | collective-permute-start | bytes 294920 | tf_op jit(solution)/shard_map/ppermute | solution.py:24
  35.1 17.2 %copy-start.1 = (bf16[2,2,384,384]{3,2,1,0:T(8,128)(2,1)S(1)}, bf16[2,2,384,384]{3,2,1,0:T(8,128)(2,1)}, u32[]{:S(2)}) copy-start(bf16[2,2,384,384]{3,2,1,0:T(8,128)(2,1)} %factors_ref.1) | copy-start | bytes 3538948
  35.1 5.1 %collective-permute-start.9 = (bf16[16,896]{1,0:T(8,128)(2,1)S(1)}, bf16[16,896]{1,0:T(8,128)(2,1)S(1)}, u32[]{:S(2)}, u32[]{:S(2)}) collective-permute-start(bf16[16,896]{1,0:T(8,128)(2,1)S(1)} %get-tuple-element.29), channel_id=1, source_target_pairs={{0,8},{1,9},{2,10},{3,11},{4,12},{5,13},{6,14},{7,15},{8,0},{9,1},... | collective-permute-start | bytes 86024 | tf_op jit(solution)/shard_map/ppermute | solution.py:24
  35.2 24.2 %all-to-all-start = ((bf16[8,32,1536]{2,1,0:T(8,128)(2,1)}), bf16[8,32,1536]{2,1,0:T(8,128)(2,1)S(1)}, u32[]{:S(2)}, u32[]{:S(2)}) async-start(bf16[8,32,1536]{2,1,0:T(8,128)(2,1)} %bitcast.5), calls=%async_computation | async-start | bytes 1572864 | tf_op jit(solution)/shard_map/all_to_all | solution.py:222
  40.2 1.3 %collective-permute-start.10 = (bf16[16,896]{1,0:T(8,128)(2,1)S(1)}, bf16[16,896]{1,0:T(8,128)(2,1)S(1)}, u32[]{:S(2)}, u32[]{:S(2)}) collective-permute-start(bf16[16,896]{1,0:T(8,128)(2,1)S(1)} %fusion), channel_id=1, source_target_pairs={{0,1},{1,0},{2,3},{3,2},{4,5},{5,4},{6,7},{7,6},{8,9},{9,8},{10,11... | collective-permute-start | bytes 86024 | tf_op jit(solution)/shard_map/ppermute | solution.py:24
  41.5 6.1 %collective-permute-start.11 = (bf16[12,896]{1,0:T(8,128)(2,1)S(1)}, bf16[12,896]{1,0:T(8,128)(2,1)S(1)}, u32[]{:S(2)}, u32[]{:S(2)}) collective-permute-start(bf16[12,896]{1,0:T(8,128)(2,1)S(1)} %pad_maximum_fusion), channel_id=1, source_target_pairs={{0,2},{1,3},{2,0},{3,1},{4,6},{5,7},{6,4},{7,5},{8,10},{9,11},{10,... | collective-permute-start | bytes 64520 | tf_op jit(solution)/shard_map/ppermute | solution.py:24
  47.7 4.6 %collective-permute-start.12 = (bf16[8,896]{1,0:T(8,128)(2,1)S(1)}, bf16[8,896]{1,0:T(8,128)(2,1)S(1)}, u32[]{:S(2)}, u32[]{:S(2)}) collective-permute-start(bf16[8,896]{1,0:T(8,128)(2,1)S(1)} %pad_maximum_fusion.2), channel_id=1, source_target_pairs={{0,4},{1,5},{2,6},{3,7},{4,0},{5,1},{6,2},{7,3},{8,12},{9,13},{10,... | collective-permute-start | bytes 43016 | tf_op jit(solution)/shard_map/ppermute | solution.py:24

commit v6 on v5

--- a/solution.py
+++ b/solution.py
@@ -97,29 +97,32 @@
         out_ref[...] = send[at * size : (at + 1) * size]
 
 
-def stage_kernel(from_ref, _, to_ref):
-    to_ref[...] = from_ref[...]
-
-
-def leaf_kernel(shots, sep_n, order, code_ref, own_ref, sibling_ref, *refs):
-    blocks, (out_ref, keep_ref, send_ref) = dict(zip(order, refs[:-8])), refs[-8:-5]
-    factor_ref, rows_ref, solved_ref, load_sems, sems = refs[-5:]
+def stage_kernel(own_ref, sibling_ref, _, *to_refs):
+    to_refs[0][...] = own_ref[...]
+    to_refs[1][...] = sibling_ref[...]
+
+
+def leaf_kernel(shots, sep_n, group, pairs, own_ref, sibling_ref, *refs):
+    blocks, refs = refs[: len(group)], refs[len(group) :]
+    if len(refs) == 5:
+        code_ref = None
+        out_ref, sums_ref, rows_ref, solved_ref, sems = refs
+        count = sums_ref.shape[0]
+    else:
+        code_ref, before_ref, _, out_ref, keep_ref, send_ref, rows_ref, solved_ref, sems = refs
+        count = 2 * keep_ref.shape[0]
     leaf_n = own_ref.shape[1]
-    loads = []
-    for at in range(4):
-        rows = (at // 2, pl.ds(at % 2 * (leaf_n // 2), leaf_n // 2))
-        loads.append(pltpu.make_async_copy(sibling_ref.at[rows], factor_ref.at[rows], load_sems.at[at]))
-        loads[at].start()
-    pairs, _, size, _ = solved_ref.shape
+    members, _, size, _ = solved_ref.shape
     capacity = size // shots
-    half = pairs * size
-    count = keep_ref.shape[0]
+    half = members * size
     own_pair = lax.axis_index("leaf") // 2
     bits = pairs.bit_length() - 1
-    row = lax.broadcasted_iota(jnp.int32, (2 * count, half), 0)
-    place = lax.broadcasted_iota(jnp.int32, (2 * count, half), 1)
-    lead = lax.broadcasted_iota(jnp.int32, (2 * count, LANES), 0)
-    distance = place // size
+    row = lax.broadcasted_iota(jnp.int32, (count, half), 0)
+    place = lax.broadcasted_iota(jnp.int32, (count, half), 1)
+    lead = lax.broadcasted_iota(jnp.int32, (count, LANES), 0)
+    distance = jnp.zeros((count, half), jnp.int32)
+    for at, block in enumerate(group):
+        distance = jnp.where(place // size == at, block, distance)
     member, here, first = row < 0, lead < 0, 0
     for other in range(2):
         for level in range(bits + 1):
@@ -131,11 +134,10 @@
                 here |= (lead >= first) & (lead < first + shots)
             first += nodes * shots
     member = one_hot(member & (place % size // capacity == row % shots))
-    codes = jnp.where(here, code_ref[0, 0].astype(F32), 0.0)
 
     copies, sums = [], [0.0, 0.0]
     for entry in range(2):
-        for at in range(pairs):
+        for at in range(members):
             real = blocks[at][entry * size : (entry + 1) * size, :leaf_n]
             imag = blocks[at][entry * size : (entry + 1) * size, leaf_n:]
             first = at * size
@@ -143,27 +145,33 @@
             rows_ref[first : first + size, leaf_n:] = -imag
             rows_ref[half + first : half + first + size, :leaf_n] = imag
             rows_ref[half + first : half + first + size, leaf_n:] = real
-        if entry:
-            for load in loads:
-                load.wait()
-        factor = (factor_ref if entry else own_ref)[...].reshape(2 * leaf_n, leaf_n)
+        factor = (sibling_ref if entry else own_ref)[...].reshape(2 * leaf_n, leaf_n)
+        both = dot(rows_ref[...], factor).astype(BF16)
         for part in range(2):
-            solved = dot(rows_ref[part * half : (part + 1) * half], factor).astype(BF16)
+            solved = both[part * half : (part + 1) * half]
             columns = pl.ds(part * leaf_n, leaf_n)
-            for at in range(pairs):
+            for at in range(members):
                 solved_ref[at, entry, :, columns] = solved[at * size : (at + 1) * size]
             sums[part] += dot(member, solved[:, :sep_n])
-        for at in range(pairs):
+        for at, block in enumerate(group):
             copies.append(
                 pltpu.make_async_copy(
-                    solved_ref.at[at, entry], out_ref.at[own_pair ^ at, entry], sems.at[entry * pairs + at]
+                    solved_ref.at[at, entry], out_ref.at[own_pair ^ block, entry], sems.at[entry * members + at]
                 )
             )
             copies[-1].start()
-    for ref, rows in ((keep_ref, slice(0, count)), (send_ref, slice(count, 2 * count))):
-        for part in range(2):
-            ref[:, part * sep_n : (part + 1) * sep_n] = sums[part][rows].astype(ref.dtype)
-        ref[:, 2 * sep_n :] = codes[rows].astype(ref.dtype)
+    for part in range(2):
+        columns = slice(part * sep_n, (part + 1) * sep_n)
+        if code_ref is None:
+            sums_ref[:, columns] = sums[part]
+        else:
+            total = sums[part] + before_ref[:, columns]
+            keep_ref[:, columns] = total[: count // 2]
+            send_ref[:, columns] = total[count // 2 :].astype(BF16)
+    if code_ref is not None:
+        codes = jnp.where(here, code_ref[0, 0].astype(F32), 0.0)
+        keep_ref[:, 2 * sep_n :] = codes[: count // 2]
+        send_ref[:, 2 * sep_n :] = codes[count // 2 :].astype(BF16)
     for copy in copies:
         copy.wait()
 
@@ -294,23 +302,34 @@
     far, near = list(range(pairs // 2, pairs)), list(range(1, pairs // 2))
     order = far[-1:] + near + far[-2::-1] + [0]
     arrived = {at: exchange(sent[at], 2 * at) if at else sent[at] for at in order}
-    own = call(stage_kernel, jax.ShapeDtypeStruct(own.shape, BF16), (own, sent[0]), hbm=(1,))
+    own, sibling = call(stage_kernel, [jax.ShapeDtypeStruct(own.shape, BF16)] * 2, (own, sibling, sent[0]), hbm=(2,))
     nodes = jax.ShapeDtypeStruct((pairs * shots, 2 * sep_n + LANES), F32)
     halves = (pairs, 2, size // 2, width2)
+    first, last = order[: pairs // 2] + [0], order[pairs // 2 : -1]
+
+    def scratch(group):
+        return [
+            VMEM((len(group) * size, width2), BF16),
+            VMEM((len(group),) + halves[1:], BF16),
+            pltpu.SemaphoreType.DMA((2 * len(group),)),
+        ]
+
+    solved, sums = call(
+        functools.partial(leaf_kernel, shots, sep_n, first, pairs),
+        [jax.ShapeDtypeStruct(halves, BF16), jax.ShapeDtypeStruct((2 * pairs * shots, 2 * sep_n), F32)],
+        (own, sibling, *(arrived[at] for at in first)),
+        hbm_out=(0,),
+        scratch=scratch(first),
+    )
     solved, keep, send = call(
-        functools.partial(leaf_kernel, shots, sep_n, order),
+        functools.partial(leaf_kernel, shots, sep_n, last, pairs),
         [jax.ShapeDtypeStruct(halves, BF16), nodes, jax.ShapeDtypeStruct(nodes.shape, BF16)],
-        (sep_code % sep_lib, own, sibling, *(arrived[at] for at in order)),
-        smem=(0,),
-        hbm=(2,),
+        (own, sibling, *(arrived[at] for at in last), sep_code % sep_lib, sums, solved),
+        smem=(2 + len(last),),
+        hbm=(4 + len(last),),
         hbm_out=(0,),
-        scratch=[
-            VMEM(own.shape, BF16),
-            VMEM((slots, width2), BF16),
-            VMEM(halves, BF16),
-            pltpu.SemaphoreType.DMA((4,)),
-            pltpu.SemaphoreType.DMA((2 * pairs,)),
-        ],
+        aliases={4 + len(last): 0},
+        scratch=scratch(last),
     )
     back = to_pairs(solved.reshape(pairs, size, width2)).reshape(slots, width2)
     keep, arrived = path_sums(keep, send, shots, levels)

time: 60.7 us -> 56.9 us (0.937)
  waiting for transfers between devices: 25 us -> 16.2 us
  starting transfers between devices: 24.8 us -> 29.6 us
    ppermute x12, waiting for transfers between devices: 18.9 us -> 10.8 us  [exchange(): return lax.ppermute(value, 'leaf', pairs)]
    ppermute x12, starting transfers between devices: 15.7 us -> 20.7 us  [exchange(): return lax.ppermute(value, 'leaf', pairs)]
    all_to_all x1, waiting for transfers between devices: 6.16 us -> 5.38 us  [to_pairs(): lax.all_to_all(value, 'leaf', 0, 0, tiled=True, axis_index_groups=groups)]
    pallas_call x7 -> x8, Pallas kernels: 7.6 us -> 7.85 us  [call(): pl.pallas_call(kernel, out_shape=out_shape, in_specs=[pl.BlockSpec(memory...]
  transfers between devices with their start and end apart: 14 -> 14, of which waited for: 10 -> 8; matrix products, arithmetic and copies ran while one was open for 2% -> 2% of each run, Pallas kernels for 5% -> 9%
where the time goes in v6:
time: 56.9 us; the launch traced here: 56.6 us
  starting transfers between devices  29.6 us (52%)
  waiting for transfers between devices  16.2 us (28%)
  Pallas kernels  7.85 us (14%)
  local copies, waits for them, and re-layouts  1.96 us (3%)
  between operations  0.88 us (2%)
    ppermute x12, starting transfers between devices, exchange(): return lax.ppermute(value, 'leaf', pairs)  20.7 us
    ppermute x12, waiting for transfers between devices, exchange(): return lax.ppermute(value, 'leaf', pairs)  10.8 us
    pallas_call x8, Pallas kernels, call(): pl.pallas_call(kernel, out_shape=out_shape, in_specs=[pl.BlockSpec(memory...  7.85 us
    all_to_all x1, waiting for transfers between devices, to_pairs(): lax.all_to_all(value, 'leaf', 0, 0, tiled=True, axis_index_groups=groups)  5.38 us
    all_to_all x1, starting transfers between devices, to_pairs(): lax.all_to_all(value, 'leaf', 0, 0, tiled=True, axis_index_groups=groups)  4.46 us
    ppermute x1, starting transfers between devices, from_behind(): return lax.ppermute(value, axis, [(at, at + 1) for at in range(count - 1)])  4.4 us
  transfers between devices with their start and end apart: 14, of which 8 were waited for; matrix products, arithmetic and copies ran while one was open for 2% of the time, Pallas kernels for 9%

profile of v6, /device:TPU:0, one launch (start us, length us, event | category | flops | bytes accessed | tf_op | source)
XLA Modules:
  0.0 56.6 jit_solution(16019605612466226032)
XLA Ops:
  0.0 0.5 collective-permute-start
  0.5 1.6 %shard_map.65 = f32[52,2,128]{2,1,0:T(2,128)} custom-call(bf16[52,2,1536]{2,1,0:T(2,128)(2,1)} %bitcast.13, f32[52,1,128]{2,1,0:T(1,128)} %bitcast.14), custom_call_target="tpu_custom_call" | custom-call | tf_op jit(solution)/shard_map/pallas_call | solution.py:216
  2.1 4.4 %collective-permute-start.1 = (f32[52,2,128]{2,1,0:T(2,128)}, f32[52,2,128]{2,1,0:T(2,128)S(1)}, u32[]{:S(2)}, u32[]{:S(2)}) collective-permute-start(f32[52,2,128]{2,1,0:T(2,128)} %shard_map.65), channel_id=1, source_target_pairs={{0,16},{1,17},{2,18},{3,19},{4,20},{5,21},{6,22},{7,23},{8,24},{9,... | collective-permute-start | bytes 159752 | tf_op jit(solution)/shard_map/ppermute | solution.py:19
  6.5 1.1 %reshape_squeeze.7.rows_ref = bf16[104,1536]{1,0:T(8,128)(2,1)S(1)} reshape(bf16[1,52,2,1536]{3,2,1,0:T(2,128)(2,1)} %param.6) | data formatting | bytes 638976 | tf_op jit(solution)/shard_map/reshape;squeeze | solution.py:298
  7.6 0.8 %copy-done.2 = s32[1,52,1]{1,2,0:T(1,128)S(1)} copy-done((s32[1,52,1]{1,2,0:T(1,128)S(1)}, s32[1,52,1]{1,2,0:T(1,128)}, u32[]{:S(2)}) %copy-start.2) | copy-done | bytes 232
  8.8 0.4 shard_map.66
  9.1 4.6 %collective-permute-start.5 = (bf16[32,1536]{1,0:T(8,128)(2,1)S(1)}, bf16[32,1536]{1,0:T(8,128)(2,1)S(1)}, u32[]{:S(2)}, u32[]{:S(2)}) collective-permute-start(bf16[32,1536]{1,0:T(8,128)(2,1)S(1)} %get-tuple-element.30), channel_id=1, source_target_pairs={{0,14},{1,15},{2,12},{3,13},{4,10},{5,11},{6,8},{7,9},{8,6},{9,7},... | collective-permute-start | bytes 294920 | tf_op jit(solution)/shard_map/ppermute | solution.py:24
  13.8 0.5 collective-permute-start.6
  14.5 3.0 %collective-permute-start.8 = (bf16[32,1536]{1,0:T(8,128)(2,1)S(1)}, bf16[32,1536]{1,0:T(8,128)(2,1)S(1)}, u32[]{:S(2)}, u32[]{:S(2)}) collective-permute-start(bf16[32,1536]{1,0:T(8,128)(2,1)S(1)} %get-tuple-element.33), channel_id=1, source_target_pairs={{0,6},{1,7},{2,4},{3,5},{4,2},{5,3},{6,0},{7,1},{8,14},{9,15},{10,... | collective-permute-start | bytes 294920 | tf_op jit(solution)/shard_map/ppermute | solution.py:24
  17.5 6.1 %collective-permute-start.3 = (bf16[32,1536]{1,0:T(8,128)(2,1)S(1)}, bf16[32,1536]{1,0:T(8,128)(2,1)S(1)}, u32[]{:S(2)}, u32[]{:S(2)}) collective-permute-start(bf16[32,1536]{1,0:T(8,128)(2,1)S(1)} %get-tuple-element.28), channel_id=1, source_target_pairs={{0,10},{1,11},{2,8},{3,9},{4,14},{5,15},{6,12},{7,13},{8,2},{9,3},... | collective-permute-start | bytes 294920 | tf_op jit(solution)/shard_map/ppermute | solution.py:24
  24.5 2.1 %collective-permute-done.8.refs_3_ = bf16[32,1536]{1,0:T(8,128)(2,1)S(1)} collective-permute-done((bf16[32,1536]{1,0:T(8,128)(2,1)S(1)}, bf16[32,1536]{1,0:T(8,128)(2,1)S(1)}, u32[]{:S(2)}, u32[]{:S(2)}) %collective-permute-start.8) | collective-permute-done | bytes 98336 | tf_op jit(solution)/shard_map/ppermute | solution.py:24
  26.6 1.7 %shard_map.68 = (bf16[8,2,16,1536]{3,2,1,0:T(8,128)(2,1)}, f32[32,768]{1,0:T(8,128)S(1)}) custom-call(bf16[2,768,768]{2,1,0:T(8,128)(2,1)S(1)} %get-tuple-element.25.own_ref, bf16[2,768,768]{2,1,0:T(8,128)(2,1)S(1)} %get-tuple-element.26.sibling_ref, bf16[32,1536]{1,0:T(8,128)(2,1)S(1)} %collective-permute-done.5.refs_0_, ...), custom_call_target="tpu_custom_call" | custom-call | tf_op jit(solution)/shard_map/pallas_call | solution.py:216
  28.3 1.7 %collective-permute-done.3.refs_1_ = bf16[32,1536]{1,0:T(8,128)(2,1)S(1)} collective-permute-done((bf16[32,1536]{1,0:T(8,128)(2,1)S(1)}, bf16[32,1536]{1,0:T(8,128)(2,1)S(1)}, u32[]{:S(2)}, u32[]{:S(2)}) %collective-permute-start.3) | collective-permute-done | bytes 98336 | tf_op jit(solution)/shard_map/ppermute | solution.py:24
  30.0 0.8 %collective-permute-done.4.refs_2_ = bf16[32,1536]{1,0:T(8,128)(2,1)S(1)} collective-permute-done((bf16[32,1536]{1,0:T(8,128)(2,1)S(1)}, bf16[32,1536]{1,0:T(8,128)(2,1)S(1)}, u32[]{:S(2)}, u32[]{:S(2)}) %collective-permute-start.4) | collective-permute-done | bytes 98336 | tf_op jit(solution)/shard_map/ppermute | solution.py:24
  30.8 1.6 %shard_map.69 = (bf16[8,2,16,1536]{3,2,1,0:T(8,128)(2,1)}, f32[16,896]{1,0:T(8,128)S(1)}, bf16[16,896]{1,0:T(8,128)(2,1)S(1)}) custom-call(bf16[2,768,768]{2,1,0:T(8,128)(2,1)S(1)} %get-tuple-element.25.own_ref, bf16[2,768,768]{2,1,0:T(8,128)(2,1)S(1)} %get-tuple-element.26.sibling_ref, ...), custom_call_target="tpu_custom_call", output_to_operand_aliasing={{0}: (7, {})} | custom-call | tf_op jit(solution)/shard_map/pallas_call | solution.py:216
  32.5 4.5 %all-to-all-start = ((bf16[8,32,1536]{2,1,0:T(8,128)(2,1)}), bf16[8,32,1536]{2,1,0:T(8,128)(2,1)S(1)}, u32[]{:S(2)}, u32[]{:S(2)}) async-start(bf16[8,32,1536]{2,1,0:T(8,128)(2,1)} %bitcast.5), calls=%async_computation | async-start | bytes 1572864 | tf_op jit(solution)/shard_map/all_to_all | solution.py:230
  37.4 1.2 %collective-permute-done.10 = bf16[16,896]{1,0:T(8,128)(2,1)S(1)} collective-permute-done((bf16[16,896]{1,0:T(8,128)(2,1)S(1)}, bf16[16,896]{1,0:T(8,128)(2,1)S(1)}, u32[]{:S(2)}, u32[]{:S(2)}) %collective-permute-start.10) | collective-permute-done | bytes 28704 | tf_op jit(solution)/shard_map/ppermute | solution.py:24
  38.6 1.8 %collective-permute-start.11 = (bf16[12,896]{1,0:T(8,128)(2,1)S(1)}, bf16[12,896]{1,0:T(8,128)(2,1)S(1)}, u32[]{:S(2)}, u32[]{:S(2)}) collective-permute-start(bf16[12,896]{1,0:T(8,128)(2,1)S(1)} %pad_maximum_fusion), channel_id=1, source_target_pairs={{0,2},{1,3},{2,0},{3,1},{4,6},{5,7},{6,4},{7,5},{8,10},{9,11},{10,... | collective-permute-start | bytes 64520 | tf_op jit(solution)/shard_map/ppermute | solution.py:24
  40.5 3.0 %collective-permute-done.11 = bf16[12,896]{1,0:T(8,128)(2,1)S(1)} collective-permute-done((bf16[12,896]{1,0:T(8,128)(2,1)S(1)}, bf16[12,896]{1,0:T(8,128)(2,1)S(1)}, u32[]{:S(2)}, u32[]{:S(2)}) %collective-permute-start.11) | collective-permute-done | bytes 21536 | tf_op jit(solution)/shard_map/ppermute | solution.py:24
  43.5 3.9 %collective-permute-start.12 = (bf16[8,896]{1,0:T(8,128)(2,1)S(1)}, bf16[8,896]{1,0:T(8,128)(2,1)S(1)}, u32[]{:S(2)}, u32[]{:S(2)}) collective-permute-start(bf16[8,896]{1,0:T(8,128)(2,1)S(1)} %pad_maximum_fusion.2), channel_id=1, source_target_pairs={{0,4},{1,5},{2,6},{3,7},{4,0},{5,1},{6,2},{7,3},{8,12},{9,13},{10,... | collective-permute-start | bytes 43016 | tf_op jit(solution)/shard_map/ppermute | solution.py:24
  47.5 1.8 %collective-permute-done.12.arrived_ref = bf16[8,896]{1,0:T(8,128)(2,1)S(1)} collective-permute-done((bf16[8,896]{1,0:T(8,128)(2,1)S(1)}, bf16[8,896]{1,0:T(8,128)(2,1)S(1)}, u32[]{:S(2)}, u32[]{:S(2)}) %collective-permute-start.12) | collective-permute-done | bytes 14368 | tf_op jit(solution)/shard_map/ppermute | solution.py:24
  49.3 0.9 %shard_map.70.above_ref = f32[4,384]{1,0:T(4,128)S(1)} custom-call(f32[8,896]{1,0:T(8,128)S(1)} %pad_maximum_fusion.1.keep_ref, bf16[8,896]{1,0:T(8,128)(2,1)S(1)} %collective-permute-done.12.arrived_ref, bf16[2,2,384,384]{3,2,1,0:T(8,128)(2,1)S(1)} %copy-done.1), custom_call_target="tpu_custom_call" | custom-call | flops 1 | bytes 1 | tf_op jit(solution)/shard_map/pallas_call | solution.py:216
  50.2 5.4 %all-to-all-done = bf16[8,32,1536]{2,1,0:T(8,128)(2,1)S(1)} async-done(((bf16[8,32,1536]{2,1,0:T(8,128)(2,1)}), bf16[8,32,1536]{2,1,0:T(8,128)(2,1)S(1)}, u32[]{:S(2)}, u32[]{:S(2)}) %all-to-all-start) | async-done | bytes 786464 | tf_op jit(solution)/shard_map/all_to_all | solution.py:230
  55.6 1.0 %shard_map.71 = bf16[52,2,1536]{2,1,0:T(2,128)(2,1)} custom-call(bf16[104,256]{1,0:T(8,128)(2,1)S(1)} %get-tuple-element.22.pick_ref, f32[4,384]{1,0:T(4,128)S(1)} %shard_map.70.above_ref, bf16[256,1536]{1,0:T(8,128)(2,1)S(1)} %bitcast.8), custom_call_target="tpu_custom_call" | custom-call | tf_op jit(solution)/shard_map/pallas_call | solution.py:216
  (33 shorter events, 1.5 us)
Async XLA Ops:
  0.0 8.8 %collective-permute-start = (bf16[2,768,768]{2,1,0:T(8,128)(2,1)}, bf16[2,768,768]{2,1,0:T(8,128)(2,1)S(1)}, u32[]{:S(2)}, u32[]{:S(2)}) collective-permute-start(bf16[2,768,768]{2,1,0:T(8,128)(2,1)} %bitcast.9), channel_id=1, source_target_pairs={{0,1},{1,0},{2,3},{3,2},{4,5},{5,4},{6,7},{7,6},{8,9},{9,8},{10,11... | collective-permute-start | bytes 7077896 | tf_op jit(solution)/shard_map/ppermute | solution.py:24
  2.1 6.7 %collective-permute-start.1 = (f32[52,2,128]{2,1,0:T(2,128)}, f32[52,2,128]{2,1,0:T(2,128)S(1)}, u32[]{:S(2)}, u32[]{:S(2)}) collective-permute-start(f32[52,2,128]{2,1,0:T(2,128)} %shard_map.65), channel_id=1, source_target_pairs={{0,16},{1,17},{2,18},{3,19},{4,20},{5,21},{6,22},{7,23},{8,24},{9,... | collective-permute-start | bytes 159752 | tf_op jit(solution)/shard_map/ppermute | solution.py:19
  7.6 16.6 %copy-start = (bf16[1,2,768,768]{3,2,1,0:T(8,128)(2,1)S(1)}, bf16[1,2,768,768]{3,2,1,0:T(8,128)(2,1)}, u32[]{:S(2)}) copy-start(bf16[1,2,768,768]{3,2,1,0:T(8,128)(2,1)} %param.10) | copy-start | bytes 7077892
  7.6 0.8 %copy-start.2 = (s32[1,52,1]{1,2,0:T(1,128)S(1)}, s32[1,52,1]{1,2,0:T(1,128)}, u32[]{:S(2)}) copy-start(s32[1,52,1]{1,2,0:T(1,128)} %param.8) | copy-start | bytes 628
  9.1 8.3 %collective-permute-start.5 = (bf16[32,1536]{1,0:T(8,128)(2,1)S(1)}, bf16[32,1536]{1,0:T(8,128)(2,1)S(1)}, u32[]{:S(2)}, u32[]{:S(2)}) collective-permute-start(bf16[32,1536]{1,0:T(8,128)(2,1)S(1)} %get-tuple-element.30), channel_id=1, source_target_pairs={{0,14},{1,15},{2,12},{3,13},{4,10},{5,11},{6,8},{7,9},{8,6},{9,7},... | collective-permute-start | bytes 294920 | tf_op jit(solution)/shard_map/ppermute | solution.py:24
  13.8 9.8 %collective-permute-start.6 = (bf16[32,1536]{1,0:T(8,128)(2,1)S(1)}, bf16[32,1536]{1,0:T(8,128)(2,1)S(1)}, u32[]{:S(2)}, u32[]{:S(2)}) collective-permute-start(bf16[32,1536]{1,0:T(8,128)(2,1)S(1)} %get-tuple-element.31), channel_id=1, source_target_pairs={{0,2},{1,3},{2,0},{3,1},{4,6},{5,7},{6,4},{7,5},{8,10},{9,11},{10,... | collective-permute-start | bytes 294920 | tf_op jit(solution)/shard_map/ppermute | solution.py:24
  14.3 14.1 %collective-permute-start.2 = (bf16[32,1536]{1,0:T(8,128)(2,1)S(1)}, bf16[32,1536]{1,0:T(8,128)(2,1)S(1)}, u32[]{:S(2)}, u32[]{:S(2)}) collective-permute-start(bf16[32,1536]{1,0:T(8,128)(2,1)S(1)} %get-tuple-element.27), channel_id=1, source_target_pairs={{0,12},{1,13},{2,14},{3,15},{4,8},{5,9},{6,10},{7,11},{8,4},{9,5},... | collective-permute-start | bytes 294920 | tf_op jit(solution)/shard_map/ppermute | solution.py:24
  14.5 10.0 %collective-permute-start.7 = (bf16[32,1536]{1,0:T(8,128)(2,1)S(1)}, bf16[32,1536]{1,0:T(8,128)(2,1)S(1)}, u32[]{:S(2)}, u32[]{:S(2)}) collective-permute-start(bf16[32,1536]{1,0:T(8,128)(2,1)S(1)} %get-tuple-element.32), channel_id=1, source_target_pairs={{0,4},{1,5},{2,6},{3,7},{4,0},{5,1},{6,2},{7,3},{8,12},{9,13},{10,... | collective-permute-start | bytes 294920 | tf_op jit(solution)/shard_map/ppermute | solution.py:24
  14.5 12.1 %collective-permute-start.8 = (bf16[32,1536]{1,0:T(8,128)(2,1)S(1)}, bf16[32,1536]{1,0:T(8,128)(2,1)S(1)}, u32[]{:S(2)}, u32[]{:S(2)}) collective-permute-start(bf16[32,1536]{1,0:T(8,128)(2,1)S(1)} %get-tuple-element.33), channel_id=1, source_target_pairs={{0,6},{1,7},{2,4},{3,5},{4,2},{5,3},{6,0},{7,1},{8,14},{9,15},{10,... | collective-permute-start | bytes 294920 | tf_op jit(solution)/shard_map/ppermute | solution.py:24
  17.5 12.6 %collective-permute-start.3 = (bf16[32,1536]{1,0:T(8,128)(2,1)S(1)}, bf16[32,1536]{1,0:T(8,128)(2,1)S(1)}, u32[]{:S(2)}, u32[]{:S(2)}) collective-permute-start(bf16[32,1536]{1,0:T(8,128)(2,1)S(1)} %get-tuple-element.28), channel_id=1, source_target_pairs={{0,10},{1,11},{2,8},{3,9},{4,14},{5,15},{6,12},{7,13},{8,2},{9,3},... | collective-permute-start | bytes 294920 | tf_op jit(solution)/shard_map/ppermute | solution.py:24
  23.5 7.3 %collective-permute-start.4 = (bf16[32,1536]{1,0:T(8,128)(2,1)S(1)}, bf16[32,1536]{1,0:T(8,128)(2,1)S(1)}, u32[]{:S(2)}, u32[]{:S(2)}) collective-permute-start(bf16[32,1536]{1,0:T(8,128)(2,1)S(1)} %get-tuple-element.29), channel_id=1, source_target_pairs={{0,8},{1,9},{2,10},{3,11},{4,12},{5,13},{6,14},{7,15},{8,0},{9,1},... | collective-permute-start | bytes 294920 | tf_op jit(solution)/shard_map/ppermute | solution.py:24
  32.4 16.8 %copy-start.1 = (bf16[2,2,384,384]{3,2,1,0:T(8,128)(2,1)S(1)}, bf16[2,2,384,384]{3,2,1,0:T(8,128)(2,1)}, u32[]{:S(2)}) copy-start(bf16[2,2,384,384]{3,2,1,0:T(8,128)(2,1)} %factors_ref.1) | copy-start | bytes 3538948
  32.5 4.8 %collective-permute-start.9 = (bf16[16,896]{1,0:T(8,128)(2,1)S(1)}, bf16[16,896]{1,0:T(8,128)(2,1)S(1)}, u32[]{:S(2)}, u32[]{:S(2)}) collective-permute-start(bf16[16,896]{1,0:T(8,128)(2,1)S(1)} %get-tuple-element.37), channel_id=1, source_target_pairs={{0,8},{1,9},{2,10},{3,11},{4,12},{5,13},{6,14},{7,15},{8,0},{9,1},... | collective-permute-start | bytes 86024 | tf_op jit(solution)/shard_map/ppermute | solution.py:24
  32.5 23.0 %all-to-all-start = ((bf16[8,32,1536]{2,1,0:T(8,128)(2,1)}), bf16[8,32,1536]{2,1,0:T(8,128)(2,1)S(1)}, u32[]{:S(2)}, u32[]{:S(2)}) async-start(bf16[8,32,1536]{2,1,0:T(8,128)(2,1)} %bitcast.5), calls=%async_computation | async-start | bytes 1572864 | tf_op jit(solution)/shard_map/all_to_all | solution.py:230
  37.3 1.3 %collective-permute-start.10 = (bf16[16,896]{1,0:T(8,128)(2,1)S(1)}, bf16[16,896]{1,0:T(8,128)(2,1)S(1)}, u32[]{:S(2)}, u32[]{:S(2)}) collective-permute-start(bf16[16,896]{1,0:T(8,128)(2,1)S(1)} %fusion), channel_id=1, source_target_pairs={{0,1},{1,0},{2,3},{3,2},{4,5},{5,4},{6,7},{7,6},{8,9},{9,8},{10,11... | collective-permute-start | bytes 86024 | tf_op jit(solution)/shard_map/ppermute | solution.py:24
  38.6 4.8 %collective-permute-start.11 = (bf16[12,896]{1,0:T(8,128)(2,1)S(1)}, bf16[12,896]{1,0:T(8,128)(2,1)S(1)}, u32[]{:S(2)}, u32[]{:S(2)}) collective-permute-start(bf16[12,896]{1,0:T(8,128)(2,1)S(1)} %pad_maximum_fusion), channel_id=1, source_target_pairs={{0,2},{1,3},{2,0},{3,1},{4,6},{5,7},{6,4},{7,5},{8,10},{9,11},{10,... | collective-permute-start | bytes 64520 | tf_op jit(solution)/shard_map/ppermute | solution.py:24
  43.5 5.8 %collective-permute-start.12 = (bf16[8,896]{1,0:T(8,128)(2,1)S(1)}, bf16[8,896]{1,0:T(8,128)(2,1)S(1)}, u32[]{:S(2)}, u32[]{:S(2)}) collective-permute-start(bf16[8,896]{1,0:T(8,128)(2,1)S(1)} %pad_maximum_fusion.2), channel_id=1, source_target_pairs={{0,4},{1,5},{2,6},{3,7},{4,0},{5,1},{6,2},{7,3},{8,12},{9,13},{10,... | collective-permute-start | bytes 43016 | tf_op jit(solution)/shard_map/ppermute | solution.py:24

commit v7 on v6

--- a/solution.py
+++ b/solution.py
@@ -14,9 +14,9 @@
 LANES = 128
 
 
-def from_behind(value, axis):
+def around(value, axis):
     count = lax.axis_size(axis)
-    return lax.ppermute(value, axis, [(at, at + 1) for at in range(count - 1)])
+    return lax.ppermute(value, axis, [(at, (at + 1) % count) for at in range(count)])
 
 
 def exchange(value, distance):
@@ -76,7 +76,7 @@
     first = lax.broadcasted_iota(jnp.int32, face_re.shape, 2) < front
     face = jnp.where(first, pltpu.roll(face_re, front, 2), face_im)
     other = jnp.where(first, pltpu.roll(face_im, front, 2), face_re)
-    out_ref[...] = by_same * face + by_other * other
+    out_ref[...] = (by_same * face + by_other * other).reshape(out_ref.shape).astype(BF16)
 
 
 def dispatch_kernel(front, pick_ref, rows_ref, arriving_ref, _, *refs):
@@ -85,11 +85,11 @@
     rhs_ref[...] = rows_ref[...]
     for part in range(2):
         face = pl.ds((part + 1) * leaf_n - 2 * front, 2 * front)
-        incoming = arriving_ref[...]
+        incoming = arriving_ref[...].astype(F32)
         lane = lax.broadcasted_iota(jnp.int32, incoming.shape, 1)
         if part == 0:
             incoming = pltpu.roll(incoming, front, 1)
-        incoming = jnp.where(lane >= front, incoming, 0.0)
+        incoming = jnp.where((lane >= front) & (lax.axis_index("panel") > 0), incoming, 0.0)
         rhs_ref[:, face] = (rows_ref[:, face].astype(F32) + incoming).astype(BF16)
     size = out_refs[0].shape[0]
     send = dot(pick_ref[...], rhs_ref[...]).astype(BF16)
@@ -269,23 +269,24 @@
     sibling = exchange(own, 1)
 
     face = jax.ShapeDtypeStruct((leaves, shots, 2 * front), BF16)
+    rows = leaves * shots
     leaving = call(
         functools.partial(face_kernel, front),
-        jax.ShapeDtypeStruct((leaves, shots, 2 * front), F32),
+        jax.ShapeDtypeStruct((rows, 2 * front), BF16),
         (source, tau),
         hbm=(0, 1),
         scratch=[VMEM(face.shape, BF16)] * 2 + [VMEM(tau.shape, F32), pltpu.SemaphoreType.DMA((3,))],
         limit=60,
     )
-    arriving = from_behind(leaving, "panel")
+    arriving = around(leaving, "panel")
     tau_re, tau_im = tau[..., :front], tau[..., front:]
     for _ in range(lax.axis_size("panel") - 2):
+        arriving = jnp.where(lax.axis_index("panel") > 0, arriving, 0).reshape(face.shape).astype(F32)
         real = arriving[..., :front] + source[..., leaf_n - front : leaf_n].astype(F32)
         imag = arriving[..., front:] + source[..., 2 * leaf_n - front :].astype(F32)
         leaving = jnp.concatenate([tau_re * real - tau_im * imag, tau_re * imag + tau_im * real], axis=-1)
-        arriving = from_behind(leaving, "panel")
-
-    rows = leaves * shots
+        arriving = around(leaving.reshape(rows, 2 * front).astype(BF16), "panel")
+
     to_slots, from_slots = call(
         functools.partial(slot_kernel, shots, capacity),
         [jax.ShapeDtypeStruct((slots, rows), BF16), jax.ShapeDtypeStruct((rows, slots), BF16)],
@@ -295,7 +296,7 @@
     sent = call(
         functools.partial(dispatch_kernel, front),
         [block] * pairs,
-        (to_slots, source.reshape(rows, width2), arriving.reshape(rows, 2 * front), sibling),
+        (to_slots, source.reshape(rows, width2), arriving, sibling),
         hbm=(3,),
         scratch=[VMEM((rows, width2), BF16)],
     )

time: 56.9 us -> 55.2 us (0.970)
  starting transfers between devices: 29.6 us -> 25.7 us
  waiting for transfers between devices: 16.2 us -> 18.4 us
    ppermute x12, starting transfers between devices: 20.7 us -> 18.6 us  [exchange(): return lax.ppermute(value, 'leaf', pairs)]
    ppermute x1, starting transfers between devices: 4.4 us -> 2.55 us  [around(): lax.ppermute(value, axis, [(at, (at + 1) % count) for at in range(count)])]
    ppermute x12, waiting for transfers between devices: 10.8 us -> 12.3 us  [exchange(): return lax.ppermute(value, 'leaf', pairs)]
    all_to_all x1, waiting for transfers between devices: 5.38 us -> 6.05 us  [to_pairs(): lax.all_to_all(value, 'leaf', 0, 0, tiled=True, axis_index_groups=groups)]
where the time goes in v7:
time: 55.2 us; the launch traced here: 54.9 us
  starting transfers between devices  25.7 us (47%)
  waiting for transfers between devices  18.4 us (33%)
  Pallas kernels  7.85 us (14%)
  local copies, waits for them, and re-layouts  1.96 us (4%)
  between operations  0.87 us (2%)
    ppermute x12, starting transfers between devices, exchange(): return lax.ppermute(value, 'leaf', pairs)  18.6 us
    ppermute x12, waiting for transfers between devices, exchange(): return lax.ppermute(value, 'leaf', pairs)  12.3 us
    pallas_call x8, Pallas kernels, call(): pl.pallas_call(kernel, out_shape=out_shape, in_specs=[pl.BlockSpec(memory...  7.85 us
    all_to_all x1, waiting for transfers between devices, to_pairs(): lax.all_to_all(value, 'leaf', 0, 0, tiled=True, axis_index_groups=groups)  6.05 us
    all_to_all x1, starting transfers between devices, to_pairs(): lax.all_to_all(value, 'leaf', 0, 0, tiled=True, axis_index_groups=groups)  4.56 us
    ppermute x1, starting transfers between devices, around(): lax.ppermute(value, axis, [(at, (at + 1) % count) for at in range(count)])  2.55 us
  transfers between devices with their start and end apart: 14, of which 8 were waited for; matrix products, arithmetic and copies ran while one was open for 2% of the time, Pallas kernels for 9%

profile of v7, /device:TPU:0, one launch (start us, length us, event | category | flops | bytes accessed | tf_op | source)
XLA Modules:
  0.0 54.9 jit_solution(16003657959105366188)
XLA Ops:
  0.0 0.5 collective-permute-start
  0.5 1.6 %shard_map.65 = bf16[104,128]{1,0:T(8,128)(2,1)} custom-call(bf16[52,2,1536]{2,1,0:T(2,128)(2,1)} %bitcast.11, f32[52,1,128]{2,1,0:T(1,128)} %bitcast.12), custom_call_target="tpu_custom_call" | custom-call | tf_op jit(solution)/shard_map/pallas_call | solution.py:216
  2.1 2.6 %collective-permute-start.1 = (bf16[104,128]{1,0:T(8,128)(2,1)}, bf16[104,128]{1,0:T(8,128)(2,1)S(1)}, u32[]{:S(2)}, u32[]{:S(2)}) collective-permute-start(bf16[104,128]{1,0:T(8,128)(2,1)} %shard_map.65), channel_id=1, source_target_pairs={{0,16},{16,0},{1,17},{17,1},{2,18},{18,2},{3,19},{19,3},{4,20},{20... | collective-permute-start | bytes 79880 | tf_op jit(solution)/shard_map/ppermute | solution.py:19
  4.6 1.1 %reshape_squeeze.7.rows_ref = bf16[104,1536]{1,0:T(8,128)(2,1)S(1)} reshape(bf16[1,52,2,1536]{3,2,1,0:T(2,128)(2,1)} %param.6) | data formatting | bytes 638976 | tf_op jit(solution)/shard_map/reshape;squeeze | solution.py:299
  5.7 0.8 %copy-done.2 = s32[1,52,1]{1,2,0:T(1,128)S(1)} copy-done((s32[1,52,1]{1,2,0:T(1,128)S(1)}, s32[1,52,1]{1,2,0:T(1,128)}, u32[]{:S(2)}) %copy-start.2) | copy-done | bytes 232
  6.9 0.4 shard_map.66
  7.3 4.9 %collective-permute-start.5 = (bf16[32,1536]{1,0:T(8,128)(2,1)S(1)}, bf16[32,1536]{1,0:T(8,128)(2,1)S(1)}, u32[]{:S(2)}, u32[]{:S(2)}) collective-permute-start(bf16[32,1536]{1,0:T(8,128)(2,1)S(1)} %get-tuple-element.30), channel_id=1, source_target_pairs={{0,14},{1,15},{2,12},{3,13},{4,10},{5,11},{6,8},{7,9},{8,6},{9,7},... | collective-permute-start | bytes 294920 | tf_op jit(solution)/shard_map/ppermute | solution.py:24
  12.2 0.5 collective-permute-start.6
  12.8 3.1 %collective-permute-start.8 = (bf16[32,1536]{1,0:T(8,128)(2,1)S(1)}, bf16[32,1536]{1,0:T(8,128)(2,1)S(1)}, u32[]{:S(2)}, u32[]{:S(2)}) collective-permute-start(bf16[32,1536]{1,0:T(8,128)(2,1)S(1)} %get-tuple-element.33), channel_id=1, source_target_pairs={{0,6},{1,7},{2,4},{3,5},{4,2},{5,3},{6,0},{7,1},{8,14},{9,15},{10,... | collective-permute-start | bytes 294920 | tf_op jit(solution)/shard_map/ppermute | solution.py:24
  15.9 6.0 %collective-permute-start.3 = (bf16[32,1536]{1,0:T(8,128)(2,1)S(1)}, bf16[32,1536]{1,0:T(8,128)(2,1)S(1)}, u32[]{:S(2)}, u32[]{:S(2)}) collective-permute-start(bf16[32,1536]{1,0:T(8,128)(2,1)S(1)} %get-tuple-element.28), channel_id=1, source_target_pairs={{0,10},{1,11},{2,8},{3,9},{4,14},{5,15},{6,12},{7,13},{8,2},{9,3},... | collective-permute-start | bytes 294920 | tf_op jit(solution)/shard_map/ppermute | solution.py:24
  23.0 1.3 %collective-permute-done.8.refs_3_ = bf16[32,1536]{1,0:T(8,128)(2,1)S(1)} collective-permute-done((bf16[32,1536]{1,0:T(8,128)(2,1)S(1)}, bf16[32,1536]{1,0:T(8,128)(2,1)S(1)}, u32[]{:S(2)}, u32[]{:S(2)}) %collective-permute-start.8) | collective-permute-done | bytes 98336 | tf_op jit(solution)/shard_map/ppermute | solution.py:24
  24.2 1.7 %shard_map.68 = (bf16[8,2,16,1536]{3,2,1,0:T(8,128)(2,1)}, f32[32,768]{1,0:T(8,128)S(1)}) custom-call(bf16[2,768,768]{2,1,0:T(8,128)(2,1)S(1)} %get-tuple-element.25.own_ref, bf16[2,768,768]{2,1,0:T(8,128)(2,1)S(1)} %get-tuple-element.26.sibling_ref, bf16[32,1536]{1,0:T(8,128)(2,1)S(1)} %collective-permute-done.5.refs_0_, ...), custom_call_target="tpu_custom_call" | custom-call | tf_op jit(solution)/shard_map/pallas_call | solution.py:216
  26.0 2.3 %collective-permute-done.3.refs_1_ = bf16[32,1536]{1,0:T(8,128)(2,1)S(1)} collective-permute-done((bf16[32,1536]{1,0:T(8,128)(2,1)S(1)}, bf16[32,1536]{1,0:T(8,128)(2,1)S(1)}, u32[]{:S(2)}, u32[]{:S(2)}) %collective-permute-start.3) | collective-permute-done | bytes 98336 | tf_op jit(solution)/shard_map/ppermute | solution.py:24
  28.3 0.7 %collective-permute-done.4.refs_2_ = bf16[32,1536]{1,0:T(8,128)(2,1)S(1)} collective-permute-done((bf16[32,1536]{1,0:T(8,128)(2,1)S(1)}, bf16[32,1536]{1,0:T(8,128)(2,1)S(1)}, u32[]{:S(2)}, u32[]{:S(2)}) %collective-permute-start.4) | collective-permute-done | bytes 98336 | tf_op jit(solution)/shard_map/ppermute | solution.py:24
  29.0 1.6 %shard_map.69 = (bf16[8,2,16,1536]{3,2,1,0:T(8,128)(2,1)}, f32[16,896]{1,0:T(8,128)S(1)}, bf16[16,896]{1,0:T(8,128)(2,1)S(1)}) custom-call(bf16[2,768,768]{2,1,0:T(8,128)(2,1)S(1)} %get-tuple-element.25.own_ref, bf16[2,768,768]{2,1,0:T(8,128)(2,1)S(1)} %get-tuple-element.26.sibling_ref, ...), custom_call_target="tpu_custom_call", output_to_operand_aliasing={{0}: (7, {})} | custom-call | tf_op jit(solution)/shard_map/pallas_call | solution.py:216
  30.7 4.6 %all-to-all-start = ((bf16[8,32,1536]{2,1,0:T(8,128)(2,1)}), bf16[8,32,1536]{2,1,0:T(8,128)(2,1)S(1)}, u32[]{:S(2)}, u32[]{:S(2)}) async-start(bf16[8,32,1536]{2,1,0:T(8,128)(2,1)} %bitcast.4), calls=%async_computation | async-start | bytes 1572864 | tf_op jit(solution)/shard_map/all_to_all | solution.py:230
  35.5 1.2 %collective-permute-done.10 = bf16[16,896]{1,0:T(8,128)(2,1)S(1)} collective-permute-done((bf16[16,896]{1,0:T(8,128)(2,1)S(1)}, bf16[16,896]{1,0:T(8,128)(2,1)S(1)}, u32[]{:S(2)}, u32[]{:S(2)}) %collective-permute-start.10) | collective-permute-done | bytes 28704 | tf_op jit(solution)/shard_map/ppermute | solution.py:24
  36.8 1.9 %collective-permute-start.11 = (bf16[12,896]{1,0:T(8,128)(2,1)S(1)}, bf16[12,896]{1,0:T(8,128)(2,1)S(1)}, u32[]{:S(2)}, u32[]{:S(2)}) collective-permute-start(bf16[12,896]{1,0:T(8,128)(2,1)S(1)} %pad_maximum_fusion), channel_id=1, source_target_pairs={{0,2},{1,3},{2,0},{3,1},{4,6},{5,7},{6,4},{7,5},{8,10},{9,11},{10,... | collective-permute-start | bytes 64520 | tf_op jit(solution)/shard_map/ppermute | solution.py:24
  38.7 3.0 %collective-permute-done.11 = bf16[12,896]{1,0:T(8,128)(2,1)S(1)} collective-permute-done((bf16[12,896]{1,0:T(8,128)(2,1)S(1)}, bf16[12,896]{1,0:T(8,128)(2,1)S(1)}, u32[]{:S(2)}, u32[]{:S(2)}) %collective-permute-start.11) | collective-permute-done | bytes 21536 | tf_op jit(solution)/shard_map/ppermute | solution.py:24
  41.8 1.4 %collective-permute-start.12 = (bf16[8,896]{1,0:T(8,128)(2,1)S(1)}, bf16[8,896]{1,0:T(8,128)(2,1)S(1)}, u32[]{:S(2)}, u32[]{:S(2)}) collective-permute-start(bf16[8,896]{1,0:T(8,128)(2,1)S(1)} %pad_maximum_fusion.2), channel_id=1, source_target_pairs={{0,4},{1,5},{2,6},{3,7},{4,0},{5,1},{6,2},{7,3},{8,12},{9,13},{10,... | collective-permute-start | bytes 43016 | tf_op jit(solution)/shard_map/ppermute | solution.py:24
  43.2 3.7 %collective-permute-done.12.arrived_ref = bf16[8,896]{1,0:T(8,128)(2,1)S(1)} collective-permute-done((bf16[8,896]{1,0:T(8,128)(2,1)S(1)}, bf16[8,896]{1,0:T(8,128)(2,1)S(1)}, u32[]{:S(2)}, u32[]{:S(2)}) %collective-permute-start.12) | collective-permute-done | bytes 14368 | tf_op jit(solution)/shard_map/ppermute | solution.py:24
  46.9 0.9 %shard_map.70.above_ref = f32[4,384]{1,0:T(4,128)S(1)} custom-call(f32[8,896]{1,0:T(8,128)S(1)} %pad_maximum_fusion.1.keep_ref, bf16[8,896]{1,0:T(8,128)(2,1)S(1)} %collective-permute-done.12.arrived_ref, bf16[2,2,384,384]{3,2,1,0:T(8,128)(2,1)S(1)} %copy-done.1), custom_call_target="tpu_custom_call" | custom-call | flops 1 | bytes 1 | tf_op jit(solution)/shard_map/pallas_call | solution.py:216
  47.8 6.1 %all-to-all-done = bf16[8,32,1536]{2,1,0:T(8,128)(2,1)S(1)} async-done(((bf16[8,32,1536]{2,1,0:T(8,128)(2,1)}), bf16[8,32,1536]{2,1,0:T(8,128)(2,1)S(1)}, u32[]{:S(2)}, u32[]{:S(2)}) %all-to-all-start) | async-done | bytes 786464 | tf_op jit(solution)/shard_map/all_to_all | solution.py:230
  53.9 1.0 %shard_map.71 = bf16[52,2,1536]{2,1,0:T(2,128)(2,1)} custom-call(bf16[104,256]{1,0:T(8,128)(2,1)S(1)} %get-tuple-element.22.pick_ref, f32[4,384]{1,0:T(4,128)S(1)} %shard_map.70.above_ref, bf16[256,1536]{1,0:T(8,128)(2,1)S(1)} %bitcast.7), custom_call_target="tpu_custom_call" | custom-call | tf_op jit(solution)/shard_map/pallas_call | solution.py:216
  (33 shorter events, 1.3 us)
Async XLA Ops:
  0.0 6.9 %collective-permute-start = (bf16[2,768,768]{2,1,0:T(8,128)(2,1)}, bf16[2,768,768]{2,1,0:T(8,128)(2,1)S(1)}, u32[]{:S(2)}, u32[]{:S(2)}) collective-permute-start(bf16[2,768,768]{2,1,0:T(8,128)(2,1)} %bitcast.8), channel_id=1, source_target_pairs={{0,1},{1,0},{2,3},{3,2},{4,5},{5,4},{6,7},{7,6},{8,9},{9,8},{10,11... | collective-permute-start | bytes 7077896 | tf_op jit(solution)/shard_map/ppermute | solution.py:24
  2.1 4.8 %collective-permute-start.1 = (bf16[104,128]{1,0:T(8,128)(2,1)}, bf16[104,128]{1,0:T(8,128)(2,1)S(1)}, u32[]{:S(2)}, u32[]{:S(2)}) collective-permute-start(bf16[104,128]{1,0:T(8,128)(2,1)} %shard_map.65), channel_id=1, source_target_pairs={{0,16},{16,0},{1,17},{17,1},{2,18},{18,2},{3,19},{19,3},{4,20},{20... | collective-permute-start | bytes 79880 | tf_op jit(solution)/shard_map/ppermute | solution.py:19
  5.7 16.9 %copy-start = (bf16[1,2,768,768]{3,2,1,0:T(8,128)(2,1)S(1)}, bf16[1,2,768,768]{3,2,1,0:T(8,128)(2,1)}, u32[]{:S(2)}) copy-start(bf16[1,2,768,768]{3,2,1,0:T(8,128)(2,1)} %param.10) | copy-start | bytes 7077892
  5.7 0.8 %copy-start.2 = (s32[1,52,1]{1,2,0:T(1,128)S(1)}, s32[1,52,1]{1,2,0:T(1,128)}, u32[]{:S(2)}) copy-start(s32[1,52,1]{1,2,0:T(1,128)} %param.8) | copy-start | bytes 628
  7.3 8.6 %collective-permute-start.5 = (bf16[32,1536]{1,0:T(8,128)(2,1)S(1)}, bf16[32,1536]{1,0:T(8,128)(2,1)S(1)}, u32[]{:S(2)}, u32[]{:S(2)}) collective-permute-start(bf16[32,1536]{1,0:T(8,128)(2,1)S(1)} %get-tuple-element.30), channel_id=1, source_target_pairs={{0,14},{1,15},{2,12},{3,13},{4,10},{5,11},{6,8},{7,9},{8,6},{9,7},... | collective-permute-start | bytes 294920 | tf_op jit(solution)/shard_map/ppermute | solution.py:24
  12.2 9.8 %collective-permute-start.6 = (bf16[32,1536]{1,0:T(8,128)(2,1)S(1)}, bf16[32,1536]{1,0:T(8,128)(2,1)S(1)}, u32[]{:S(2)}, u32[]{:S(2)}) collective-permute-start(bf16[32,1536]{1,0:T(8,128)(2,1)S(1)} %get-tuple-element.31), channel_id=1, source_target_pairs={{0,2},{1,3},{2,0},{3,1},{4,6},{5,7},{6,4},{7,5},{8,10},{9,11},{10,... | collective-permute-start | bytes 294920 | tf_op jit(solution)/shard_map/ppermute | solution.py:24
  12.7 13.3 %collective-permute-start.2 = (bf16[32,1536]{1,0:T(8,128)(2,1)S(1)}, bf16[32,1536]{1,0:T(8,128)(2,1)S(1)}, u32[]{:S(2)}, u32[]{:S(2)}) collective-permute-start(bf16[32,1536]{1,0:T(8,128)(2,1)S(1)} %get-tuple-element.27), channel_id=1, source_target_pairs={{0,12},{1,13},{2,14},{3,15},{4,8},{5,9},{6,10},{7,11},{8,4},{9,5},... | collective-permute-start | bytes 294920 | tf_op jit(solution)/shard_map/ppermute | solution.py:24
  12.8 10.1 %collective-permute-start.7 = (bf16[32,1536]{1,0:T(8,128)(2,1)S(1)}, bf16[32,1536]{1,0:T(8,128)(2,1)S(1)}, u32[]{:S(2)}, u32[]{:S(2)}) collective-permute-start(bf16[32,1536]{1,0:T(8,128)(2,1)S(1)} %get-tuple-element.32), channel_id=1, source_target_pairs={{0,4},{1,5},{2,6},{3,7},{4,0},{5,1},{6,2},{7,3},{8,12},{9,13},{10,... | collective-permute-start | bytes 294920 | tf_op jit(solution)/shard_map/ppermute | solution.py:24
  12.8 11.4 %collective-permute-start.8 = (bf16[32,1536]{1,0:T(8,128)(2,1)S(1)}, bf16[32,1536]{1,0:T(8,128)(2,1)S(1)}, u32[]{:S(2)}, u32[]{:S(2)}) collective-permute-start(bf16[32,1536]{1,0:T(8,128)(2,1)S(1)} %get-tuple-element.33), channel_id=1, source_target_pairs={{0,6},{1,7},{2,4},{3,5},{4,2},{5,3},{6,0},{7,1},{8,14},{9,15},{10,... | collective-permute-start | bytes 294920 | tf_op jit(solution)/shard_map/ppermute | solution.py:24
  15.9 12.4 %collective-permute-start.3 = (bf16[32,1536]{1,0:T(8,128)(2,1)S(1)}, bf16[32,1536]{1,0:T(8,128)(2,1)S(1)}, u32[]{:S(2)}, u32[]{:S(2)}) collective-permute-start(bf16[32,1536]{1,0:T(8,128)(2,1)S(1)} %get-tuple-element.28), channel_id=1, source_target_pairs={{0,10},{1,11},{2,8},{3,9},{4,14},{5,15},{6,12},{7,13},{8,2},{9,3},... | collective-permute-start | bytes 294920 | tf_op jit(solution)/shard_map/ppermute | solution.py:24
  22.0 7.0 %collective-permute-start.4 = (bf16[32,1536]{1,0:T(8,128)(2,1)S(1)}, bf16[32,1536]{1,0:T(8,128)(2,1)S(1)}, u32[]{:S(2)}, u32[]{:S(2)}) collective-permute-start(bf16[32,1536]{1,0:T(8,128)(2,1)S(1)} %get-tuple-element.29), channel_id=1, source_target_pairs={{0,8},{1,9},{2,10},{3,11},{4,12},{5,13},{6,14},{7,15},{8,0},{9,1},... | collective-permute-start | bytes 294920 | tf_op jit(solution)/shard_map/ppermute | solution.py:24
  30.6 16.3 %copy-start.1 = (bf16[2,2,384,384]{3,2,1,0:T(8,128)(2,1)S(1)}, bf16[2,2,384,384]{3,2,1,0:T(8,128)(2,1)}, u32[]{:S(2)}) copy-start(bf16[2,2,384,384]{3,2,1,0:T(8,128)(2,1)} %factors_ref.1) | copy-start | bytes 3538948
  30.6 4.8 %collective-permute-start.9 = (bf16[16,896]{1,0:T(8,128)(2,1)S(1)}, bf16[16,896]{1,0:T(8,128)(2,1)S(1)}, u32[]{:S(2)}, u32[]{:S(2)}) collective-permute-start(bf16[16,896]{1,0:T(8,128)(2,1)S(1)} %get-tuple-element.37), channel_id=1, source_target_pairs={{0,8},{1,9},{2,10},{3,11},{4,12},{5,13},{6,14},{7,15},{8,0},{9,1},... | collective-permute-start | bytes 86024 | tf_op jit(solution)/shard_map/ppermute | solution.py:24
  30.7 23.2 %all-to-all-start = ((bf16[8,32,1536]{2,1,0:T(8,128)(2,1)}), bf16[8,32,1536]{2,1,0:T(8,128)(2,1)S(1)}, u32[]{:S(2)}, u32[]{:S(2)}) async-start(bf16[8,32,1536]{2,1,0:T(8,128)(2,1)} %bitcast.4), calls=%async_computation | async-start | bytes 1572864 | tf_op jit(solution)/shard_map/all_to_all | solution.py:230
  35.5 1.3 %collective-permute-start.10 = (bf16[16,896]{1,0:T(8,128)(2,1)S(1)}, bf16[16,896]{1,0:T(8,128)(2,1)S(1)}, u32[]{:S(2)}, u32[]{:S(2)}) collective-permute-start(bf16[16,896]{1,0:T(8,128)(2,1)S(1)} %fusion), channel_id=1, source_target_pairs={{0,1},{1,0},{2,3},{3,2},{4,5},{5,4},{6,7},{7,6},{8,9},{9,8},{10,11... | collective-permute-start | bytes 86024 | tf_op jit(solution)/shard_map/ppermute | solution.py:24
  36.8 4.9 %collective-permute-start.11 = (bf16[12,896]{1,0:T(8,128)(2,1)S(1)}, bf16[12,896]{1,0:T(8,128)(2,1)S(1)}, u32[]{:S(2)}, u32[]{:S(2)}) collective-permute-start(bf16[12,896]{1,0:T(8,128)(2,1)S(1)} %pad_maximum_fusion), channel_id=1, source_target_pairs={{0,2},{1,3},{2,0},{3,1},{4,6},{5,7},{6,4},{7,5},{8,10},{9,11},{10,... | collective-permute-start | bytes 64520 | tf_op jit(solution)/shard_map/ppermute | solution.py:24
  41.8 5.1 %collective-permute-start.12 = (bf16[8,896]{1,0:T(8,128)(2,1)S(1)}, bf16[8,896]{1,0:T(8,128)(2,1)S(1)}, u32[]{:S(2)}, u32[]{:S(2)}) collective-permute-start(bf16[8,896]{1,0:T(8,128)(2,1)S(1)} %pad_maximum_fusion.2), channel_id=1, source_target_pairs={{0,4},{1,5},{2,6},{3,7},{4,0},{5,1},{6,2},{7,3},{8,12},{9,13},{10,... | collective-permute-start | bytes 43016 | tf_op jit(solution)/shard_map/ppermute | solution.py:24

commit v8 on v7

--- a/solution.py
+++ b/solution.py
@@ -221,7 +221,7 @@
         scratch_shapes=list(scratch),
         input_output_aliases=aliases,
         cost_estimate=cost and pl.CostEstimate(flops=cost[0], bytes_accessed=cost[1], transcendentals=0),
-        compiler_params=pltpu.CompilerParams(vmem_limit_bytes=limit * 2**20),
+        compiler_params=pltpu.CompilerParams(vmem_limit_bytes=int(limit * 2**20)),
     )(*args)
 
 
@@ -276,7 +276,7 @@
         (source, tau),
         hbm=(0, 1),
         scratch=[VMEM(face.shape, BF16)] * 2 + [VMEM(tau.shape, F32), pltpu.SemaphoreType.DMA((3,))],
-        limit=60,
+        limit=53.9,
     )
     arriving = around(leaving, "panel")
     tau_re, tau_im = tau[..., :front], tau[..., front:]

time: 55.2 us -> 54.5 us (0.987)
  waiting for transfers between devices: 18.4 us -> 15.6 us
  starting transfers between devices: 25.7 us -> 28.4 us
  Pallas kernels: 7.85 us -> 7.24 us
    ppermute x12, starting transfers between devices: 18.6 us -> 21.2 us  [exchange(): return lax.ppermute(value, 'leaf', pairs)]
    ppermute x12, waiting for transfers between devices: 12.3 us -> 10.8 us  [exchange(): return lax.ppermute(value, 'leaf', pairs)]
    all_to_all x1, waiting for transfers between devices: 6.05 us -> 4.75 us  [to_pairs(): lax.all_to_all(value, 'leaf', 0, 0, tiled=True, axis_index_groups=groups)]
    pallas_call x8, Pallas kernels: 7.85 us -> 7.24 us  [call(): pl.pallas_call(kernel, out_shape=out_shape, in_specs=[pl.BlockSpec(memory...]
  transfers between devices with their start and end apart: 14 -> 14, of which waited for: 8 -> 8; matrix products, arithmetic and copies ran while one was open for 2% -> 2% of each run, Pallas kernels for 9% -> 8%
where the time goes in v8:
time: 54.5 us; the launch traced here: 54.1 us
  starting transfers between devices  28.4 us (52%)
  waiting for transfers between devices  15.6 us (29%)
  Pallas kernels  7.24 us (13%)
  local copies, waits for them, and re-layouts  1.96 us (4%)
  between operations  0.87 us (2%)
    ppermute x12, starting transfers between devices, exchange(): return lax.ppermute(value, 'leaf', pairs)  21.2 us
    ppermute x12, waiting for transfers between devices, exchange(): return lax.ppermute(value, 'leaf', pairs)  10.8 us
    pallas_call x8, Pallas kernels, call(): pl.pallas_call(kernel, out_shape=out_shape, in_specs=[pl.BlockSpec(memory...  7.24 us
    all_to_all x1, waiting for transfers between devices, to_pairs(): lax.all_to_all(value, 'leaf', 0, 0, tiled=True, axis_index_groups=groups)  4.75 us
    all_to_all x1, starting transfers between devices, to_pairs(): lax.all_to_all(value, 'leaf', 0, 0, tiled=True, axis_index_groups=groups)  4.69 us
    ppermute x1, starting transfers between devices, around(): lax.ppermute(value, axis, [(at, (at + 1) % count) for at in range(count)])  2.55 us
  transfers between devices with their start and end apart: 14, of which 8 were waited for; matrix products, arithmetic and copies ran while one was open for 2% of the time, Pallas kernels for 8%

profile of v8, /device:TPU:0, one launch (start us, length us, event | category | flops | bytes accessed | tf_op | source)
XLA Modules:
  0.0 54.1 jit_solution(10163268519075157416)
XLA Ops:
  0.0 0.5 collective-permute-start
  0.5 1.0 %shard_map.65 = bf16[104,128]{1,0:T(8,128)(2,1)S(1)} custom-call(bf16[52,2,1536]{2,1,0:T(2,128)(2,1)} %bitcast.11, f32[52,1,128]{2,1,0:T(1,128)} %bitcast.12), custom_call_target="tpu_custom_call" | custom-call | tf_op jit(solution)/shard_map/pallas_call | solution.py:216
  1.5 2.6 %collective-permute-start.1 = (bf16[104,128]{1,0:T(8,128)(2,1)S(1)}, bf16[104,128]{1,0:T(8,128)(2,1)S(1)}, u32[]{:S(2)}, u32[]{:S(2)}) collective-permute-start(bf16[104,128]{1,0:T(8,128)(2,1)S(1)} %shard_map.65), channel_id=1, source_target_pairs={{0,16},{16,0},{1,17},{17,1},{2,18},{18,2},{3,19},{19,3},{4,20},{20... | collective-permute-start | bytes 79880 | tf_op jit(solution)/shard_map/ppermute | solution.py:19
  4.0 1.1 %reshape_squeeze.7.rows_ref = bf16[104,1536]{1,0:T(8,128)(2,1)S(1)} reshape(bf16[1,52,2,1536]{3,2,1,0:T(2,128)(2,1)} %param.6) | data formatting | bytes 638976 | tf_op jit(solution)/shard_map/reshape;squeeze | solution.py:299
  5.1 0.8 %copy-done.2 = s32[1,52,1]{1,2,0:T(1,128)S(1)} copy-done((s32[1,52,1]{1,2,0:T(1,128)S(1)}, s32[1,52,1]{1,2,0:T(1,128)}, u32[]{:S(2)}) %copy-start.2) | copy-done | bytes 232
  6.3 0.4 shard_map.66
  6.7 4.7 %collective-permute-start.5 = (bf16[32,1536]{1,0:T(8,128)(2,1)S(1)}, bf16[32,1536]{1,0:T(8,128)(2,1)S(1)}, u32[]{:S(2)}, u32[]{:S(2)}) collective-permute-start(bf16[32,1536]{1,0:T(8,128)(2,1)S(1)} %get-tuple-element.30), channel_id=1, source_target_pairs={{0,14},{1,15},{2,12},{3,13},{4,10},{5,11},{6,8},{7,9},{8,6},{9,7},... | collective-permute-start | bytes 294920 | tf_op jit(solution)/shard_map/ppermute | solution.py:24
  11.4 0.5 collective-permute-start.6
  12.0 3.1 %collective-permute-start.8 = (bf16[32,1536]{1,0:T(8,128)(2,1)S(1)}, bf16[32,1536]{1,0:T(8,128)(2,1)S(1)}, u32[]{:S(2)}, u32[]{:S(2)}) collective-permute-start(bf16[32,1536]{1,0:T(8,128)(2,1)S(1)} %get-tuple-element.33), channel_id=1, source_target_pairs={{0,6},{1,7},{2,4},{3,5},{4,2},{5,3},{6,0},{7,1},{8,14},{9,15},{10,... | collective-permute-start | bytes 294920 | tf_op jit(solution)/shard_map/ppermute | solution.py:24
  15.1 6.1 %collective-permute-start.3 = (bf16[32,1536]{1,0:T(8,128)(2,1)S(1)}, bf16[32,1536]{1,0:T(8,128)(2,1)S(1)}, u32[]{:S(2)}, u32[]{:S(2)}) collective-permute-start(bf16[32,1536]{1,0:T(8,128)(2,1)S(1)} %get-tuple-element.28), channel_id=1, source_target_pairs={{0,10},{1,11},{2,8},{3,9},{4,14},{5,15},{6,12},{7,13},{8,2},{9,3},... | collective-permute-start | bytes 294920 | tf_op jit(solution)/shard_map/ppermute | solution.py:24
  22.2 1.9 %collective-permute-done.8.refs_3_ = bf16[32,1536]{1,0:T(8,128)(2,1)S(1)} collective-permute-done((bf16[32,1536]{1,0:T(8,128)(2,1)S(1)}, bf16[32,1536]{1,0:T(8,128)(2,1)S(1)}, u32[]{:S(2)}, u32[]{:S(2)}) %collective-permute-start.8) | collective-permute-done | bytes 98336 | tf_op jit(solution)/shard_map/ppermute | solution.py:24
  24.1 1.7 %shard_map.68 = (bf16[8,2,16,1536]{3,2,1,0:T(8,128)(2,1)}, f32[32,768]{1,0:T(8,128)S(1)}) custom-call(bf16[2,768,768]{2,1,0:T(8,128)(2,1)S(1)} %get-tuple-element.25.own_ref, bf16[2,768,768]{2,1,0:T(8,128)(2,1)S(1)} %get-tuple-element.26.sibling_ref, bf16[32,1536]{1,0:T(8,128)(2,1)S(1)} %collective-permute-done.5.refs_0_, ...), custom_call_target="tpu_custom_call" | custom-call | tf_op jit(solution)/shard_map/pallas_call | solution.py:216
  25.8 1.8 %collective-permute-done.3.refs_1_ = bf16[32,1536]{1,0:T(8,128)(2,1)S(1)} collective-permute-done((bf16[32,1536]{1,0:T(8,128)(2,1)S(1)}, bf16[32,1536]{1,0:T(8,128)(2,1)S(1)}, u32[]{:S(2)}, u32[]{:S(2)}) %collective-permute-start.3) | collective-permute-done | bytes 98336 | tf_op jit(solution)/shard_map/ppermute | solution.py:24
  27.6 0.8 %collective-permute-done.4.refs_2_ = bf16[32,1536]{1,0:T(8,128)(2,1)S(1)} collective-permute-done((bf16[32,1536]{1,0:T(8,128)(2,1)S(1)}, bf16[32,1536]{1,0:T(8,128)(2,1)S(1)}, u32[]{:S(2)}, u32[]{:S(2)}) %collective-permute-start.4) | collective-permute-done | bytes 98336 | tf_op jit(solution)/shard_map/ppermute | solution.py:24
  28.4 1.6 %shard_map.69 = (bf16[8,2,16,1536]{3,2,1,0:T(8,128)(2,1)}, f32[16,896]{1,0:T(8,128)S(1)}, bf16[16,896]{1,0:T(8,128)(2,1)S(1)}) custom-call(bf16[2,768,768]{2,1,0:T(8,128)(2,1)S(1)} %get-tuple-element.25.own_ref, bf16[2,768,768]{2,1,0:T(8,128)(2,1)S(1)} %get-tuple-element.26.sibling_ref, ...), custom_call_target="tpu_custom_call", output_to_operand_aliasing={{0}: (7, {})} | custom-call | tf_op jit(solution)/shard_map/pallas_call | solution.py:216
  30.1 4.7 %all-to-all-start = ((bf16[8,32,1536]{2,1,0:T(8,128)(2,1)}), bf16[8,32,1536]{2,1,0:T(8,128)(2,1)S(1)}, u32[]{:S(2)}, u32[]{:S(2)}) async-start(bf16[8,32,1536]{2,1,0:T(8,128)(2,1)} %bitcast.4), calls=%async_computation | async-start | bytes 1572864 | tf_op jit(solution)/shard_map/all_to_all | solution.py:230
  34.9 1.2 %collective-permute-done.10 = bf16[16,896]{1,0:T(8,128)(2,1)S(1)} collective-permute-done((bf16[16,896]{1,0:T(8,128)(2,1)S(1)}, bf16[16,896]{1,0:T(8,128)(2,1)S(1)}, u32[]{:S(2)}, u32[]{:S(2)}) %collective-permute-start.10) | collective-permute-done | bytes 28704 | tf_op jit(solution)/shard_map/ppermute | solution.py:24
  36.2 2.0 %collective-permute-start.11 = (bf16[12,896]{1,0:T(8,128)(2,1)S(1)}, bf16[12,896]{1,0:T(8,128)(2,1)S(1)}, u32[]{:S(2)}, u32[]{:S(2)}) collective-permute-start(bf16[12,896]{1,0:T(8,128)(2,1)S(1)} %pad_maximum_fusion), channel_id=1, source_target_pairs={{0,2},{1,3},{2,0},{3,1},{4,6},{5,7},{6,4},{7,5},{8,10},{9,11},{10,... | collective-permute-start | bytes 64520 | tf_op jit(solution)/shard_map/ppermute | solution.py:24
  38.2 2.7 %collective-permute-done.11 = bf16[12,896]{1,0:T(8,128)(2,1)S(1)} collective-permute-done((bf16[12,896]{1,0:T(8,128)(2,1)S(1)}, bf16[12,896]{1,0:T(8,128)(2,1)S(1)}, u32[]{:S(2)}, u32[]{:S(2)}) %collective-permute-start.11) | collective-permute-done | bytes 21536 | tf_op jit(solution)/shard_map/ppermute | solution.py:24
  41.1 4.1 %collective-permute-start.12 = (bf16[8,896]{1,0:T(8,128)(2,1)S(1)}, bf16[8,896]{1,0:T(8,128)(2,1)S(1)}, u32[]{:S(2)}, u32[]{:S(2)}) collective-permute-start(bf16[8,896]{1,0:T(8,128)(2,1)S(1)} %pad_maximum_fusion.2), channel_id=1, source_target_pairs={{0,4},{1,5},{2,6},{3,7},{4,0},{5,1},{6,2},{7,3},{8,12},{9,13},{10,... | collective-permute-start | bytes 43016 | tf_op jit(solution)/shard_map/ppermute | solution.py:24
  45.2 2.3 %collective-permute-done.12.arrived_ref = bf16[8,896]{1,0:T(8,128)(2,1)S(1)} collective-permute-done((bf16[8,896]{1,0:T(8,128)(2,1)S(1)}, bf16[8,896]{1,0:T(8,128)(2,1)S(1)}, u32[]{:S(2)}, u32[]{:S(2)}) %collective-permute-start.12) | collective-permute-done | bytes 14368 | tf_op jit(solution)/shard_map/ppermute | solution.py:24
  47.5 0.9 %shard_map.70.above_ref = f32[4,384]{1,0:T(4,128)S(1)} custom-call(f32[8,896]{1,0:T(8,128)S(1)} %pad_maximum_fusion.1.keep_ref, bf16[8,896]{1,0:T(8,128)(2,1)S(1)} %collective-permute-done.12.arrived_ref, bf16[2,2,384,384]{3,2,1,0:T(8,128)(2,1)S(1)} %copy-done.1), custom_call_target="tpu_custom_call" | custom-call | flops 1 | bytes 1 | tf_op jit(solution)/shard_map/pallas_call | solution.py:216
  48.4 4.8 %all-to-all-done = bf16[8,32,1536]{2,1,0:T(8,128)(2,1)S(1)} async-done(((bf16[8,32,1536]{2,1,0:T(8,128)(2,1)}), bf16[8,32,1536]{2,1,0:T(8,128)(2,1)S(1)}, u32[]{:S(2)}, u32[]{:S(2)}) %all-to-all-start) | async-done | bytes 786464 | tf_op jit(solution)/shard_map/all_to_all | solution.py:230
  53.1 1.0 %shard_map.71 = bf16[52,2,1536]{2,1,0:T(2,128)(2,1)} custom-call(bf16[104,256]{1,0:T(8,128)(2,1)S(1)} %get-tuple-element.22.pick_ref, f32[4,384]{1,0:T(4,128)S(1)} %shard_map.70.above_ref, bf16[256,1536]{1,0:T(8,128)(2,1)S(1)} %bitcast.7), custom_call_target="tpu_custom_call" | custom-call | tf_op jit(solution)/shard_map/pallas_call | solution.py:216
  (33 shorter events, 1.2 us)
Async XLA Ops:
  0.0 6.3 %collective-permute-start = (bf16[2,768,768]{2,1,0:T(8,128)(2,1)}, bf16[2,768,768]{2,1,0:T(8,128)(2,1)S(1)}, u32[]{:S(2)}, u32[]{:S(2)}) collective-permute-start(bf16[2,768,768]{2,1,0:T(8,128)(2,1)} %bitcast.8), channel_id=1, source_target_pairs={{0,1},{1,0},{2,3},{3,2},{4,5},{5,4},{6,7},{7,6},{8,9},{9,8},{10,11... | collective-permute-start | bytes 7077896 | tf_op jit(solution)/shard_map/ppermute | solution.py:24
  1.5 4.8 %collective-permute-start.1 = (bf16[104,128]{1,0:T(8,128)(2,1)S(1)}, bf16[104,128]{1,0:T(8,128)(2,1)S(1)}, u32[]{:S(2)}, u32[]{:S(2)}) collective-permute-start(bf16[104,128]{1,0:T(8,128)(2,1)S(1)} %shard_map.65), channel_id=1, source_target_pairs={{0,16},{16,0},{1,17},{17,1},{2,18},{18,2},{3,19},{19,3},{4,20},{20... | collective-permute-start | bytes 79880 | tf_op jit(solution)/shard_map/ppermute | solution.py:19
  5.1 16.7 %copy-start = (bf16[1,2,768,768]{3,2,1,0:T(8,128)(2,1)S(1)}, bf16[1,2,768,768]{3,2,1,0:T(8,128)(2,1)}, u32[]{:S(2)}) copy-start(bf16[1,2,768,768]{3,2,1,0:T(8,128)(2,1)} %param.10) | copy-start | bytes 7077892
  5.1 0.8 %copy-start.2 = (s32[1,52,1]{1,2,0:T(1,128)S(1)}, s32[1,52,1]{1,2,0:T(1,128)}, u32[]{:S(2)}) copy-start(s32[1,52,1]{1,2,0:T(1,128)} %param.8) | copy-start | bytes 628
  6.7 8.4 %collective-permute-start.5 = (bf16[32,1536]{1,0:T(8,128)(2,1)S(1)}, bf16[32,1536]{1,0:T(8,128)(2,1)S(1)}, u32[]{:S(2)}, u32[]{:S(2)}) collective-permute-start(bf16[32,1536]{1,0:T(8,128)(2,1)S(1)} %get-tuple-element.30), channel_id=1, source_target_pairs={{0,14},{1,15},{2,12},{3,13},{4,10},{5,11},{6,8},{7,9},{8,6},{9,7},... | collective-permute-start | bytes 294920 | tf_op jit(solution)/shard_map/ppermute | solution.py:24
  11.4 9.8 %collective-permute-start.6 = (bf16[32,1536]{1,0:T(8,128)(2,1)S(1)}, bf16[32,1536]{1,0:T(8,128)(2,1)S(1)}, u32[]{:S(2)}, u32[]{:S(2)}) collective-permute-start(bf16[32,1536]{1,0:T(8,128)(2,1)S(1)} %get-tuple-element.31), channel_id=1, source_target_pairs={{0,2},{1,3},{2,0},{3,1},{4,6},{5,7},{6,4},{7,5},{8,10},{9,11},{10,... | collective-permute-start | bytes 294920 | tf_op jit(solution)/shard_map/ppermute | solution.py:24
  11.9 13.9 %collective-permute-start.2 = (bf16[32,1536]{1,0:T(8,128)(2,1)S(1)}, bf16[32,1536]{1,0:T(8,128)(2,1)S(1)}, u32[]{:S(2)}, u32[]{:S(2)}) collective-permute-start(bf16[32,1536]{1,0:T(8,128)(2,1)S(1)} %get-tuple-element.27), channel_id=1, source_target_pairs={{0,12},{1,13},{2,14},{3,15},{4,8},{5,9},{6,10},{7,11},{8,4},{9,5},... | collective-permute-start | bytes 294920 | tf_op jit(solution)/shard_map/ppermute | solution.py:24
  12.0 10.1 %collective-permute-start.7 = (bf16[32,1536]{1,0:T(8,128)(2,1)S(1)}, bf16[32,1536]{1,0:T(8,128)(2,1)S(1)}, u32[]{:S(2)}, u32[]{:S(2)}) collective-permute-start(bf16[32,1536]{1,0:T(8,128)(2,1)S(1)} %get-tuple-element.32), channel_id=1, source_target_pairs={{0,4},{1,5},{2,6},{3,7},{4,0},{5,1},{6,2},{7,3},{8,12},{9,13},{10,... | collective-permute-start | bytes 294920 | tf_op jit(solution)/shard_map/ppermute | solution.py:24
  12.0 12.0 %collective-permute-start.8 = (bf16[32,1536]{1,0:T(8,128)(2,1)S(1)}, bf16[32,1536]{1,0:T(8,128)(2,1)S(1)}, u32[]{:S(2)}, u32[]{:S(2)}) collective-permute-start(bf16[32,1536]{1,0:T(8,128)(2,1)S(1)} %get-tuple-element.33), channel_id=1, source_target_pairs={{0,6},{1,7},{2,4},{3,5},{4,2},{5,3},{6,0},{7,1},{8,14},{9,15},{10,... | collective-permute-start | bytes 294920 | tf_op jit(solution)/shard_map/ppermute | solution.py:24
  15.1 12.5 %collective-permute-start.3 = (bf16[32,1536]{1,0:T(8,128)(2,1)S(1)}, bf16[32,1536]{1,0:T(8,128)(2,1)S(1)}, u32[]{:S(2)}, u32[]{:S(2)}) collective-permute-start(bf16[32,1536]{1,0:T(8,128)(2,1)S(1)} %get-tuple-element.28), channel_id=1, source_target_pairs={{0,10},{1,11},{2,8},{3,9},{4,14},{5,15},{6,12},{7,13},{8,2},{9,3},... | collective-permute-start | bytes 294920 | tf_op jit(solution)/shard_map/ppermute | solution.py:24
  21.2 7.2 %collective-permute-start.4 = (bf16[32,1536]{1,0:T(8,128)(2,1)S(1)}, bf16[32,1536]{1,0:T(8,128)(2,1)S(1)}, u32[]{:S(2)}, u32[]{:S(2)}) collective-permute-start(bf16[32,1536]{1,0:T(8,128)(2,1)S(1)} %get-tuple-element.29), channel_id=1, source_target_pairs={{0,8},{1,9},{2,10},{3,11},{4,12},{5,13},{6,14},{7,15},{8,0},{9,1},... | collective-permute-start | bytes 294920 | tf_op jit(solution)/shard_map/ppermute | solution.py:24
  30.0 17.5 %copy-start.1 = (bf16[2,2,384,384]{3,2,1,0:T(8,128)(2,1)S(1)}, bf16[2,2,384,384]{3,2,1,0:T(8,128)(2,1)}, u32[]{:S(2)}) copy-start(bf16[2,2,384,384]{3,2,1,0:T(8,128)(2,1)} %factors_ref.1) | copy-start | bytes 3538948
  30.0 4.8 %collective-permute-start.9 = (bf16[16,896]{1,0:T(8,128)(2,1)S(1)}, bf16[16,896]{1,0:T(8,128)(2,1)S(1)}, u32[]{:S(2)}, u32[]{:S(2)}) collective-permute-start(bf16[16,896]{1,0:T(8,128)(2,1)S(1)} %get-tuple-element.37), channel_id=1, source_target_pairs={{0,8},{1,9},{2,10},{3,11},{4,12},{5,13},{6,14},{7,15},{8,0},{9,1},... | collective-permute-start | bytes 86024 | tf_op jit(solution)/shard_map/ppermute | solution.py:24
  30.1 23.1 %all-to-all-start = ((bf16[8,32,1536]{2,1,0:T(8,128)(2,1)}), bf16[8,32,1536]{2,1,0:T(8,128)(2,1)S(1)}, u32[]{:S(2)}, u32[]{:S(2)}) async-start(bf16[8,32,1536]{2,1,0:T(8,128)(2,1)} %bitcast.4), calls=%async_computation | async-start | bytes 1572864 | tf_op jit(solution)/shard_map/all_to_all | solution.py:230
  34.8 1.3 %collective-permute-start.10 = (bf16[16,896]{1,0:T(8,128)(2,1)S(1)}, bf16[16,896]{1,0:T(8,128)(2,1)S(1)}, u32[]{:S(2)}, u32[]{:S(2)}) collective-permute-start(bf16[16,896]{1,0:T(8,128)(2,1)S(1)} %fusion), channel_id=1, source_target_pairs={{0,1},{1,0},{2,3},{3,2},{4,5},{5,4},{6,7},{7,6},{8,9},{9,8},{10,11... | collective-permute-start | bytes 86024 | tf_op jit(solution)/shard_map/ppermute | solution.py:24
  36.2 4.8 %collective-permute-start.11 = (bf16[12,896]{1,0:T(8,128)(2,1)S(1)}, bf16[12,896]{1,0:T(8,128)(2,1)S(1)}, u32[]{:S(2)}, u32[]{:S(2)}) collective-permute-start(bf16[12,896]{1,0:T(8,128)(2,1)S(1)} %pad_maximum_fusion), channel_id=1, source_target_pairs={{0,2},{1,3},{2,0},{3,1},{4,6},{5,7},{6,4},{7,5},{8,10},{9,11},{10,... | collective-permute-start | bytes 64520 | tf_op jit(solution)/shard_map/ppermute | solution.py:24
  41.1 6.4 %collective-permute-start.12 = (bf16[8,896]{1,0:T(8,128)(2,1)S(1)}, bf16[8,896]{1,0:T(8,128)(2,1)S(1)}, u32[]{:S(2)}, u32[]{:S(2)}) collective-permute-start(bf16[8,896]{1,0:T(8,128)(2,1)S(1)} %pad_maximum_fusion.2), channel_id=1, source_target_pairs={{0,4},{1,5},{2,6},{3,7},{4,0},{5,1},{6,2},{7,3},{8,12},{9,13},{10,... | collective-permute-start | bytes 43016 | tf_op jit(solution)/shard_map/ppermute | solution.py:24

commit v9 on v8

--- a/solution.py
+++ b/solution.py
@@ -76,7 +76,7 @@
     first = lax.broadcasted_iota(jnp.int32, face_re.shape, 2) < front
     face = jnp.where(first, pltpu.roll(face_re, front, 2), face_im)
     other = jnp.where(first, pltpu.roll(face_im, front, 2), face_re)
-    out_ref[...] = (by_same * face + by_other * other).reshape(out_ref.shape).astype(BF16)
+    out_ref[...] = (by_same * face + by_other * other).reshape(out_ref.shape).astype(out_ref.dtype)
 
 
 def dispatch_kernel(front, pick_ref, rows_ref, arriving_ref, _, *refs):
@@ -167,11 +167,11 @@
         else:
             total = sums[part] + before_ref[:, columns]
             keep_ref[:, columns] = total[: count // 2]
-            send_ref[:, columns] = total[count // 2 :].astype(BF16)
+            send_ref[:, columns] = total[count // 2 :].astype(send_ref.dtype)
     if code_ref is not None:
         codes = jnp.where(here, code_ref[0, 0].astype(F32), 0.0)
         keep_ref[:, 2 * sep_n :] = codes[: count // 2]
-        send_ref[:, 2 * sep_n :] = codes[count // 2 :].astype(BF16)
+        send_ref[:, 2 * sep_n :] = codes[count // 2 :].astype(send_ref.dtype)
     for copy in copies:
         copy.wait()
 
@@ -249,7 +249,8 @@
             if level <= bit:
                 sizes[level] //= 2
         keep = jnp.concatenate(mine)
-        arrived = exchange(jnp.concatenate(other).astype(BF16), 2 << bit if bit >= 0 else 1)
+        other = jnp.concatenate(other)
+        arrived = exchange(other, 2 << bit) if bit >= 0 else exchange(other.astype(BF16), 1)
     return keep, arrived
 
 
@@ -324,7 +325,7 @@
     )
     solved, keep, send = call(
         functools.partial(leaf_kernel, shots, sep_n, last, pairs),
-        [jax.ShapeDtypeStruct(halves, BF16), nodes, jax.ShapeDtypeStruct(nodes.shape, BF16)],
+        [jax.ShapeDtypeStruct(halves, BF16), nodes, nodes],
         (own, sibling, *(arrived[at] for at in last), sep_code % sep_lib, sums, solved),
         smem=(2 + len(last),),
         hbm=(4 + len(last),),

time: 54.5 us -> 54.5 us (level)
  waiting for transfers between devices: 15.6 us -> 16.4 us
  starting transfers between devices: 28.4 us -> 27.6 us
    ppermute x12, waiting for transfers between devices: 10.8 us -> 12.3 us  [exchange(): return lax.ppermute(value, 'leaf', pairs)]
    ppermute x12, starting transfers between devices: 21.2 us -> 20.4 us  [exchange(): return lax.ppermute(value, 'leaf', pairs)]
    all_to_all x1, waiting for transfers between devices: 4.75 us -> 4.08 us  [to_pairs(): lax.all_to_all(value, 'leaf', 0, 0, tiled=True, axis_index_groups=groups)]
where the time goes in v9:
time: 54.5 us; the launch traced here: 54.2 us
  starting transfers between devices  27.6 us (51%)
  waiting for transfers between devices  16.4 us (30%)
  Pallas kernels  7.23 us (13%)
  local copies, waits for them, and re-layouts  1.94 us (4%)
  between operations  0.87 us (2%)
    ppermute x12, starting transfers between devices, exchange(): return lax.ppermute(value, 'leaf', pairs)  20.4 us
    ppermute x12, waiting for transfers between devices, exchange(): return lax.ppermute(value, 'leaf', pairs)  12.3 us
    pallas_call x8, Pallas kernels, call(): pl.pallas_call(kernel, out_shape=out_shape, in_specs=[pl.BlockSpec(memory...  7.23 us
    all_to_all x1, starting transfers between devices, to_pairs(): lax.all_to_all(value, 'leaf', 0, 0, tiled=True, axis_index_groups=groups)  4.7 us
    all_to_all x1, waiting for transfers between devices, to_pairs(): lax.all_to_all(value, 'leaf', 0, 0, tiled=True, axis_index_groups=groups)  4.08 us
    ppermute x1, starting transfers between devices, around(): lax.ppermute(value, axis, [(at, (at + 1) % count) for at in range(count)])  2.55 us
  transfers between devices with their start and end apart: 14, of which 8 were waited for; matrix products, arithmetic and copies ran while one was open for 2% of the time, Pallas kernels for 8%

profile of v9, /device:TPU:0, one launch (start us, length us, event | category | flops | bytes accessed | tf_op | source)
XLA Modules:
  0.0 54.2 jit_solution(702425947505942108)
XLA Ops:
  0.0 0.5 collective-permute-start
  0.5 1.0 %shard_map.65 = bf16[104,128]{1,0:T(8,128)(2,1)S(1)} custom-call(bf16[52,2,1536]{2,1,0:T(2,128)(2,1)} %bitcast.11, f32[52,1,128]{2,1,0:T(1,128)} %bitcast.12), custom_call_target="tpu_custom_call" | custom-call | tf_op jit(solution)/shard_map/pallas_call | solution.py:216
  1.5 2.6 %collective-permute-start.1 = (bf16[104,128]{1,0:T(8,128)(2,1)S(1)}, bf16[104,128]{1,0:T(8,128)(2,1)S(1)}, u32[]{:S(2)}, u32[]{:S(2)}) collective-permute-start(bf16[104,128]{1,0:T(8,128)(2,1)S(1)} %shard_map.65), channel_id=1, source_target_pairs={{0,16},{16,0},{1,17},{17,1},{2,18},{18,2},{3,19},{19,3},{4,20},{20... | collective-permute-start | bytes 79880 | tf_op jit(solution)/shard_map/ppermute | solution.py:19
  4.0 1.1 %reshape_squeeze.7.rows_ref = bf16[104,1536]{1,0:T(8,128)(2,1)S(1)} reshape(bf16[1,52,2,1536]{3,2,1,0:T(2,128)(2,1)} %param.6) | data formatting | bytes 638976 | tf_op jit(solution)/shard_map/reshape;squeeze | solution.py:300
  5.1 0.8 %copy-done.2 = s32[1,52,1]{1,2,0:T(1,128)S(1)} copy-done((s32[1,52,1]{1,2,0:T(1,128)S(1)}, s32[1,52,1]{1,2,0:T(1,128)}, u32[]{:S(2)}) %copy-start.2) | copy-done | bytes 232
  6.7 4.7 %collective-permute-start.5 = (bf16[32,1536]{1,0:T(8,128)(2,1)S(1)}, bf16[32,1536]{1,0:T(8,128)(2,1)S(1)}, u32[]{:S(2)}, u32[]{:S(2)}) collective-permute-start(bf16[32,1536]{1,0:T(8,128)(2,1)S(1)} %get-tuple-element.30), channel_id=1, source_target_pairs={{0,14},{1,15},{2,12},{3,13},{4,10},{5,11},{6,8},{7,9},{8,6},{9,7},... | collective-permute-start | bytes 294920 | tf_op jit(solution)/shard_map/ppermute | solution.py:24
  11.4 0.5 collective-permute-start.6
  12.0 3.1 %collective-permute-start.8 = (bf16[32,1536]{1,0:T(8,128)(2,1)S(1)}, bf16[32,1536]{1,0:T(8,128)(2,1)S(1)}, u32[]{:S(2)}, u32[]{:S(2)}) collective-permute-start(bf16[32,1536]{1,0:T(8,128)(2,1)S(1)} %get-tuple-element.33), channel_id=1, source_target_pairs={{0,6},{1,7},{2,4},{3,5},{4,2},{5,3},{6,0},{7,1},{8,14},{9,15},{10,... | collective-permute-start | bytes 294920 | tf_op jit(solution)/shard_map/ppermute | solution.py:24
  15.1 6.1 %collective-permute-start.3 = (bf16[32,1536]{1,0:T(8,128)(2,1)S(1)}, bf16[32,1536]{1,0:T(8,128)(2,1)S(1)}, u32[]{:S(2)}, u32[]{:S(2)}) collective-permute-start(bf16[32,1536]{1,0:T(8,128)(2,1)S(1)} %get-tuple-element.28), channel_id=1, source_target_pairs={{0,10},{1,11},{2,8},{3,9},{4,14},{5,15},{6,12},{7,13},{8,2},{9,3},... | collective-permute-start | bytes 294920 | tf_op jit(solution)/shard_map/ppermute | solution.py:24
  22.2 1.9 %collective-permute-done.8.refs_3_ = bf16[32,1536]{1,0:T(8,128)(2,1)S(1)} collective-permute-done((bf16[32,1536]{1,0:T(8,128)(2,1)S(1)}, bf16[32,1536]{1,0:T(8,128)(2,1)S(1)}, u32[]{:S(2)}, u32[]{:S(2)}) %collective-permute-start.8) | collective-permute-done | bytes 98336 | tf_op jit(solution)/shard_map/ppermute | solution.py:24
  24.1 1.7 %shard_map.68 = (bf16[8,2,16,1536]{3,2,1,0:T(8,128)(2,1)}, f32[32,768]{1,0:T(8,128)S(1)}) custom-call(bf16[2,768,768]{2,1,0:T(8,128)(2,1)S(1)} %get-tuple-element.25.own_ref, bf16[2,768,768]{2,1,0:T(8,128)(2,1)S(1)} %get-tuple-element.26.sibling_ref, bf16[32,1536]{1,0:T(8,128)(2,1)S(1)} %collective-permute-done.5.refs_0_, ...), custom_call_target="tpu_custom_call" | custom-call | tf_op jit(solution)/shard_map/pallas_call | solution.py:216
  25.8 1.8 %collective-permute-done.3.refs_1_ = bf16[32,1536]{1,0:T(8,128)(2,1)S(1)} collective-permute-done((bf16[32,1536]{1,0:T(8,128)(2,1)S(1)}, bf16[32,1536]{1,0:T(8,128)(2,1)S(1)}, u32[]{:S(2)}, u32[]{:S(2)}) %collective-permute-start.3) | collective-permute-done | bytes 98336 | tf_op jit(solution)/shard_map/ppermute | solution.py:24
  27.6 0.8 %collective-permute-done.4.refs_2_ = bf16[32,1536]{1,0:T(8,128)(2,1)S(1)} collective-permute-done((bf16[32,1536]{1,0:T(8,128)(2,1)S(1)}, bf16[32,1536]{1,0:T(8,128)(2,1)S(1)}, u32[]{:S(2)}, u32[]{:S(2)}) %collective-permute-start.4) | collective-permute-done | bytes 98336 | tf_op jit(solution)/shard_map/ppermute | solution.py:24
  28.4 1.6 %shard_map.69 = (bf16[8,2,16,1536]{3,2,1,0:T(8,128)(2,1)}, f32[16,896]{1,0:T(8,128)S(1)}, f32[16,896]{1,0:T(8,128)S(1)}) custom-call(bf16[2,768,768]{2,1,0:T(8,128)(2,1)S(1)} %get-tuple-element.25.own_ref, bf16[2,768,768]{2,1,0:T(8,128)(2,1)S(1)} %get-tuple-element.26.sibling_ref, ...), custom_call_target="tpu_custom_call", output_to_operand_aliasing={{0}: (7, {})} | custom-call | tf_op jit(solution)/shard_map/pallas_call | solution.py:216
  30.1 4.7 %all-to-all-start = ((bf16[8,32,1536]{2,1,0:T(8,128)(2,1)}), bf16[8,32,1536]{2,1,0:T(8,128)(2,1)S(1)}, u32[]{:S(2)}, u32[]{:S(2)}) async-start(bf16[8,32,1536]{2,1,0:T(8,128)(2,1)} %bitcast.4), calls=%async_computation | async-start | bytes 1572864 | tf_op jit(solution)/shard_map/all_to_all | solution.py:230
  34.8 0.6 %collective-permute-done.9 = f32[16,896]{1,0:T(8,128)S(1)} collective-permute-done((f32[16,896]{1,0:T(8,128)S(1)}, f32[16,896]{1,0:T(8,128)S(1)}, u32[]{:S(2)}, u32[]{:S(2)}) %collective-permute-start.9) | collective-permute-done | bytes 57376 | tf_op jit(solution)/shard_map/ppermute | solution.py:24
  35.4 1.2 %collective-permute-done.10 = bf16[16,896]{1,0:T(8,128)(2,1)S(1)} collective-permute-done((bf16[16,896]{1,0:T(8,128)(2,1)S(1)}, bf16[16,896]{1,0:T(8,128)(2,1)S(1)}, u32[]{:S(2)}, u32[]{:S(2)}) %collective-permute-start.10) | collective-permute-done | bytes 28704 | tf_op jit(solution)/shard_map/ppermute | solution.py:24
  36.7 1.5 %collective-permute-start.11 = (f32[12,896]{1,0:T(8,128)S(1)}, f32[12,896]{1,0:T(8,128)S(1)}, u32[]{:S(2)}, u32[]{:S(2)}) collective-permute-start(f32[12,896]{1,0:T(8,128)S(1)} %pad_maximum_fusion), channel_id=1, source_target_pairs={{0,2},{1,3},{2,0},{3,1},{4,6},{5,7},{6,4},{7,5},{8,10},{9,11},{10,... | collective-permute-start | bytes 129032 | tf_op jit(solution)/shard_map/ppermute | solution.py:24
  38.2 3.5 %collective-permute-done.11 = f32[12,896]{1,0:T(8,128)S(1)} collective-permute-done((f32[12,896]{1,0:T(8,128)S(1)}, f32[12,896]{1,0:T(8,128)S(1)}, u32[]{:S(2)}, u32[]{:S(2)}) %collective-permute-start.11) | collective-permute-done | bytes 43040 | tf_op jit(solution)/shard_map/ppermute | solution.py:24
  41.8 3.8 %collective-permute-start.12 = (f32[8,896]{1,0:T(8,128)S(1)}, f32[8,896]{1,0:T(8,128)S(1)}, u32[]{:S(2)}, u32[]{:S(2)}) collective-permute-start(f32[8,896]{1,0:T(8,128)S(1)} %pad_maximum_fusion.2), channel_id=1, source_target_pairs={{0,4},{1,5},{2,6},{3,7},{4,0},{5,1},{6,2},{7,3},{8,12},{9,13},{10,... | collective-permute-start | bytes 86024 | tf_op jit(solution)/shard_map/ppermute | solution.py:24
  45.5 2.6 %collective-permute-done.12.arrived_ref = f32[8,896]{1,0:T(8,128)S(1)} collective-permute-done((f32[8,896]{1,0:T(8,128)S(1)}, f32[8,896]{1,0:T(8,128)S(1)}, u32[]{:S(2)}, u32[]{:S(2)}) %collective-permute-start.12) | collective-permute-done | bytes 28704 | tf_op jit(solution)/shard_map/ppermute | solution.py:24
  48.2 0.9 %shard_map.70.above_ref = f32[4,384]{1,0:T(4,128)S(1)} custom-call(f32[8,896]{1,0:T(8,128)S(1)} %pad_maximum_fusion.1.keep_ref, f32[8,896]{1,0:T(8,128)S(1)} %collective-permute-done.12.arrived_ref, bf16[2,2,384,384]{3,2,1,0:T(8,128)(2,1)S(1)} %copy-done.1), custom_call_target="tpu_custom_call" | custom-call | flops 1 | bytes 1 | tf_op jit(solution)/shard_map/pallas_call | solution.py:216
  49.1 4.1 %all-to-all-done = bf16[8,32,1536]{2,1,0:T(8,128)(2,1)S(1)} async-done(((bf16[8,32,1536]{2,1,0:T(8,128)(2,1)}), bf16[8,32,1536]{2,1,0:T(8,128)(2,1)S(1)}, u32[]{:S(2)}, u32[]{:S(2)}) %all-to-all-start) | async-done | bytes 786464 | tf_op jit(solution)/shard_map/all_to_all | solution.py:230
  53.1 1.0 %shard_map.71 = bf16[52,2,1536]{2,1,0:T(2,128)(2,1)} custom-call(bf16[104,256]{1,0:T(8,128)(2,1)S(1)} %get-tuple-element.22.pick_ref, f32[4,384]{1,0:T(4,128)S(1)} %shard_map.70.above_ref, bf16[256,1536]{1,0:T(8,128)(2,1)S(1)} %bitcast.7), custom_call_target="tpu_custom_call" | custom-call | tf_op jit(solution)/shard_map/pallas_call | solution.py:216
  (31 shorter events, 1.5 us)
Async XLA Ops:
  0.0 6.3 %collective-permute-start = (bf16[2,768,768]{2,1,0:T(8,128)(2,1)}, bf16[2,768,768]{2,1,0:T(8,128)(2,1)S(1)}, u32[]{:S(2)}, u32[]{:S(2)}) collective-permute-start(bf16[2,768,768]{2,1,0:T(8,128)(2,1)} %bitcast.8), channel_id=1, source_target_pairs={{0,1},{1,0},{2,3},{3,2},{4,5},{5,4},{6,7},{7,6},{8,9},{9,8},{10,11... | collective-permute-start | bytes 7077896 | tf_op jit(solution)/shard_map/ppermute | solution.py:24
  1.5 4.8 %collective-permute-start.1 = (bf16[104,128]{1,0:T(8,128)(2,1)S(1)}, bf16[104,128]{1,0:T(8,128)(2,1)S(1)}, u32[]{:S(2)}, u32[]{:S(2)}) collective-permute-start(bf16[104,128]{1,0:T(8,128)(2,1)S(1)} %shard_map.65), channel_id=1, source_target_pairs={{0,16},{16,0},{1,17},{17,1},{2,18},{18,2},{3,19},{19,3},{4,20},{20... | collective-permute-start | bytes 79880 | tf_op jit(solution)/shard_map/ppermute | solution.py:19
  5.1 16.7 %copy-start = (bf16[1,2,768,768]{3,2,1,0:T(8,128)(2,1)S(1)}, bf16[1,2,768,768]{3,2,1,0:T(8,128)(2,1)}, u32[]{:S(2)}) copy-start(bf16[1,2,768,768]{3,2,1,0:T(8,128)(2,1)} %param.10) | copy-start | bytes 7077892
  5.1 0.8 %copy-start.2 = (s32[1,52,1]{1,2,0:T(1,128)S(1)}, s32[1,52,1]{1,2,0:T(1,128)}, u32[]{:S(2)}) copy-start(s32[1,52,1]{1,2,0:T(1,128)} %param.8) | copy-start | bytes 628
  6.7 8.4 %collective-permute-start.5 = (bf16[32,1536]{1,0:T(8,128)(2,1)S(1)}, bf16[32,1536]{1,0:T(8,128)(2,1)S(1)}, u32[]{:S(2)}, u32[]{:S(2)}) collective-permute-start(bf16[32,1536]{1,0:T(8,128)(2,1)S(1)} %get-tuple-element.30), channel_id=1, source_target_pairs={{0,14},{1,15},{2,12},{3,13},{4,10},{5,11},{6,8},{7,9},{8,6},{9,7},... | collective-permute-start | bytes 294920 | tf_op jit(solution)/shard_map/ppermute | solution.py:24
  11.4 9.8 %collective-permute-start.6 = (bf16[32,1536]{1,0:T(8,128)(2,1)S(1)}, bf16[32,1536]{1,0:T(8,128)(2,1)S(1)}, u32[]{:S(2)}, u32[]{:S(2)}) collective-permute-start(bf16[32,1536]{1,0:T(8,128)(2,1)S(1)} %get-tuple-element.31), channel_id=1, source_target_pairs={{0,2},{1,3},{2,0},{3,1},{4,6},{5,7},{6,4},{7,5},{8,10},{9,11},{10,... | collective-permute-start | bytes 294920 | tf_op jit(solution)/shard_map/ppermute | solution.py:24
  11.9 13.9 %collective-permute-start.2 = (bf16[32,1536]{1,0:T(8,128)(2,1)S(1)}, bf16[32,1536]{1,0:T(8,128)(2,1)S(1)}, u32[]{:S(2)}, u32[]{:S(2)}) collective-permute-start(bf16[32,1536]{1,0:T(8,128)(2,1)S(1)} %get-tuple-element.27), channel_id=1, source_target_pairs={{0,12},{1,13},{2,14},{3,15},{4,8},{5,9},{6,10},{7,11},{8,4},{9,5},... | collective-permute-start | bytes 294920 | tf_op jit(solution)/shard_map/ppermute | solution.py:24
  12.0 10.1 %collective-permute-start.7 = (bf16[32,1536]{1,0:T(8,128)(2,1)S(1)}, bf16[32,1536]{1,0:T(8,128)(2,1)S(1)}, u32[]{:S(2)}, u32[]{:S(2)}) collective-permute-start(bf16[32,1536]{1,0:T(8,128)(2,1)S(1)} %get-tuple-element.32), channel_id=1, source_target_pairs={{0,4},{1,5},{2,6},{3,7},{4,0},{5,1},{6,2},{7,3},{8,12},{9,13},{10,... | collective-permute-start | bytes 294920 | tf_op jit(solution)/shard_map/ppermute | solution.py:24
  12.0 12.0 %collective-permute-start.8 = (bf16[32,1536]{1,0:T(8,128)(2,1)S(1)}, bf16[32,1536]{1,0:T(8,128)(2,1)S(1)}, u32[]{:S(2)}, u32[]{:S(2)}) collective-permute-start(bf16[32,1536]{1,0:T(8,128)(2,1)S(1)} %get-tuple-element.33), channel_id=1, source_target_pairs={{0,6},{1,7},{2,4},{3,5},{4,2},{5,3},{6,0},{7,1},{8,14},{9,15},{10,... | collective-permute-start | bytes 294920 | tf_op jit(solution)/shard_map/ppermute | solution.py:24
  15.1 12.5 %collective-permute-start.3 = (bf16[32,1536]{1,0:T(8,128)(2,1)S(1)}, bf16[32,1536]{1,0:T(8,128)(2,1)S(1)}, u32[]{:S(2)}, u32[]{:S(2)}) collective-permute-start(bf16[32,1536]{1,0:T(8,128)(2,1)S(1)} %get-tuple-element.28), channel_id=1, source_target_pairs={{0,10},{1,11},{2,8},{3,9},{4,14},{5,15},{6,12},{7,13},{8,2},{9,3},... | collective-permute-start | bytes 294920 | tf_op jit(solution)/shard_map/ppermute | solution.py:24
  21.2 7.2 %collective-permute-start.4 = (bf16[32,1536]{1,0:T(8,128)(2,1)S(1)}, bf16[32,1536]{1,0:T(8,128)(2,1)S(1)}, u32[]{:S(2)}, u32[]{:S(2)}) collective-permute-start(bf16[32,1536]{1,0:T(8,128)(2,1)S(1)} %get-tuple-element.29), channel_id=1, source_target_pairs={{0,8},{1,9},{2,10},{3,11},{4,12},{5,13},{6,14},{7,15},{8,0},{9,1},... | collective-permute-start | bytes 294920 | tf_op jit(solution)/shard_map/ppermute | solution.py:24
  30.0 18.2 %copy-start.1 = (bf16[2,2,384,384]{3,2,1,0:T(8,128)(2,1)S(1)}, bf16[2,2,384,384]{3,2,1,0:T(8,128)(2,1)}, u32[]{:S(2)}) copy-start(bf16[2,2,384,384]{3,2,1,0:T(8,128)(2,1)} %factors_ref.1) | copy-start | bytes 3538948
  30.0 5.4 %collective-permute-start.9 = (f32[16,896]{1,0:T(8,128)S(1)}, f32[16,896]{1,0:T(8,128)S(1)}, u32[]{:S(2)}, u32[]{:S(2)}) collective-permute-start(f32[16,896]{1,0:T(8,128)S(1)} %get-tuple-element.37), channel_id=1, source_target_pairs={{0,8},{1,9},{2,10},{3,11},{4,12},{5,13},{6,14},{7,15},{8,0},{9,1},... | collective-permute-start | bytes 172040 | tf_op jit(solution)/shard_map/ppermute | solution.py:24
  30.1 23.1 %all-to-all-start = ((bf16[8,32,1536]{2,1,0:T(8,128)(2,1)}), bf16[8,32,1536]{2,1,0:T(8,128)(2,1)S(1)}, u32[]{:S(2)}, u32[]{:S(2)}) async-start(bf16[8,32,1536]{2,1,0:T(8,128)(2,1)} %bitcast.4), calls=%async_computation | async-start | bytes 1572864 | tf_op jit(solution)/shard_map/all_to_all | solution.py:230
  35.4 1.3 %collective-permute-start.10 = (bf16[16,896]{1,0:T(8,128)(2,1)S(1)}, bf16[16,896]{1,0:T(8,128)(2,1)S(1)}, u32[]{:S(2)}, u32[]{:S(2)}) collective-permute-start(bf16[16,896]{1,0:T(8,128)(2,1)S(1)} %get-tuple-element.39), channel_id=1, source_target_pairs={{0,1},{1,0},{2,3},{3,2},{4,5},{5,4},{6,7},{7,6},{8,9},{9,8},{10,11... | collective-permute-start | bytes 86024 | tf_op jit(solution)/shard_map/ppermute | solution.py:24
  36.7 5.0 %collective-permute-start.11 = (f32[12,896]{1,0:T(8,128)S(1)}, f32[12,896]{1,0:T(8,128)S(1)}, u32[]{:S(2)}, u32[]{:S(2)}) collective-permute-start(f32[12,896]{1,0:T(8,128)S(1)} %pad_maximum_fusion), channel_id=1, source_target_pairs={{0,2},{1,3},{2,0},{3,1},{4,6},{5,7},{6,4},{7,5},{8,10},{9,11},{10,... | collective-permute-start | bytes 129032 | tf_op jit(solution)/shard_map/ppermute | solution.py:24
  41.8 6.4 %collective-permute-start.12 = (f32[8,896]{1,0:T(8,128)S(1)}, f32[8,896]{1,0:T(8,128)S(1)}, u32[]{:S(2)}, u32[]{:S(2)}) collective-permute-start(f32[8,896]{1,0:T(8,128)S(1)} %pad_maximum_fusion.2), channel_id=1, source_target_pairs={{0,4},{1,5},{2,6},{3,7},{4,0},{5,1},{6,2},{7,3},{8,12},{9,13},{10,... | collective-permute-start | bytes 86024 | tf_op jit(solution)/shard_map/ppermute | solution.py:24

commit v10 on v9

--- a/solution.py
+++ b/solution.py
@@ -152,7 +152,6 @@
             columns = pl.ds(part * leaf_n, leaf_n)
             for at in range(members):
                 solved_ref[at, entry, :, columns] = solved[at * size : (at + 1) * size]
-            sums[part] += dot(member, solved[:, :sep_n])
         for at, block in enumerate(group):
             copies.append(
                 pltpu.make_async_copy(
@@ -160,6 +159,8 @@
                 )
             )
             copies[-1].start()
+        for part in range(2):
+            sums[part] += dot(member, both[part * half : (part + 1) * half, :sep_n])
     for part in range(2):
         columns = slice(part * sep_n, (part + 1) * sep_n)
         if code_ref is None:

time: 54.5 us -> 54.5 us (level)
  no operation moved by 1% of the time
where the time goes in v10:
time: 54.5 us; the launch traced here: 54.2 us
  starting transfers between devices  27.6 us (51%)
  waiting for transfers between devices  16.4 us (30%)
  Pallas kernels  7.23 us (13%)
  local copies, waits for them, and re-layouts  1.94 us (4%)
  between operations  0.87 us (2%)
    ppermute x12, starting transfers between devices, exchange(): return lax.ppermute(value, 'leaf', pairs)  20.4 us
    ppermute x12, waiting for transfers between devices, exchange(): return lax.ppermute(value, 'leaf', pairs)  12.3 us
    pallas_call x8, Pallas kernels, call(): pl.pallas_call(kernel, out_shape=out_shape, in_specs=[pl.BlockSpec(memory...  7.23 us
    all_to_all x1, starting transfers between devices, to_pairs(): lax.all_to_all(value, 'leaf', 0, 0, tiled=True, axis_index_groups=groups)  4.7 us
    all_to_all x1, waiting for transfers between devices, to_pairs(): lax.all_to_all(value, 'leaf', 0, 0, tiled=True, axis_index_groups=groups)  4.08 us
    ppermute x1, starting transfers between devices, around(): lax.ppermute(value, axis, [(at, (at + 1) % count) for at in range(count)])  2.55 us
  transfers between devices with their start and end apart: 14, of which 8 were waited for; matrix products, arithmetic and copies ran while one was open for 2% of the time, Pallas kernels for 8%

profile of v10, /device:TPU:0, one launch (start us, length us, event | category | flops | bytes accessed | tf_op | source)
XLA Modules:
  0.0 54.2 jit_solution(702425947505942108)
XLA Ops:
  0.0 0.5 collective-permute-start
  0.5 1.0 %shard_map.65 = bf16[104,128]{1,0:T(8,128)(2,1)S(1)} custom-call(bf16[52,2,1536]{2,1,0:T(2,128)(2,1)} %bitcast.11, f32[52,1,128]{2,1,0:T(1,128)} %bitcast.12), custom_call_target="tpu_custom_call" | custom-call | tf_op jit(solution)/shard_map/pallas_call | solution.py:217
  1.5 2.6 %collective-permute-start.1 = (bf16[104,128]{1,0:T(8,128)(2,1)S(1)}, bf16[104,128]{1,0:T(8,128)(2,1)S(1)}, u32[]{:S(2)}, u32[]{:S(2)}) collective-permute-start(bf16[104,128]{1,0:T(8,128)(2,1)S(1)} %shard_map.65), channel_id=1, source_target_pairs={{0,16},{16,0},{1,17},{17,1},{2,18},{18,2},{3,19},{19,3},{4,20},{20... | collective-permute-start | bytes 79880 | tf_op jit(solution)/shard_map/ppermute | solution.py:19
  4.0 1.1 %reshape_squeeze.7.rows_ref = bf16[104,1536]{1,0:T(8,128)(2,1)S(1)} reshape(bf16[1,52,2,1536]{3,2,1,0:T(2,128)(2,1)} %param.6) | data formatting | bytes 638976 | tf_op jit(solution)/shard_map/reshape;squeeze | solution.py:301
  5.1 0.8 %copy-done.2 = s32[1,52,1]{1,2,0:T(1,128)S(1)} copy-done((s32[1,52,1]{1,2,0:T(1,128)S(1)}, s32[1,52,1]{1,2,0:T(1,128)}, u32[]{:S(2)}) %copy-start.2) | copy-done | bytes 232
  6.7 4.7 %collective-permute-start.5 = (bf16[32,1536]{1,0:T(8,128)(2,1)S(1)}, bf16[32,1536]{1,0:T(8,128)(2,1)S(1)}, u32[]{:S(2)}, u32[]{:S(2)}) collective-permute-start(bf16[32,1536]{1,0:T(8,128)(2,1)S(1)} %get-tuple-element.30), channel_id=1, source_target_pairs={{0,14},{1,15},{2,12},{3,13},{4,10},{5,11},{6,8},{7,9},{8,6},{9,7},... | collective-permute-start | bytes 294920 | tf_op jit(solution)/shard_map/ppermute | solution.py:24
  11.4 0.5 collective-permute-start.6
  12.0 3.1 %collective-permute-start.8 = (bf16[32,1536]{1,0:T(8,128)(2,1)S(1)}, bf16[32,1536]{1,0:T(8,128)(2,1)S(1)}, u32[]{:S(2)}, u32[]{:S(2)}) collective-permute-start(bf16[32,1536]{1,0:T(8,128)(2,1)S(1)} %get-tuple-element.33), channel_id=1, source_target_pairs={{0,6},{1,7},{2,4},{3,5},{4,2},{5,3},{6,0},{7,1},{8,14},{9,15},{10,... | collective-permute-start | bytes 294920 | tf_op jit(solution)/shard_map/ppermute | solution.py:24
  15.1 6.1 %collective-permute-start.3 = (bf16[32,1536]{1,0:T(8,128)(2,1)S(1)}, bf16[32,1536]{1,0:T(8,128)(2,1)S(1)}, u32[]{:S(2)}, u32[]{:S(2)}) collective-permute-start(bf16[32,1536]{1,0:T(8,128)(2,1)S(1)} %get-tuple-element.28), channel_id=1, source_target_pairs={{0,10},{1,11},{2,8},{3,9},{4,14},{5,15},{6,12},{7,13},{8,2},{9,3},... | collective-permute-start | bytes 294920 | tf_op jit(solution)/shard_map/ppermute | solution.py:24
  22.2 1.9 %collective-permute-done.8.refs_3_ = bf16[32,1536]{1,0:T(8,128)(2,1)S(1)} collective-permute-done((bf16[32,1536]{1,0:T(8,128)(2,1)S(1)}, bf16[32,1536]{1,0:T(8,128)(2,1)S(1)}, u32[]{:S(2)}, u32[]{:S(2)}) %collective-permute-start.8) | collective-permute-done | bytes 98336 | tf_op jit(solution)/shard_map/ppermute | solution.py:24
  24.1 1.7 %shard_map.68 = (bf16[8,2,16,1536]{3,2,1,0:T(8,128)(2,1)}, f32[32,768]{1,0:T(8,128)S(1)}) custom-call(bf16[2,768,768]{2,1,0:T(8,128)(2,1)S(1)} %get-tuple-element.25.own_ref, bf16[2,768,768]{2,1,0:T(8,128)(2,1)S(1)} %get-tuple-element.26.sibling_ref, bf16[32,1536]{1,0:T(8,128)(2,1)S(1)} %collective-permute-done.5.refs_0_, ...), custom_call_target="tpu_custom_call" | custom-call | tf_op jit(solution)/shard_map/pallas_call | solution.py:217
  25.8 1.8 %collective-permute-done.3.refs_1_ = bf16[32,1536]{1,0:T(8,128)(2,1)S(1)} collective-permute-done((bf16[32,1536]{1,0:T(8,128)(2,1)S(1)}, bf16[32,1536]{1,0:T(8,128)(2,1)S(1)}, u32[]{:S(2)}, u32[]{:S(2)}) %collective-permute-start.3) | collective-permute-done | bytes 98336 | tf_op jit(solution)/shard_map/ppermute | solution.py:24
  27.6 0.8 %collective-permute-done.4.refs_2_ = bf16[32,1536]{1,0:T(8,128)(2,1)S(1)} collective-permute-done((bf16[32,1536]{1,0:T(8,128)(2,1)S(1)}, bf16[32,1536]{1,0:T(8,128)(2,1)S(1)}, u32[]{:S(2)}, u32[]{:S(2)}) %collective-permute-start.4) | collective-permute-done | bytes 98336 | tf_op jit(solution)/shard_map/ppermute | solution.py:24
  28.4 1.6 %shard_map.69 = (bf16[8,2,16,1536]{3,2,1,0:T(8,128)(2,1)}, f32[16,896]{1,0:T(8,128)S(1)}, f32[16,896]{1,0:T(8,128)S(1)}) custom-call(bf16[2,768,768]{2,1,0:T(8,128)(2,1)S(1)} %get-tuple-element.25.own_ref, bf16[2,768,768]{2,1,0:T(8,128)(2,1)S(1)} %get-tuple-element.26.sibling_ref, ...), custom_call_target="tpu_custom_call", output_to_operand_aliasing={{0}: (7, {})} | custom-call | tf_op jit(solution)/shard_map/pallas_call | solution.py:217
  30.1 4.7 %all-to-all-start = ((bf16[8,32,1536]{2,1,0:T(8,128)(2,1)}), bf16[8,32,1536]{2,1,0:T(8,128)(2,1)S(1)}, u32[]{:S(2)}, u32[]{:S(2)}) async-start(bf16[8,32,1536]{2,1,0:T(8,128)(2,1)} %bitcast.4), calls=%async_computation | async-start | bytes 1572864 | tf_op jit(solution)/shard_map/all_to_all | solution.py:231
  34.8 0.6 %collective-permute-done.9 = f32[16,896]{1,0:T(8,128)S(1)} collective-permute-done((f32[16,896]{1,0:T(8,128)S(1)}, f32[16,896]{1,0:T(8,128)S(1)}, u32[]{:S(2)}, u32[]{:S(2)}) %collective-permute-start.9) | collective-permute-done | bytes 57376 | tf_op jit(solution)/shard_map/ppermute | solution.py:24
  35.4 1.2 %collective-permute-done.10 = bf16[16,896]{1,0:T(8,128)(2,1)S(1)} collective-permute-done((bf16[16,896]{1,0:T(8,128)(2,1)S(1)}, bf16[16,896]{1,0:T(8,128)(2,1)S(1)}, u32[]{:S(2)}, u32[]{:S(2)}) %collective-permute-start.10) | collective-permute-done | bytes 28704 | tf_op jit(solution)/shard_map/ppermute | solution.py:24
  36.7 1.5 %collective-permute-start.11 = (f32[12,896]{1,0:T(8,128)S(1)}, f32[12,896]{1,0:T(8,128)S(1)}, u32[]{:S(2)}, u32[]{:S(2)}) collective-permute-start(f32[12,896]{1,0:T(8,128)S(1)} %pad_maximum_fusion), channel_id=1, source_target_pairs={{0,2},{1,3},{2,0},{3,1},{4,6},{5,7},{6,4},{7,5},{8,10},{9,11},{10,... | collective-permute-start | bytes 129032 | tf_op jit(solution)/shard_map/ppermute | solution.py:24
  38.2 3.5 %collective-permute-done.11 = f32[12,896]{1,0:T(8,128)S(1)} collective-permute-done((f32[12,896]{1,0:T(8,128)S(1)}, f32[12,896]{1,0:T(8,128)S(1)}, u32[]{:S(2)}, u32[]{:S(2)}) %collective-permute-start.11) | collective-permute-done | bytes 43040 | tf_op jit(solution)/shard_map/ppermute | solution.py:24
  41.8 3.8 %collective-permute-start.12 = (f32[8,896]{1,0:T(8,128)S(1)}, f32[8,896]{1,0:T(8,128)S(1)}, u32[]{:S(2)}, u32[]{:S(2)}) collective-permute-start(f32[8,896]{1,0:T(8,128)S(1)} %pad_maximum_fusion.2), channel_id=1, source_target_pairs={{0,4},{1,5},{2,6},{3,7},{4,0},{5,1},{6,2},{7,3},{8,12},{9,13},{10,... | collective-permute-start | bytes 86024 | tf_op jit(solution)/shard_map/ppermute | solution.py:24
  45.5 2.6 %collective-permute-done.12.arrived_ref = f32[8,896]{1,0:T(8,128)S(1)} collective-permute-done((f32[8,896]{1,0:T(8,128)S(1)}, f32[8,896]{1,0:T(8,128)S(1)}, u32[]{:S(2)}, u32[]{:S(2)}) %collective-permute-start.12) | collective-permute-done | bytes 28704 | tf_op jit(solution)/shard_map/ppermute | solution.py:24
  48.2 0.9 %shard_map.70.above_ref = f32[4,384]{1,0:T(4,128)S(1)} custom-call(f32[8,896]{1,0:T(8,128)S(1)} %pad_maximum_fusion.1.keep_ref, f32[8,896]{1,0:T(8,128)S(1)} %collective-permute-done.12.arrived_ref, bf16[2,2,384,384]{3,2,1,0:T(8,128)(2,1)S(1)} %copy-done.1), custom_call_target="tpu_custom_call" | custom-call | flops 1 | bytes 1 | tf_op jit(solution)/shard_map/pallas_call | solution.py:217
  49.1 4.1 %all-to-all-done = bf16[8,32,1536]{2,1,0:T(8,128)(2,1)S(1)} async-done(((bf16[8,32,1536]{2,1,0:T(8,128)(2,1)}), bf16[8,32,1536]{2,1,0:T(8,128)(2,1)S(1)}, u32[]{:S(2)}, u32[]{:S(2)}) %all-to-all-start) | async-done | bytes 786464 | tf_op jit(solution)/shard_map/all_to_all | solution.py:231
  53.1 1.0 %shard_map.71 = bf16[52,2,1536]{2,1,0:T(2,128)(2,1)} custom-call(bf16[104,256]{1,0:T(8,128)(2,1)S(1)} %get-tuple-element.22.pick_ref, f32[4,384]{1,0:T(4,128)S(1)} %shard_map.70.above_ref, bf16[256,1536]{1,0:T(8,128)(2,1)S(1)} %bitcast.7), custom_call_target="tpu_custom_call" | custom-call | tf_op jit(solution)/shard_map/pallas_call | solution.py:217
  (31 shorter events, 1.5 us)
Async XLA Ops:
  0.0 6.3 %collective-permute-start = (bf16[2,768,768]{2,1,0:T(8,128)(2,1)}, bf16[2,768,768]{2,1,0:T(8,128)(2,1)S(1)}, u32[]{:S(2)}, u32[]{:S(2)}) collective-permute-start(bf16[2,768,768]{2,1,0:T(8,128)(2,1)} %bitcast.8), channel_id=1, source_target_pairs={{0,1},{1,0},{2,3},{3,2},{4,5},{5,4},{6,7},{7,6},{8,9},{9,8},{10,11... | collective-permute-start | bytes 7077896 | tf_op jit(solution)/shard_map/ppermute | solution.py:24
  1.5 4.8 %collective-permute-start.1 = (bf16[104,128]{1,0:T(8,128)(2,1)S(1)}, bf16[104,128]{1,0:T(8,128)(2,1)S(1)}, u32[]{:S(2)}, u32[]{:S(2)}) collective-permute-start(bf16[104,128]{1,0:T(8,128)(2,1)S(1)} %shard_map.65), channel_id=1, source_target_pairs={{0,16},{16,0},{1,17},{17,1},{2,18},{18,2},{3,19},{19,3},{4,20},{20... | collective-permute-start | bytes 79880 | tf_op jit(solution)/shard_map/ppermute | solution.py:19
  5.1 16.7 %copy-start = (bf16[1,2,768,768]{3,2,1,0:T(8,128)(2,1)S(1)}, bf16[1,2,768,768]{3,2,1,0:T(8,128)(2,1)}, u32[]{:S(2)}) copy-start(bf16[1,2,768,768]{3,2,1,0:T(8,128)(2,1)} %param.10) | copy-start | bytes 7077892
  5.1 0.8 %copy-start.2 = (s32[1,52,1]{1,2,0:T(1,128)S(1)}, s32[1,52,1]{1,2,0:T(1,128)}, u32[]{:S(2)}) copy-start(s32[1,52,1]{1,2,0:T(1,128)} %param.8) | copy-start | bytes 628
  6.7 8.4 %collective-permute-start.5 = (bf16[32,1536]{1,0:T(8,128)(2,1)S(1)}, bf16[32,1536]{1,0:T(8,128)(2,1)S(1)}, u32[]{:S(2)}, u32[]{:S(2)}) collective-permute-start(bf16[32,1536]{1,0:T(8,128)(2,1)S(1)} %get-tuple-element.30), channel_id=1, source_target_pairs={{0,14},{1,15},{2,12},{3,13},{4,10},{5,11},{6,8},{7,9},{8,6},{9,7},... | collective-permute-start | bytes 294920 | tf_op jit(solution)/shard_map/ppermute | solution.py:24
  11.4 9.8 %collective-permute-start.6 = (bf16[32,1536]{1,0:T(8,128)(2,1)S(1)}, bf16[32,1536]{1,0:T(8,128)(2,1)S(1)}, u32[]{:S(2)}, u32[]{:S(2)}) collective-permute-start(bf16[32,1536]{1,0:T(8,128)(2,1)S(1)} %get-tuple-element.31), channel_id=1, source_target_pairs={{0,2},{1,3},{2,0},{3,1},{4,6},{5,7},{6,4},{7,5},{8,10},{9,11},{10,... | collective-permute-start | bytes 294920 | tf_op jit(solution)/shard_map/ppermute | solution.py:24
  11.9 13.9 %collective-permute-start.2 = (bf16[32,1536]{1,0:T(8,128)(2,1)S(1)}, bf16[32,1536]{1,0:T(8,128)(2,1)S(1)}, u32[]{:S(2)}, u32[]{:S(2)}) collective-permute-start(bf16[32,1536]{1,0:T(8,128)(2,1)S(1)} %get-tuple-element.27), channel_id=1, source_target_pairs={{0,12},{1,13},{2,14},{3,15},{4,8},{5,9},{6,10},{7,11},{8,4},{9,5},... | collective-permute-start | bytes 294920 | tf_op jit(solution)/shard_map/ppermute | solution.py:24
  12.0 10.1 %collective-permute-start.7 = (bf16[32,1536]{1,0:T(8,128)(2,1)S(1)}, bf16[32,1536]{1,0:T(8,128)(2,1)S(1)}, u32[]{:S(2)}, u32[]{:S(2)}) collective-permute-start(bf16[32,1536]{1,0:T(8,128)(2,1)S(1)} %get-tuple-element.32), channel_id=1, source_target_pairs={{0,4},{1,5},{2,6},{3,7},{4,0},{5,1},{6,2},{7,3},{8,12},{9,13},{10,... | collective-permute-start | bytes 294920 | tf_op jit(solution)/shard_map/ppermute | solution.py:24
  12.0 12.0 %collective-permute-start.8 = (bf16[32,1536]{1,0:T(8,128)(2,1)S(1)}, bf16[32,1536]{1,0:T(8,128)(2,1)S(1)}, u32[]{:S(2)}, u32[]{:S(2)}) collective-permute-start(bf16[32,1536]{1,0:T(8,128)(2,1)S(1)} %get-tuple-element.33), channel_id=1, source_target_pairs={{0,6},{1,7},{2,4},{3,5},{4,2},{5,3},{6,0},{7,1},{8,14},{9,15},{10,... | collective-permute-start | bytes 294920 | tf_op jit(solution)/shard_map/ppermute | solution.py:24
  15.1 12.5 %collective-permute-start.3 = (bf16[32,1536]{1,0:T(8,128)(2,1)S(1)}, bf16[32,1536]{1,0:T(8,128)(2,1)S(1)}, u32[]{:S(2)}, u32[]{:S(2)}) collective-permute-start(bf16[32,1536]{1,0:T(8,128)(2,1)S(1)} %get-tuple-element.28), channel_id=1, source_target_pairs={{0,10},{1,11},{2,8},{3,9},{4,14},{5,15},{6,12},{7,13},{8,2},{9,3},... | collective-permute-start | bytes 294920 | tf_op jit(solution)/shard_map/ppermute | solution.py:24
  21.2 7.2 %collective-permute-start.4 = (bf16[32,1536]{1,0:T(8,128)(2,1)S(1)}, bf16[32,1536]{1,0:T(8,128)(2,1)S(1)}, u32[]{:S(2)}, u32[]{:S(2)}) collective-permute-start(bf16[32,1536]{1,0:T(8,128)(2,1)S(1)} %get-tuple-element.29), channel_id=1, source_target_pairs={{0,8},{1,9},{2,10},{3,11},{4,12},{5,13},{6,14},{7,15},{8,0},{9,1},... | collective-permute-start | bytes 294920 | tf_op jit(solution)/shard_map/ppermute | solution.py:24
  30.0 18.2 %copy-start.1 = (bf16[2,2,384,384]{3,2,1,0:T(8,128)(2,1)S(1)}, bf16[2,2,384,384]{3,2,1,0:T(8,128)(2,1)}, u32[]{:S(2)}) copy-start(bf16[2,2,384,384]{3,2,1,0:T(8,128)(2,1)} %factors_ref.1) | copy-start | bytes 3538948
  30.0 5.4 %collective-permute-start.9 = (f32[16,896]{1,0:T(8,128)S(1)}, f32[16,896]{1,0:T(8,128)S(1)}, u32[]{:S(2)}, u32[]{:S(2)}) collective-permute-start(f32[16,896]{1,0:T(8,128)S(1)} %get-tuple-element.37), channel_id=1, source_target_pairs={{0,8},{1,9},{2,10},{3,11},{4,12},{5,13},{6,14},{7,15},{8,0},{9,1},... | collective-permute-start | bytes 172040 | tf_op jit(solution)/shard_map/ppermute | solution.py:24
  30.1 23.1 %all-to-all-start = ((bf16[8,32,1536]{2,1,0:T(8,128)(2,1)}), bf16[8,32,1536]{2,1,0:T(8,128)(2,1)S(1)}, u32[]{:S(2)}, u32[]{:S(2)}) async-start(bf16[8,32,1536]{2,1,0:T(8,128)(2,1)} %bitcast.4), calls=%async_computation | async-start | bytes 1572864 | tf_op jit(solution)/shard_map/all_to_all | solution.py:231
  35.4 1.3 %collective-permute-start.10 = (bf16[16,896]{1,0:T(8,128)(2,1)S(1)}, bf16[16,896]{1,0:T(8,128)(2,1)S(1)}, u32[]{:S(2)}, u32[]{:S(2)}) collective-permute-start(bf16[16,896]{1,0:T(8,128)(2,1)S(1)} %get-tuple-element.39), channel_id=1, source_target_pairs={{0,1},{1,0},{2,3},{3,2},{4,5},{5,4},{6,7},{7,6},{8,9},{9,8},{10,11... | collective-permute-start | bytes 86024 | tf_op jit(solution)/shard_map/ppermute | solution.py:24
  36.7 5.0 %collective-permute-start.11 = (f32[12,896]{1,0:T(8,128)S(1)}, f32[12,896]{1,0:T(8,128)S(1)}, u32[]{:S(2)}, u32[]{:S(2)}) collective-permute-start(f32[12,896]{1,0:T(8,128)S(1)} %pad_maximum_fusion), channel_id=1, source_target_pairs={{0,2},{1,3},{2,0},{3,1},{4,6},{5,7},{6,4},{7,5},{8,10},{9,11},{10,... | collective-permute-start | bytes 129032 | tf_op jit(solution)/shard_map/ppermute | solution.py:24
  41.8 6.4 %collective-permute-start.12 = (f32[8,896]{1,0:T(8,128)S(1)}, f32[8,896]{1,0:T(8,128)S(1)}, u32[]{:S(2)}, u32[]{:S(2)}) collective-permute-start(f32[8,896]{1,0:T(8,128)S(1)} %pad_maximum_fusion.2), channel_id=1, source_target_pairs={{0,4},{1,5},{2,6},{3,7},{4,0},{5,1},{6,2},{7,3},{8,12},{9,13},{10,... | collective-permute-start | bytes 86024 | tf_op jit(solution)/shard_map/ppermute | solution.py:24

commit v11 on v10

--- a/solution.py
+++ b/solution.py
@@ -193,12 +193,13 @@
     out_ref[...] = above
 
 
-def result_kernel(shots, pick_ref, above_ref, back_ref, out_ref):
+def result_kernel(shots, pick_ref, above_ref, back_ref, out_ref, solved_ref, sems):
     leaves, _, width2 = out_ref.shape
     count = leaves * shots
     leaf_n = width2 // 2
     sep_n = above_ref.shape[1]
     shot = lax.broadcasted_iota(jnp.int32, (count, sep_n), 0) % shots
+    copies = []
     for part in range(2):
         start = part * leaf_n
         solved = dot(pick_ref[...], back_ref[:, start : start + leaf_n])
@@ -207,7 +208,14 @@
             here = part * shots + at
             lifted = jnp.where(shot == at, above_ref[here : here + 1], lifted)
         solved = jnp.concatenate([solved[:, :sep_n] - lifted, solved[:, sep_n:]], axis=1).astype(BF16)
-        out_ref[:, :, start : start + leaf_n] = solved.reshape(leaves, shots, leaf_n)
+        columns = pl.ds(start, leaf_n)
+        solved_ref[:, :, columns] = solved.reshape(leaves, shots, leaf_n)
+        copies.append(
+            pltpu.make_async_copy(solved_ref.at[:, :, columns], out_ref.at[:, :, columns], sems.at[part])
+        )
+        copies[part].start()
+    for copy in copies:
+        copy.wait()
 
 
 def call(kernel, out_shape, args, smem=(), hbm=(), hbm_out=(), aliases={}, scratch=(), cost=None, limit=16):
@@ -347,6 +355,8 @@
         functools.partial(result_kernel, shots),
         jax.ShapeDtypeStruct((leaves, shots, width2), BF16),
         (from_slots, above, back),
+        hbm_out=(0,),
+        scratch=[VMEM((leaves, shots, width2), BF16), pltpu.SemaphoreType.DMA((2,))],
     )
     return result[None]
 

time: 54.5 us -> 54.4 us (level)
  no operation moved by 1% of the time
where the time goes in v11:
time: 54.4 us; the launch traced here: 54.1 us
  starting transfers between devices  27.6 us (51%)
  waiting for transfers between devices  16.4 us (30%)
  Pallas kernels  7.2 us (13%)
  local copies, waits for them, and re-layouts  1.94 us (4%)
  between operations  0.87 us (2%)
    ppermute x12, starting transfers between devices, exchange(): return lax.ppermute(value, 'leaf', pairs)  20.4 us
    ppermute x12, waiting for transfers between devices, exchange(): return lax.ppermute(value, 'leaf', pairs)  12.3 us
    pallas_call x8, Pallas kernels, call(): pl.pallas_call(kernel, out_shape=out_shape, in_specs=[pl.BlockSpec(memory...  7.2 us
    all_to_all x1, starting transfers between devices, to_pairs(): lax.all_to_all(value, 'leaf', 0, 0, tiled=True, axis_index_groups=groups)  4.7 us
    all_to_all x1, waiting for transfers between devices, to_pairs(): lax.all_to_all(value, 'leaf', 0, 0, tiled=True, axis_index_groups=groups)  4.08 us
    ppermute x1, starting transfers between devices, around(): lax.ppermute(value, axis, [(at, (at + 1) % count) for at in range(count)])  2.55 us
    another operation x1, local copies, waits for them, and re-layouts, on_device(): source.reshape(rows, width2)  1.09 us
  transfers between devices with their start and end apart: 14, of which 8 were waited for; matrix products, arithmetic and copies ran while one was open for 2% of the time, Pallas kernels for 8%

profile of v11, /device:TPU:0, one launch (start us, length us, event | category | flops | bytes accessed | tf_op | source)
XLA Modules:
  0.0 54.1 jit_solution(18139513784862980918)
XLA Ops:
  0.0 0.5 collective-permute-start
  0.5 1.0 %shard_map.65 = bf16[104,128]{1,0:T(8,128)(2,1)S(1)} custom-call(bf16[52,2,1536]{2,1,0:T(2,128)(2,1)} %bitcast.11, f32[52,1,128]{2,1,0:T(1,128)} %bitcast.12), custom_call_target="tpu_custom_call" | custom-call | tf_op jit(solution)/shard_map/pallas_call | solution.py:225
  1.5 2.6 %collective-permute-start.1 = (bf16[104,128]{1,0:T(8,128)(2,1)S(1)}, bf16[104,128]{1,0:T(8,128)(2,1)S(1)}, u32[]{:S(2)}, u32[]{:S(2)}) collective-permute-start(bf16[104,128]{1,0:T(8,128)(2,1)S(1)} %shard_map.65), channel_id=1, source_target_pairs={{0,16},{16,0},{1,17},{17,1},{2,18},{18,2},{3,19},{19,3},{4,20},{20... | collective-permute-start | bytes 79880 | tf_op jit(solution)/shard_map/ppermute | solution.py:19
  4.0 1.1 %reshape_squeeze.7.rows_ref = bf16[104,1536]{1,0:T(8,128)(2,1)S(1)} reshape(bf16[1,52,2,1536]{3,2,1,0:T(2,128)(2,1)} %param.6) | data formatting | bytes 638976 | tf_op jit(solution)/shard_map/reshape;squeeze | solution.py:309
  5.1 0.8 %copy-done.2 = s32[1,52,1]{1,2,0:T(1,128)S(1)} copy-done((s32[1,52,1]{1,2,0:T(1,128)S(1)}, s32[1,52,1]{1,2,0:T(1,128)}, u32[]{:S(2)}) %copy-start.2) | copy-done | bytes 232
  6.7 4.7 %collective-permute-start.5 = (bf16[32,1536]{1,0:T(8,128)(2,1)S(1)}, bf16[32,1536]{1,0:T(8,128)(2,1)S(1)}, u32[]{:S(2)}, u32[]{:S(2)}) collective-permute-start(bf16[32,1536]{1,0:T(8,128)(2,1)S(1)} %get-tuple-element.30), channel_id=1, source_target_pairs={{0,14},{1,15},{2,12},{3,13},{4,10},{5,11},{6,8},{7,9},{8,6},{9,7},... | collective-permute-start | bytes 294920 | tf_op jit(solution)/shard_map/ppermute | solution.py:24
  11.4 0.5 collective-permute-start.6
  12.0 3.1 %collective-permute-start.8 = (bf16[32,1536]{1,0:T(8,128)(2,1)S(1)}, bf16[32,1536]{1,0:T(8,128)(2,1)S(1)}, u32[]{:S(2)}, u32[]{:S(2)}) collective-permute-start(bf16[32,1536]{1,0:T(8,128)(2,1)S(1)} %get-tuple-element.33), channel_id=1, source_target_pairs={{0,6},{1,7},{2,4},{3,5},{4,2},{5,3},{6,0},{7,1},{8,14},{9,15},{10,... | collective-permute-start | bytes 294920 | tf_op jit(solution)/shard_map/ppermute | solution.py:24
  15.1 6.1 %collective-permute-start.3 = (bf16[32,1536]{1,0:T(8,128)(2,1)S(1)}, bf16[32,1536]{1,0:T(8,128)(2,1)S(1)}, u32[]{:S(2)}, u32[]{:S(2)}) collective-permute-start(bf16[32,1536]{1,0:T(8,128)(2,1)S(1)} %get-tuple-element.28), channel_id=1, source_target_pairs={{0,10},{1,11},{2,8},{3,9},{4,14},{5,15},{6,12},{7,13},{8,2},{9,3},... | collective-permute-start | bytes 294920 | tf_op jit(solution)/shard_map/ppermute | solution.py:24
  22.2 1.9 %collective-permute-done.8.refs_3_ = bf16[32,1536]{1,0:T(8,128)(2,1)S(1)} collective-permute-done((bf16[32,1536]{1,0:T(8,128)(2,1)S(1)}, bf16[32,1536]{1,0:T(8,128)(2,1)S(1)}, u32[]{:S(2)}, u32[]{:S(2)}) %collective-permute-start.8) | collective-permute-done | bytes 98336 | tf_op jit(solution)/shard_map/ppermute | solution.py:24
  24.1 1.7 %shard_map.68 = (bf16[8,2,16,1536]{3,2,1,0:T(8,128)(2,1)}, f32[32,768]{1,0:T(8,128)S(1)}) custom-call(bf16[2,768,768]{2,1,0:T(8,128)(2,1)S(1)} %get-tuple-element.25.own_ref, bf16[2,768,768]{2,1,0:T(8,128)(2,1)S(1)} %get-tuple-element.26.sibling_ref, bf16[32,1536]{1,0:T(8,128)(2,1)S(1)} %collective-permute-done.5.refs_0_, ...), custom_call_target="tpu_custom_call" | custom-call | tf_op jit(solution)/shard_map/pallas_call | solution.py:225
  25.8 1.8 %collective-permute-done.3.refs_1_ = bf16[32,1536]{1,0:T(8,128)(2,1)S(1)} collective-permute-done((bf16[32,1536]{1,0:T(8,128)(2,1)S(1)}, bf16[32,1536]{1,0:T(8,128)(2,1)S(1)}, u32[]{:S(2)}, u32[]{:S(2)}) %collective-permute-start.3) | collective-permute-done | bytes 98336 | tf_op jit(solution)/shard_map/ppermute | solution.py:24
  27.6 0.8 %collective-permute-done.4.refs_2_ = bf16[32,1536]{1,0:T(8,128)(2,1)S(1)} collective-permute-done((bf16[32,1536]{1,0:T(8,128)(2,1)S(1)}, bf16[32,1536]{1,0:T(8,128)(2,1)S(1)}, u32[]{:S(2)}, u32[]{:S(2)}) %collective-permute-start.4) | collective-permute-done | bytes 98336 | tf_op jit(solution)/shard_map/ppermute | solution.py:24
  28.4 1.6 %shard_map.69 = (bf16[8,2,16,1536]{3,2,1,0:T(8,128)(2,1)}, f32[16,896]{1,0:T(8,128)S(1)}, f32[16,896]{1,0:T(8,128)S(1)}) custom-call(bf16[2,768,768]{2,1,0:T(8,128)(2,1)S(1)} %get-tuple-element.25.own_ref, bf16[2,768,768]{2,1,0:T(8,128)(2,1)S(1)} %get-tuple-element.26.sibling_ref, ...), custom_call_target="tpu_custom_call", output_to_operand_aliasing={{0}: (7, {})} | custom-call | tf_op jit(solution)/shard_map/pallas_call | solution.py:225
  30.1 4.7 %all-to-all-start = ((bf16[8,32,1536]{2,1,0:T(8,128)(2,1)}), bf16[8,32,1536]{2,1,0:T(8,128)(2,1)S(1)}, u32[]{:S(2)}, u32[]{:S(2)}) async-start(bf16[8,32,1536]{2,1,0:T(8,128)(2,1)} %bitcast.4), calls=%async_computation | async-start | bytes 1572864 | tf_op jit(solution)/shard_map/all_to_all | solution.py:239
  34.8 0.6 %collective-permute-done.9 = f32[16,896]{1,0:T(8,128)S(1)} collective-permute-done((f32[16,896]{1,0:T(8,128)S(1)}, f32[16,896]{1,0:T(8,128)S(1)}, u32[]{:S(2)}, u32[]{:S(2)}) %collective-permute-start.9) | collective-permute-done | bytes 57376 | tf_op jit(solution)/shard_map/ppermute | solution.py:24
  35.4 1.2 %collective-permute-done.10 = bf16[16,896]{1,0:T(8,128)(2,1)S(1)} collective-permute-done((bf16[16,896]{1,0:T(8,128)(2,1)S(1)}, bf16[16,896]{1,0:T(8,128)(2,1)S(1)}, u32[]{:S(2)}, u32[]{:S(2)}) %collective-permute-start.10) | collective-permute-done | bytes 28704 | tf_op jit(solution)/shard_map/ppermute | solution.py:24
  36.7 1.5 %collective-permute-start.11 = (f32[12,896]{1,0:T(8,128)S(1)}, f32[12,896]{1,0:T(8,128)S(1)}, u32[]{:S(2)}, u32[]{:S(2)}) collective-permute-start(f32[12,896]{1,0:T(8,128)S(1)} %pad_maximum_fusion), channel_id=1, source_target_pairs={{0,2},{1,3},{2,0},{3,1},{4,6},{5,7},{6,4},{7,5},{8,10},{9,11},{10,... | collective-permute-start | bytes 129032 | tf_op jit(solution)/shard_map/ppermute | solution.py:24
  38.2 3.5 %collective-permute-done.11 = f32[12,896]{1,0:T(8,128)S(1)} collective-permute-done((f32[12,896]{1,0:T(8,128)S(1)}, f32[12,896]{1,0:T(8,128)S(1)}, u32[]{:S(2)}, u32[]{:S(2)}) %collective-permute-start.11) | collective-permute-done | bytes 43040 | tf_op jit(solution)/shard_map/ppermute | solution.py:24
  41.8 3.8 %collective-permute-start.12 = (f32[8,896]{1,0:T(8,128)S(1)}, f32[8,896]{1,0:T(8,128)S(1)}, u32[]{:S(2)}, u32[]{:S(2)}) collective-permute-start(f32[8,896]{1,0:T(8,128)S(1)} %pad_maximum_fusion.2), channel_id=1, source_target_pairs={{0,4},{1,5},{2,6},{3,7},{4,0},{5,1},{6,2},{7,3},{8,12},{9,13},{10,... | collective-permute-start | bytes 86024 | tf_op jit(solution)/shard_map/ppermute | solution.py:24
  45.5 2.6 %collective-permute-done.12.arrived_ref = f32[8,896]{1,0:T(8,128)S(1)} collective-permute-done((f32[8,896]{1,0:T(8,128)S(1)}, f32[8,896]{1,0:T(8,128)S(1)}, u32[]{:S(2)}, u32[]{:S(2)}) %collective-permute-start.12) | collective-permute-done | bytes 28704 | tf_op jit(solution)/shard_map/ppermute | solution.py:24
  48.2 0.9 %shard_map.70.above_ref = f32[4,384]{1,0:T(4,128)S(1)} custom-call(f32[8,896]{1,0:T(8,128)S(1)} %pad_maximum_fusion.1.keep_ref, f32[8,896]{1,0:T(8,128)S(1)} %collective-permute-done.12.arrived_ref, bf16[2,2,384,384]{3,2,1,0:T(8,128)(2,1)S(1)} %copy-done.1), custom_call_target="tpu_custom_call" | custom-call | flops 1 | bytes 1 | tf_op jit(solution)/shard_map/pallas_call | solution.py:225
  49.1 4.1 %all-to-all-done = bf16[8,32,1536]{2,1,0:T(8,128)(2,1)S(1)} async-done(((bf16[8,32,1536]{2,1,0:T(8,128)(2,1)}), bf16[8,32,1536]{2,1,0:T(8,128)(2,1)S(1)}, u32[]{:S(2)}, u32[]{:S(2)}) %all-to-all-start) | async-done | bytes 786464 | tf_op jit(solution)/shard_map/all_to_all | solution.py:239
  53.1 1.0 %shard_map.71 = bf16[52,2,1536]{2,1,0:T(2,128)(2,1)} custom-call(bf16[104,256]{1,0:T(8,128)(2,1)S(1)} %get-tuple-element.22.pick_ref, f32[4,384]{1,0:T(4,128)S(1)} %shard_map.70.above_ref, bf16[256,1536]{1,0:T(8,128)(2,1)S(1)} %bitcast.7), custom_call_target="tpu_custom_call" | custom-call | tf_op jit(solution)/shard_map/pallas_call | solution.py:225
  (31 shorter events, 1.5 us)
Async XLA Ops:
  0.0 6.3 %collective-permute-start = (bf16[2,768,768]{2,1,0:T(8,128)(2,1)}, bf16[2,768,768]{2,1,0:T(8,128)(2,1)S(1)}, u32[]{:S(2)}, u32[]{:S(2)}) collective-permute-start(bf16[2,768,768]{2,1,0:T(8,128)(2,1)} %bitcast.8), channel_id=1, source_target_pairs={{0,1},{1,0},{2,3},{3,2},{4,5},{5,4},{6,7},{7,6},{8,9},{9,8},{10,11... | collective-permute-start | bytes 7077896 | tf_op jit(solution)/shard_map/ppermute | solution.py:24
  1.5 4.8 %collective-permute-start.1 = (bf16[104,128]{1,0:T(8,128)(2,1)S(1)}, bf16[104,128]{1,0:T(8,128)(2,1)S(1)}, u32[]{:S(2)}, u32[]{:S(2)}) collective-permute-start(bf16[104,128]{1,0:T(8,128)(2,1)S(1)} %shard_map.65), channel_id=1, source_target_pairs={{0,16},{16,0},{1,17},{17,1},{2,18},{18,2},{3,19},{19,3},{4,20},{20... | collective-permute-start | bytes 79880 | tf_op jit(solution)/shard_map/ppermute | solution.py:19
  5.1 16.7 %copy-start = (bf16[1,2,768,768]{3,2,1,0:T(8,128)(2,1)S(1)}, bf16[1,2,768,768]{3,2,1,0:T(8,128)(2,1)}, u32[]{:S(2)}) copy-start(bf16[1,2,768,768]{3,2,1,0:T(8,128)(2,1)} %param.10) | copy-start | bytes 7077892
  5.1 0.8 %copy-start.2 = (s32[1,52,1]{1,2,0:T(1,128)S(1)}, s32[1,52,1]{1,2,0:T(1,128)}, u32[]{:S(2)}) copy-start(s32[1,52,1]{1,2,0:T(1,128)} %param.8) | copy-start | bytes 628
  6.7 8.4 %collective-permute-start.5 = (bf16[32,1536]{1,0:T(8,128)(2,1)S(1)}, bf16[32,1536]{1,0:T(8,128)(2,1)S(1)}, u32[]{:S(2)}, u32[]{:S(2)}) collective-permute-start(bf16[32,1536]{1,0:T(8,128)(2,1)S(1)} %get-tuple-element.30), channel_id=1, source_target_pairs={{0,14},{1,15},{2,12},{3,13},{4,10},{5,11},{6,8},{7,9},{8,6},{9,7},... | collective-permute-start | bytes 294920 | tf_op jit(solution)/shard_map/ppermute | solution.py:24
  11.4 9.8 %collective-permute-start.6 = (bf16[32,1536]{1,0:T(8,128)(2,1)S(1)}, bf16[32,1536]{1,0:T(8,128)(2,1)S(1)}, u32[]{:S(2)}, u32[]{:S(2)}) collective-permute-start(bf16[32,1536]{1,0:T(8,128)(2,1)S(1)} %get-tuple-element.31), channel_id=1, source_target_pairs={{0,2},{1,3},{2,0},{3,1},{4,6},{5,7},{6,4},{7,5},{8,10},{9,11},{10,... | collective-permute-start | bytes 294920 | tf_op jit(solution)/shard_map/ppermute | solution.py:24
  11.9 13.9 %collective-permute-start.2 = (bf16[32,1536]{1,0:T(8,128)(2,1)S(1)}, bf16[32,1536]{1,0:T(8,128)(2,1)S(1)}, u32[]{:S(2)}, u32[]{:S(2)}) collective-permute-start(bf16[32,1536]{1,0:T(8,128)(2,1)S(1)} %get-tuple-element.27), channel_id=1, source_target_pairs={{0,12},{1,13},{2,14},{3,15},{4,8},{5,9},{6,10},{7,11},{8,4},{9,5},... | collective-permute-start | bytes 294920 | tf_op jit(solution)/shard_map/ppermute | solution.py:24
  12.0 10.1 %collective-permute-start.7 = (bf16[32,1536]{1,0:T(8,128)(2,1)S(1)}, bf16[32,1536]{1,0:T(8,128)(2,1)S(1)}, u32[]{:S(2)}, u32[]{:S(2)}) collective-permute-start(bf16[32,1536]{1,0:T(8,128)(2,1)S(1)} %get-tuple-element.32), channel_id=1, source_target_pairs={{0,4},{1,5},{2,6},{3,7},{4,0},{5,1},{6,2},{7,3},{8,12},{9,13},{10,... | collective-permute-start | bytes 294920 | tf_op jit(solution)/shard_map/ppermute | solution.py:24
  12.0 12.0 %collective-permute-start.8 = (bf16[32,1536]{1,0:T(8,128)(2,1)S(1)}, bf16[32,1536]{1,0:T(8,128)(2,1)S(1)}, u32[]{:S(2)}, u32[]{:S(2)}) collective-permute-start(bf16[32,1536]{1,0:T(8,128)(2,1)S(1)} %get-tuple-element.33), channel_id=1, source_target_pairs={{0,6},{1,7},{2,4},{3,5},{4,2},{5,3},{6,0},{7,1},{8,14},{9,15},{10,... | collective-permute-start | bytes 294920 | tf_op jit(solution)/shard_map/ppermute | solution.py:24
  15.1 12.5 %collective-permute-start.3 = (bf16[32,1536]{1,0:T(8,128)(2,1)S(1)}, bf16[32,1536]{1,0:T(8,128)(2,1)S(1)}, u32[]{:S(2)}, u32[]{:S(2)}) collective-permute-start(bf16[32,1536]{1,0:T(8,128)(2,1)S(1)} %get-tuple-element.28), channel_id=1, source_target_pairs={{0,10},{1,11},{2,8},{3,9},{4,14},{5,15},{6,12},{7,13},{8,2},{9,3},... | collective-permute-start | bytes 294920 | tf_op jit(solution)/shard_map/ppermute | solution.py:24
  21.2 7.2 %collective-permute-start.4 = (bf16[32,1536]{1,0:T(8,128)(2,1)S(1)}, bf16[32,1536]{1,0:T(8,128)(2,1)S(1)}, u32[]{:S(2)}, u32[]{:S(2)}) collective-permute-start(bf16[32,1536]{1,0:T(8,128)(2,1)S(1)} %get-tuple-element.29), channel_id=1, source_target_pairs={{0,8},{1,9},{2,10},{3,11},{4,12},{5,13},{6,14},{7,15},{8,0},{9,1},... | collective-permute-start | bytes 294920 | tf_op jit(solution)/shard_map/ppermute | solution.py:24
  30.0 18.2 %copy-start.1 = (bf16[2,2,384,384]{3,2,1,0:T(8,128)(2,1)S(1)}, bf16[2,2,384,384]{3,2,1,0:T(8,128)(2,1)}, u32[]{:S(2)}) copy-start(bf16[2,2,384,384]{3,2,1,0:T(8,128)(2,1)} %factors_ref.1) | copy-start | bytes 3538948
  30.0 5.4 %collective-permute-start.9 = (f32[16,896]{1,0:T(8,128)S(1)}, f32[16,896]{1,0:T(8,128)S(1)}, u32[]{:S(2)}, u32[]{:S(2)}) collective-permute-start(f32[16,896]{1,0:T(8,128)S(1)} %get-tuple-element.37), channel_id=1, source_target_pairs={{0,8},{1,9},{2,10},{3,11},{4,12},{5,13},{6,14},{7,15},{8,0},{9,1},... | collective-permute-start | bytes 172040 | tf_op jit(solution)/shard_map/ppermute | solution.py:24
  30.1 23.1 %all-to-all-start = ((bf16[8,32,1536]{2,1,0:T(8,128)(2,1)}), bf16[8,32,1536]{2,1,0:T(8,128)(2,1)S(1)}, u32[]{:S(2)}, u32[]{:S(2)}) async-start(bf16[8,32,1536]{2,1,0:T(8,128)(2,1)} %bitcast.4), calls=%async_computation | async-start | bytes 1572864 | tf_op jit(solution)/shard_map/all_to_all | solution.py:239
  35.4 1.3 %collective-permute-start.10 = (bf16[16,896]{1,0:T(8,128)(2,1)S(1)}, bf16[16,896]{1,0:T(8,128)(2,1)S(1)}, u32[]{:S(2)}, u32[]{:S(2)}) collective-permute-start(bf16[16,896]{1,0:T(8,128)(2,1)S(1)} %get-tuple-element.39), channel_id=1, source_target_pairs={{0,1},{1,0},{2,3},{3,2},{4,5},{5,4},{6,7},{7,6},{8,9},{9,8},{10,11... | collective-permute-start | bytes 86024 | tf_op jit(solution)/shard_map/ppermute | solution.py:24
  36.7 5.0 %collective-permute-start.11 = (f32[12,896]{1,0:T(8,128)S(1)}, f32[12,896]{1,0:T(8,128)S(1)}, u32[]{:S(2)}, u32[]{:S(2)}) collective-permute-start(f32[12,896]{1,0:T(8,128)S(1)} %pad_maximum_fusion), channel_id=1, source_target_pairs={{0,2},{1,3},{2,0},{3,1},{4,6},{5,7},{6,4},{7,5},{8,10},{9,11},{10,... | collective-permute-start | bytes 129032 | tf_op jit(solution)/shard_map/ppermute | solution.py:24
  41.8 6.4 %collective-permute-start.12 = (f32[8,896]{1,0:T(8,128)S(1)}, f32[8,896]{1,0:T(8,128)S(1)}, u32[]{:S(2)}, u32[]{:S(2)}) collective-permute-start(f32[8,896]{1,0:T(8,128)S(1)} %pad_maximum_fusion.2), channel_id=1, source_target_pairs={{0,4},{1,5},{2,6},{3,7},{4,0},{5,1},{6,2},{7,3},{8,12},{9,13},{10,... | collective-permute-start | bytes 86024 | tf_op jit(solution)/shard_map/ppermute | solution.py:24
